TPU v7x, 32 devices: a whole 2x2x4 slice. The times are simulated.
32 devices in a mesh: ctx: 8 (over z, x), exp: 4 (over y, core).
Axes of the slice: x: 2, y: 2, z: 4, core: 2. Of those that a mesh axis runs over, the one named last changes fastest.
Arguments:
- residual: bfloat16 [4096, 2048], P(('ctx', 'exp')), may hold values from -6 to 6
- mixed_qkv: bfloat16 [4096, 4096], P(('ctx', 'exp')), may hold values from -6 to 6
- output_gate: bfloat16 [4096, 2048], P(('ctx', 'exp')), may hold values from -6 to 6
- log_decay: float32 [4096, 16], P(('ctx', 'exp')), may hold values from -0.8 to 0, as said below
- write_strength: float32 [4096, 16], P(('ctx', 'exp')), may hold values from 0 to 1, as said below
- conv_weight: float32 [4, 4096], replicated, may hold values from -3 to 3
- norm_gain: float32 [128], replicated, may hold values from 0.1 to 1.9
- out_weight: bfloat16 [2048, 2048], P(None, 'exp'), may hold values from -0.125 to 0.125
- post_gain: float32 [2048], replicated, may hold values from 0.1 to 1.9
- router_weight: bfloat16 [2048, 64], replicated, may hold values from -0.125 to 0.125
- expert_ids: int32 [4096, 10], P(('ctx', 'exp')), may hold values from 0 to 63, all different within a row; in each aligned block of 128 rows (0 to 127, 128 to 255, ...) at most 24 rows name the same one
- expert_gate: bfloat16 [64, 2048, 512], P(('ctx', 'exp')), may hold values from -0.125 to 0.125
- expert_up: bfloat16 [64, 2048, 512], P(('ctx', 'exp')), may hold values from -0.125 to 0.125
- expert_down: bfloat16 [64, 512, 2048], P(('ctx', 'exp')), may hold values from -0.25 to 0.25
- shared_gate: bfloat16 [2048, 512], replicated, may hold values from -0.125 to 0.125
- shared_up: bfloat16 [2048, 512], replicated, may hold values from -0.125 to 0.125
- shared_down: bfloat16 [512, 2048], replicated, may hold values from -0.25 to 0.25
- shared_switch: bfloat16 [2048], replicated, may hold values from -0.125 to 0.125
Outputs:
- layer_out: bfloat16 [4096, 2048], P(('ctx', 'exp'))
Inputs may be any that keep to these rules, and one draw needn't show every extreme that they name: `expert_ids`: in the 128 rows of one device no expert is named more than 24 times. `log_decay`: negative. `write_strength`: positive.
All inputs are finite; a program needn't handle non-finite values.
Results may differ from a plain program's by a relative error of at most 0.011.
Values may be sent and summed in bfloat16 or wider, within the bound.
No kernel may reach another device: no remote copies, remote signals or barrier semaphores. Data moves between devices by JAX's collectives and lax.ppermute only.
A program may use at most 128 MiB of HBM per device.

v0:
```python
import jax
import jax.numpy as jnp
from jax import lax
from jax.sharding import PartitionSpec as P

VHEADS = 16
KHEADS = 8
HEAD = 128
TOP = 10
SPAN = 64


highest_precision = lax.Precision.HIGHEST
epsilon = 1e-06


def passed_along(value, axis, steps):
    count = lax.axis_size(axis)
    first, last = (max(0, -steps), min(count, count - steps))
    return lax.ppermute(value, axis, [(source, source + steps) for source in range(first, last)])


def entering(part, axis, combine, identity):
    place = lax.axis_index(axis)
    gathered = jax.tree.map(lambda a: lax.all_gather(a, axis), part)
    state = jax.tree.map(lambda a, e: jnp.zeros_like(a) + jnp.asarray(e, a.dtype), part, identity)

    def one(turn, state):
        return combine(
            state, jax.tree.map(lambda a: lax.dynamic_index_in_dim(a, turn, 0, False), gathered)
        )

    return lax.fori_loop(0, place, one, state)


def short_conv(mixed_qkv, conv_weight, before):
    row_count = mixed_qkv.shape[0]
    padded = jnp.concatenate([before, mixed_qkv], axis=0).astype(jnp.float32)
    summed = conv_weight[3] * padded[3 : 3 + row_count]
    for tap_index in range(3):
        summed = summed + conv_weight[tap_index] * padded[tap_index : tap_index + row_count]
    return jax.nn.silu(summed)


def unit_rows(values_in):
    return values_in * lax.rsqrt(jnp.sum(values_in * values_in, axis=-1, keepdims=True) + epsilon)


def prepare(mixed_qkv, conv_weight, before):
    activated = short_conv(mixed_qkv, conv_weight, before)
    row_count = activated.shape[0]
    key_width = KHEADS * HEAD
    query_rows = unit_rows(activated[:, :key_width].reshape(row_count, KHEADS, HEAD)) * HEAD ** (
        -0.5
    )
    key_rows = unit_rows(activated[:, key_width : 2 * key_width].reshape(row_count, KHEADS, HEAD))
    value_rows = activated[:, 2 * key_width :].reshape(row_count, VHEADS, HEAD)
    per_group = VHEADS // KHEADS
    query_rows = jnp.repeat(query_rows, per_group, axis=1)
    key_rows = jnp.repeat(key_rows, per_group, axis=1)
    return (
        query_rows.transpose(1, 0, 2),
        key_rows.transpose(1, 0, 2),
        value_rows.transpose(1, 0, 2),
    )


def to_spans(head_rows):
    head_count, row_count, inner_width = head_rows.shape
    return head_rows.reshape(head_count, row_count // SPAN, SPAN, inner_width).transpose(1, 0, 2, 3)


def rates_to_spans(token_rates):
    row_count, head_count = token_rates.shape
    return token_rates.T.reshape(head_count, row_count // SPAN, SPAN).transpose(1, 0, 2)


def span_terms(query_rows, key_rows, value_rows, decay_rows, strength_rows):
    length = query_rows.shape[1]
    inner_width = key_rows.shape[2]
    cumul = jnp.cumsum(decay_rows, axis=1)
    causal = (
        jnp.arange(length, dtype=jnp.int32)[:, None] >= jnp.arange(length, dtype=jnp.int32)[None, :]
    )
    strict = (
        jnp.arange(length, dtype=jnp.int32)[:, None] > jnp.arange(length, dtype=jnp.int32)[None, :]
    )
    log_gap = cumul[:, :, None] - cumul[:, None, :]
    ratios = jnp.where(causal, jnp.exp(jnp.where(causal, log_gap, 0.0)), 0.0)
    key_inner = jnp.einsum("hck,hsk->hcs", key_rows, key_rows, precision=highest_precision)
    lower_part = jnp.where(strict, ratios * key_inner, 0.0) * strength_rows[:, :, None]
    system = jnp.eye(length, dtype=jnp.float32)[None] + lower_part
    decays = jnp.exp(cumul)
    right_operand = jnp.concatenate(
        [
            strength_rows[:, :, None] * decays[:, :, None] * key_rows,
            strength_rows[:, :, None] * value_rows,
        ],
        axis=2,
    )
    solved = jax.scipy.linalg.solve_triangular(
        system, right_operand, lower=True, unit_diagonal=True
    )
    key_weights = solved[:, :, :inner_width]
    fresh_values = solved[:, :, inner_width:]
    to_end = jnp.exp(cumul[:, -1:] - cumul)
    decayed_state = key_rows * to_end[:, :, None]
    identity = jnp.eye(inner_width, dtype=jnp.float32)[None]
    carry_transform = jnp.exp(cumul[:, -1])[:, None, None] * identity - jnp.einsum(
        "hck,hcj->hkj", decayed_state, key_weights, precision=highest_precision
    )
    carry_offset = jnp.einsum(
        "nae,nap->nep", decayed_state, fresh_values, precision=highest_precision
    )
    scores = jnp.einsum("hck,hsk->hcs", query_rows, key_rows, precision=highest_precision) * ratios
    read_transform = query_rows * decays[:, :, None] - jnp.einsum(
        "hcs,hsk->hck", scores, key_weights, precision=highest_precision
    )
    read_offset = jnp.einsum("hcs,hsv->hcv", scores, fresh_values, precision=highest_precision)
    return (carry_transform, carry_offset, read_transform, read_offset)


def apply_map(left_transform, right_operand):
    return jnp.einsum("coq,cqd->cod", left_transform, right_operand, precision=highest_precision)


def chain_pair(earlier, later):
    return (apply_map(later[0], earlier[0]), apply_map(later[0], earlier[1]) + later[1])


def run_experts(received, expert_gate, expert_up, expert_down):
    gate_part = jnp.einsum(
        "nesd,edf->nesf", received, expert_gate, preferred_element_type=jnp.float32
    )
    up_part = jnp.einsum("nesd,edf->nesf", received, expert_up, preferred_element_type=jnp.float32)
    expert_hidden = (jax.nn.silu(gate_part) * up_part).astype(jnp.bfloat16)
    return jnp.einsum(
        "nesf,efd->nesd", expert_hidden, expert_down, preferred_element_type=jnp.float32
    ).astype(jnp.bfloat16)


def local(
    residual,
    mixed_qkv,
    output_gate,
    log_decay,
    write_strength,
    conv_weight,
    norm_gain,
    out_weight,
    post_gain,
    router_weight,
    expert_ids,
    expert_gate,
    expert_up,
    expert_down,
    shared_gate,
    shared_up,
    shared_down,
    shared_switch,
):
    row_count = mixed_qkv.shape[0]
    model_width = residual.shape[1]
    before = passed_along(mixed_qkv[row_count - 3 :], ("ctx", "exp"), 1)
    query_rows, key_rows, value_rows = prepare(mixed_qkv, conv_weight, before)
    span_parts = jax.vmap(span_terms)(
        to_spans(query_rows),
        to_spans(key_rows),
        to_spans(value_rows),
        rates_to_spans(log_decay),
        rates_to_spans(write_strength),
    )
    identity = jnp.broadcast_to(jnp.eye(HEAD, dtype=jnp.float32)[None], (VHEADS, HEAD, HEAD))
    zero_add = jnp.zeros((VHEADS, HEAD, HEAD), jnp.float32)

    def compose(carried, step_parts):
        return (chain_pair(carried, step_parts), None)

    (block_map, block_add), _ = lax.scan(
        compose, (identity, zero_add), (span_parts[0], span_parts[1])
    )
    exp_count = lax.axis_size("exp")
    share = VHEADS // exp_count
    member_map, member_add = (
        lax.all_to_all(
            block_map.reshape(exp_count, share, HEAD, HEAD),
            "exp",
            split_axis=0,
            concat_axis=0,
            tiled=True,
        ),
        lax.all_to_all(
            block_add.reshape(exp_count, share, HEAD, HEAD),
            "exp",
            split_axis=0,
            concat_axis=0,
            tiled=True,
        ),
    )
    running = (identity[:share], zero_add[:share])
    prefixes = []
    for member in range(exp_count):
        prefixes.append(running)
        running = chain_pair(running, (member_map[member], member_add[member]))
    _, outer_add = entering(running, "ctx", chain_pair, (identity[:share], zero_add[:share]))
    starts = jnp.stack([apply_map(prefix[0], outer_add) + prefix[1] for prefix in prefixes])
    start_state = lax.all_to_all(starts, "exp", split_axis=0, concat_axis=0, tiled=True).reshape(
        VHEADS, HEAD, HEAD
    )

    def emit_rows(current_state, step_parts):
        carry_transform, carry_offset, read_transform, read_offset = step_parts
        produced_output = (
            jnp.einsum("urm,umn->urn", read_transform, current_state, precision=highest_precision)
            + read_offset
        )
        return (apply_map(carry_transform, current_state) + carry_offset, produced_output)

    _, produced_output = lax.scan(emit_rows, start_state, span_parts)
    mixer_out = produced_output.transpose(0, 2, 1, 3).reshape(row_count, VHEADS, HEAD)
    gate_rows = output_gate.reshape(row_count, VHEADS, HEAD).astype(jnp.float32)
    normed = mixer_out * lax.rsqrt(
        jnp.mean(mixer_out * mixer_out, axis=-1, keepdims=True) + epsilon
    )
    normed = (
        (normed * norm_gain * jax.nn.silu(gate_rows))
        .reshape(row_count, VHEADS * HEAD)
        .astype(jnp.bfloat16)
    )
    projected = jnp.dot(
        normed,
        lax.all_gather(out_weight, "exp", axis=1, tiled=True),
        preferred_element_type=jnp.float32,
    )
    after_mix = (residual.astype(jnp.float32) + projected).astype(jnp.bfloat16)
    after_wide = after_mix.astype(jnp.float32)
    routed_in = (
        after_wide
        * lax.rsqrt(jnp.mean(after_wide * after_wide, axis=-1, keepdims=True) + epsilon)
        * post_gain
    ).astype(jnp.bfloat16)
    logits = jnp.dot(routed_in, router_weight, preferred_element_type=jnp.float32)
    chosen = jnp.exp(jnp.take_along_axis(logits, expert_ids, axis=1))
    gate_weights = chosen / jnp.sum(chosen, axis=1, keepdims=True)
    ctx_count = lax.axis_size("ctx")
    devices = ctx_count * exp_count
    local_count = expert_gate.shape[0]
    experts_total = local_count * devices
    capacity = row_count * TOP * 6 // (experts_total * 5)
    flat_ids = expert_ids.reshape(-1)
    onehot = (flat_ids[:, None] == jnp.arange(experts_total, dtype=jnp.int32)[None, :]).astype(
        jnp.int32
    )
    slot_rank = jnp.sum((jnp.cumsum(onehot, axis=0) - onehot) * onehot, axis=1)
    token_of = jnp.arange(row_count * TOP, dtype=jnp.int32) // TOP
    outgoing = (
        jnp.zeros((experts_total, capacity, model_width), jnp.bfloat16)
        .at[flat_ids, slot_rank]
        .set(routed_in[token_of])
    )
    shared_hidden = (
        jax.nn.silu(jnp.dot(routed_in, shared_gate, preferred_element_type=jnp.float32))
        * jnp.dot(routed_in, shared_up, preferred_element_type=jnp.float32)
    ).astype(jnp.bfloat16)
    switch_rows = jax.nn.sigmoid(
        jnp.dot(routed_in, shared_switch, preferred_element_type=jnp.float32)
    )
    shared_out = switch_rows[:, None] * jnp.dot(
        shared_hidden, shared_down, preferred_element_type=jnp.float32
    )
    result = run_experts(
        lax.all_to_all(
            outgoing.reshape(devices, local_count, capacity, model_width),
            ("ctx", "exp"),
            split_axis=0,
            concat_axis=0,
            tiled=True,
        ),
        expert_gate,
        expert_up,
        expert_down,
    )
    returned = lax.all_to_all(result, ("ctx", "exp"), split_axis=0, concat_axis=0, tiled=True)
    returned = returned.reshape(experts_total, capacity, model_width)
    pulled = returned[flat_ids, slot_rank].reshape(row_count, TOP, model_width)
    routed = jnp.sum(pulled.astype(jnp.float32) * gate_weights[:, :, None], axis=1)
    return (after_wide + routed + shared_out).astype(jnp.bfloat16)


def solution(mesh):
    return jax.shard_map(
        local,
        mesh=mesh,
        in_specs=(
            P(("ctx", "exp"), None),
            P(("ctx", "exp"), None),
            P(("ctx", "exp"), None),
            P(("ctx", "exp"), None),
            P(("ctx", "exp"), None),
            P(),
            P(),
            P(None, "exp"),
            P(),
            P(),
            P(("ctx", "exp"), None),
            P(("ctx", "exp"), None, None),
            P(("ctx", "exp"), None, None),
            P(("ctx", "exp"), None, None),
            P(),
            P(),
            P(),
            P(),
        ),
        out_specs=P(("ctx", "exp"), None),
        check_vma=False,
    )
```

profile of v0, /device:TPU:0, one launch (start us, length us, event | category | flops | bytes accessed | tf_op | source)
XLA Modules:
  0.0 841.6 jit_solution(13653261362320057624)
XLA Ops:
  7.6 2.4 collective-permute-start
  13.4 1.6 copy.121
  15.1 1.4 copy.120
  16.5 2.0 maximum_convert_fusion
  18.5 4.6 divide_multiply_fusion
  27.4 2.9 fusion.61
  30.2 158.8 %custom-call.4 = f32[2,16,1,64,64]{3,4,2,1,0:T(8,128)} custom-call(f32[2,16,1,64,64]{4,3,2,1,0:T(8,128)} %fusion.61), custom_call_target="InvertDiagBlocksLowerTriangular" | custom-call | tf_op jit(solution)/shard_map/vmap(jit(_solve_triangular))/vmap()/triangular_solve | solution.py:101
  190.4 2.5 copy.125
  193.0 1.7 bitcast_multiply_fusion.4
  194.8 2.0 fusion.43
  196.8 5.1 fusion.80
  202.0 5.3 multiply_subtract_fusion
  207.4 13.4 %while.39 = (s32[]{:T(128)}, f32[16,128,128]{2,1,0:T(8,128)S(1)}, f32[16,128,128]{2,1,0:T(8,128)}, f32[2,16,128,128]{3,2,1,0:T(8,128)}, f32[2,16,128,128]{3,2,1,0:T(8,128)}, /*index=5*/s32[]{:T(128)}, s32[]{:T(128)}) while((s32[]{:T(128)}, f32[16,128,128]{2,1,0:T(8,128)S(1)}, f32[16,128,128]{2,1,0:T(8,128)}, ...), condition=%wide.region_3.4_spmd.clone, body=%wide.region_2.3_spmd.clone.sunk | while | flops 805830656 | bytes 19924088 | solution.py:179
  209.6 3.4 convolution_add_fusion.17
  216.1 3.4 convolution_add_fusion.17
  220.8 19.3 %all_to_all.25 = f32[4,4,128,128]{3,2,1,0:T(8,128)S(1)} all-to-all(f32[4,4,128,128]{3,2,1,0:T(8,128)S(1)} %bitcast.288), channel_id=1, replica_groups=mesh['ctx'=8,'exp'=4] {'exp'}, dimensions={0} | all-to-all | bytes 2097152 | tf_op jit(solution)/shard_map/all_to_all | solution.py:185
  240.1 16.9 %all_to_all.26 = f32[4,4,128,128]{3,2,1,0:T(8,128)S(1)} all-to-all(f32[4,4,128,128]{3,2,1,0:T(8,128)S(1)} %bitcast.289), channel_id=1, replica_groups=mesh['ctx'=8,'exp'=4] {'exp'}, dimensions={0} | all-to-all | bytes 2097152 | tf_op jit(solution)/shard_map/all_to_all | solution.py:192
  265.6 2.0 fusion.105
  270.3 31.5 %reduce-window.6 = s32[64,10,128]{2,1,0:T(8,128)S(1)} reduce-window(s32[64,10,128]{2,1,0:T(8,128)} %fusion.96, s32[]{:T(128)} %copy.231), window={size=1x1x128 pad=0_0x0_0x127_0}, to_apply=%region_10.11 | reduce-window | flops 10403840 | bytes 655364 | tf_op jit(solution)/shard_map/reduce-window
  309.5 2.0 copy.128
  311.5 49.1 %all-gather.8.cloned.1.call-done = f32[32,128,128]{2,1,0:T(8,128)} async-done(((f32[4,128,128]{2,1,0:T(8,128)}), f32[32,128,128]{2,1,0:T(8,128)}) %all-gather.8.cloned.1.call-update) | async-done | bytes 2097168 | tf_op jit(solution)/shard_map/all_gather | solution.py:25
  365.2 4.1 all-to-all-start.2
  369.4 1.4 broadcast_in_dim.43
  371.0 1.8 convolution_multiply_fusion.1
  372.8 2.2 fusion.81
  375.0 2.4 convolution_subtract_fusion
  377.4 17.5 %all-to-all-done.2 = f32[4,4,128,128]{3,2,1,0:T(8,128)S(1)} async-done(((f32[4,4,128,128]{3,2,1,0:T(8,128)}), f32[4,4,128,128]{3,2,1,0:T(8,128)S(1)}, u32[]{:S(2)}, u32[]{:S(2)}) %all-to-all-start.2) | async-done | bytes 1048608 | tf_op jit(solution)/shard_map/all_to_all | solution.py:207
  394.9 10.7 %while.38 = (s32[]{:T(128)}, f32[16,128,128]{2,1,0:T(8,128)S(1)}, f32[2,16,64,128]{3,2,1,0:T(8,128)}, f32[2,16,128,128]{3,2,1,0:T(8,128)}, f32[2,16,128,128]{3,2...) while((s32[]{:T(128)}, f32[16,128,128]{2,1,0:T(8,128)S(1)}, ...), condition=%wide.region_8.9_spmd, body=%wide.region_7.8_spmd.sunk | while | flops 604372992 | bytes 25692356 | solution.py:219
  394.9 3.1 convolution_add_fusion.16
  400.3 3.1 convolution_add_fusion.16
  405.6 1.6 multiply_reduce_fusion.2
  407.3 1.8 copy.130
  409.1 21.1 %all-gather.6.cloned.1.call-done = bf16[2048,2048]{1,0:T(8,128)(2,1)} async-done(((bf16[2048,512]{1,0:T(8,128)(2,1)}), bf16[2048,2048]{1,0:T(8,128)(2,1)}) %all-gather.6.cloned.1.call-update) | async-done | bytes 8388624 | tf_op jit(solution)/shard_map/all_gather | solution.py:232
  430.5 5.7 multiply_reduce_fusion.1
  437.4 34.2 %scatter_custom_fusion = bf16[1536,2048]{1,0:T(8,128)(2,1)} fusion(s32[1280]{0:T(1024)S(1)} %broadcast_select_fusion, bf16[128,2048]{1,0:T(8,128)(2,1)S(1)} %multiply_convert_fusion, s32[2048]{0:T(1024)} %pad_clamp_fusion, bf16[]{:T(256)} %constant.105.clone.1), kind=kCustom, calls=%fused_computation.36 | custom fusion | bytes 6291968
  471.6 143.2 %all_to_all.27 = bf16[32,2,24,2048]{3,2,1,0:T(8,128)(2,1)S(1)} all-to-all(bf16[32,2,24,2048]{3,2,1,0:T(8,128)(2,1)} %bitcast.295), channel_id=1, replica_groups=mesh['ctx'=8,'exp'=4] {'ctx','exp'}, dimensions={0} | all-to-all | bytes 12582912 | tf_op jit(solution)/shard_map/all_to_all | solution.py:272
  614.8 2.6 copy-done.10
  617.5 5.1 fusion.22
  622.6 12.6 %convert_bitcast_fusion = bf16[32,2,24,2048]{3,2,0,1:T(8,128)(2,1)} fusion(bf16[2,512,2048]{2,1,0:T(8,128)(2,1)} %param.37, f32[2,32,24,512]{3,2,1,0:T(8,128)} %fusion.22, bf16[2,2048,512]{2,1,0:T(8,128)(2,1)} %param.35, bf16[32,2,24,2048]{3,2,1,0:T(8,128)(2,1)} %copy-done.10), kind=kOutput, calls=%fused_computation.31 | convolution fusion | flops 6450315264 | bytes 24117248 | tf_op jit(solution)/shard_map/nesf,efd->nesd/dot_general | solution.py:137
  635.2 6.5 copy.140
  641.7 4.1 all-to-all-start.4
  646.5 8.2 gather_fusion.1
  655.3 2.1 fusion.127
  657.4 128.5 %all-to-all-done.4 = bf16[32,2,24,2048]{3,2,1,0:T(8,128)(2,1)} async-done(((bf16[32,2,24,2048]{3,2,1,0:T(8,128)(2,1)}), bf16[32,2,24,2048]{3,2,1,0:T(8,128)(2,1)}, u32[]{:S(2)}, u32[]{:S(2)}) %all-to-all-start.4) | async-done | bytes 6291488 | tf_op jit(solution)/shard_map/all_to_all | solution.py:283
  785.9 24.2 %gather_fusion = bf16[1280,2048]{1,0:T(8,128)(2,1)} fusion(bf16[64,24,2048]{2,1,0:T(8,128)(2,1)} %bitcast.63, s32[1280]{0:T(1024)S(1)} %get-tuple-element.172), kind=kCustom, calls=%fused_computation.1 | custom fusion | bytes 10496000 | tf_op jit(solution)/shard_map/gather | solution.py:285
  810.1 10.3 %reshape.292 = f32[128,10,2048]{2,1,0:T(8,128)} reshape(bf16[1280,2048]{1,0:T(8,128)(2,1)} %gather_fusion) | data formatting | bytes 15728640 | tf_op jit(solution)/shard_map/convert_element_type | solution.py:286
  820.4 10.5 %multiply_reduce_fusion = f32[128,2048]{1,0:T(8,128)} fusion(f32[128,10,2048]{2,1,0:T(8,128)} %reshape.292, f32[128,10]{1,0:T(8,128)S(1)} %copy.143), kind=kLoop, calls=%fused_computation.30 | loop fusion | flops 4980736 | bytes 11539456 | tf_op jit(solution)/shard_map/reduce_sum | solution.py:286
  831.0 3.9 fusion.39
  (154 shorter events, 47.3 us)
Async XLA Ops:
  6.5 824.4 %copy-start = (bf16[512,2048]{1,0:T(8,128)(2,1)S(1)}, bf16[512,2048]{1,0:T(8,128)(2,1)}, u32[]{:S(2)}) copy-start(bf16[512,2048]{1,0:T(8,128)(2,1)} %param.40) | copy-start | bytes 6291460
  6.5 305.0 %all-gather.10.cloned.1.call-start = ((), (), s32[]{:S(2)}) async-start(), calls=%async_computation.7 | async-start | bytes 2359296 | tf_op jit(solution)/shard_map/all_gather | solution.py:25
  7.6 7.5 collective-permute-start
  13.4 13.9 %copy-start.22 = (pred[64,64]{1,0:T(8,128)(4,1)}, pred[64,64]{1,0:T(8,128)(4,1)S(1)}, u32[]{:S(2)}) copy-start(pred[64,64]{1,0:T(8,128)(4,1)S(1)} %get-tuple-element.188) | copy-start | bytes 12292
  27.3 174.6 %copy-start.3 = (f32[128,8,2,128]{3,0,2,1:T(8,128)}, f32[128,8,2,128]{3,0,2,1:T(8,128)S(1)}, u32[]{:S(2)}) copy-start(f32[128,8,2,128]{3,0,2,1:T(8,128)S(1)} %broadcast_in_dim.38) | copy-start | bytes 3145732
  193.0 1.7 copy-start.11
  193.0 1.9 copy-start.19
  196.8 5.2 copy-start.5
  207.7 1.9 copy-start.1
  214.2 1.9 copy-start.1
  220.8 19.3 %copy-start.2 = (f32[16,128,128]{2,1,0:T(8,128)S(1)}, f32[16,128,128]{2,1,0:T(8,128)}, u32[]{:S(2)}) copy-start(f32[16,128,128]{2,1,0:T(8,128)} %get-tuple-element.115) | copy-start | bytes 3145732
  240.1 19.5 %copy-start.9 = (f32[4,4,128,128]{3,2,1,0:T(8,128)}, f32[4,4,128,128]{3,2,1,0:T(8,128)S(1)}, u32[]{:S(2)}) copy-start(f32[4,4,128,128]{3,2,1,0:T(8,128)S(1)} %all_to_all.25) | copy-start | bytes 3145732
  257.4 0.7 copy-start.15
  258.5 0.7 copy-start.18
  259.6 0.7 copy-start.16
  261.5 99.1 %all-gather.8.cloned.1.call-start = ((), (), s32[]{:S(2)}) async-start(), calls=%async_computation.6 | async-start | bytes 2359296 | tf_op jit(solution)/shard_map/all_gather | solution.py:25
  264.2 4.2 copy-start.21
  267.6 162.6 %all-gather.6.cloned.1.call-start = ((), (), s32[]{:S(2)}) async-start(), calls=%async_computation.5 | async-start | bytes 10485760 | tf_op jit(solution)/shard_map/all_gather | solution.py:232
  360.6 3.1 copy-start.17
  365.2 5.5 copy-start.23
  365.2 29.7 %all-to-all-start.2 = ((f32[4,4,128,128]{3,2,1,0:T(8,128)}), f32[4,4,128,128]{3,2,1,0:T(8,128)S(1)}, u32[]{:S(2)}, u32[]{:S(2)}) async-start(f32[4,4,128,128]{3,2,1,0:T(8,128)} %pad_maximum_fusion), calls=%async_computation.2 | async-start | bytes 2097152 | tf_op jit(solution)/shard_map/all_to_all | solution.py:207
  369.3 1.6 copy-start.4
  369.3 3.5 copy-start.6
  394.9 3.1 copy-start.7
  394.9 3.1 copy-start.8
  394.9 3.1 copy-start.12
  399.2 1.0 copy-start.13
  400.3 3.1 copy-start.7
  400.3 3.1 copy-start.8
  400.3 3.1 copy-start.12
  404.5 1.0 copy-start.13
  430.5 6.7 copy-start.24
  436.2 1.0 copy-start.14
  471.6 145.9 %copy-start.26 = (bf16[2,2048,512]{2,1,0:T(8,128)(2,1)S(1)}, bf16[2,2048,512]{2,1,0:T(8,128)(2,1)}, u32[]{:S(2)}) copy-start(bf16[2,2048,512]{2,1,0:T(8,128)(2,1)} %param.36) | copy-start | bytes 12582916
  614.8 2.6 copy-start.10
  641.7 4.4 copy-start.25
  641.7 4.4 copy-start.20
  641.7 144.1 %all-to-all-start.4 = ((bf16[32,2,24,2048]{3,2,1,0:T(8,128)(2,1)}), bf16[32,2,24,2048]{3,2,1,0:T(8,128)(2,1)}, u32[]{:S(2)}, u32[]{:S(2)}) async-start(bf16[32,2,24,2048]{3,2,1,0:T(8,128)(2,1)} %copy.140), calls=%async_computation.4 | async-start | bytes 12582912 | tf_op jit(solution)/shard_map/all_to_all | solution.py:283
Sparse Core Ops, SparseCore 0:
  261.6 48.3 all-gather.9
  312.1 48.3 all-gather.7
  362.1 68.0 all-gather.5
where the time goes:
time: 849 us; the launch traced here: 842 us
  other arithmetic  220 us (26%)
  waiting for transfers between devices  217 us (26%)
  blocking collectives  179 us (21%)
  local copies, waits for them, and re-layouts  120 us (14%)
  matrix products  80.9 us (10%)
  between operations  14 us (2%)
  starting transfers between devices  10.6 us (1%)
    another operation x4, other arithmetic, span_terms(): jax.scipy.linalg.solve_triangular(system, right_operand, lower=True, unit...  159 us
    all_to_all x1, blocking collectives, local(): lax.all_to_all(outgoing.reshape(devices, local_count, capacity, model_wid...  143 us
    all_to_all x1, waiting for transfers between devices, local(): lax.all_to_all(result, ('ctx', 'exp'), split_axis=0, concat_axis=0, tiled...  129 us
    all_gather x2, waiting for transfers between devices, entering(): gathered = jax.tree.map(lambda a: lax.all_gather(a, axis), part)  49.1 us
    unnamed x48, local copies, waits for them, and re-layouts  42.1 us
    another operation x3, other arithmetic  32.3 us
    dot_general x18, matrix products, apply_map(): jnp.einsum('coq,cqd->cod', left_transform, right_operand, precision=highe...  27 us
    gather x1, local copies, waits for them, and re-layouts, local(): pulled = returned[flat_ids, slot_rank].reshape(row_count, TOP, model_width)  24.2 us
  transfers between devices with their start and end apart: 6, of which 4 were waited for; matrix products, arithmetic and copies ran while one was open for 11% of the time, Pallas kernels for 0%

commit v1 on v0

v1 whole, which is shorter than its diff:
```python
import functools

import jax
import jax.numpy as jnp
from jax import lax
from jax.experimental import pallas as pl
from jax.experimental.pallas import tpu as pltpu
from jax.sharding import PartitionSpec as P

AXES = ("ctx", "exp")
EPS = 1e-06
F32, BF16 = jnp.float32, jnp.bfloat16


def dot(a, b, dims=((1,), (0,))):
    return lax.dot_general(a, b, (dims, ((), ())), preferred_element_type=F32)


def halves(x):
    hi = x.astype(BF16)
    return hi, (x - hi.astype(F32)).astype(BF16)


def dot_square(a, b):
    n = b.shape[1]
    ah, al = halves(a)
    bh, bl = halves(b)
    left = jnp.concatenate([ah, al], axis=1)
    right = jnp.concatenate(
        [jnp.concatenate([bh, bl], axis=1), jnp.concatenate([bh, jnp.zeros_like(bl)], axis=1)], axis=0
    )
    both = dot(left, right)
    return both[:, :n] + both[:, n:]


def dot_wide(a, b):
    ah, al = halves(a)
    bh, bl = halves(b)
    return dot(jnp.concatenate([ah, al], axis=1), jnp.concatenate([bh, bh], axis=0)) + dot(ah, bl)


def unit_lower_inverse(lower):
    n = lower[0].shape[0]
    row = lax.broadcasted_iota(jnp.int32, (n, n), 0)
    col = lax.broadcasted_iota(jnp.int32, (n, n), 1)
    eye = jnp.where(row == col, 1.0, 0.0)
    size = 1
    done = None
    while size < n:
        pair = (row // (2 * size) == col // (2 * size)) & (row // size != col // size)
        corner = [jnp.where(pair, m, 0.0) for m in lower]
        if size == 1:
            done = [eye - c for c in corner]
        else:
            half = [dot_square(d, c) for d, c in zip(done, corner)]
            done = [d - dot_square(h, d) for d, h in zip(done, half)]
        size *= 2
    return done


def delta_kernel(q_ref, k_ref, v_ref, qb_ref, kb_ref, vb_ref, qw_ref, kw_ref, vw_ref, cols_ref, rows_ref, map_ref, read_ref, *, head, per):
    rows = q_ref.shape[0]
    groups = q_ref.shape[1] // head

    def conv(x_ref, b_ref, w_ref):
        x = jnp.concatenate([b_ref[...].astype(F32), x_ref[...].astype(F32)], axis=0)
        w = w_ref[...]
        y = w[3:4] * x[8 : 8 + rows]
        for tap in range(3):
            y = y + w[tap : tap + 1] * x[5 + tap : 5 + tap + rows]
        return y / (1.0 + jnp.exp(-y))

    def unit(x):
        return x * lax.rsqrt(jnp.sum(x * x, axis=-1, keepdims=True) + EPS)

    q_all, k_all, v_all = conv(q_ref, qb_ref, qw_ref), conv(k_ref, kb_ref, kw_ref), conv(v_ref, vb_ref, vw_ref)
    row = lax.broadcasted_iota(jnp.int32, (rows, rows), 0)
    col = lax.broadcasted_iota(jnp.int32, (rows, rows), 1)
    lower, info = [], []
    for g in range(groups):
        q = unit(q_all[:, g * head : (g + 1) * head]) * head**-0.5
        k = unit(k_all[:, g * head : (g + 1) * head])
        kh, kl = halves(k)
        qh, ql = halves(q)
        top = jnp.concatenate([jnp.concatenate([kh, kl], axis=1), jnp.concatenate([qh, ql], axis=1)], axis=0)
        inner = dot(top, jnp.concatenate([kh, kh], axis=1), ((1,), (1,)))
        inner = inner + dot(jnp.concatenate([kh, qh], axis=0), kl, ((1,), (1,)))
        kk, qk = inner[:rows], inner[rows:]
        for i in range(per):
            j = g * per + i
            cum_col = cols_ref[j, :, 0:1]
            strength = cols_ref[j, :, 1:2]
            cum_row = rows_ref[j, 0:1, :]
            gap = cum_col - cum_row
            ratios = jnp.where(row >= col, jnp.exp(jnp.where(row >= col, gap, 0.0)), 0.0)
            lower.append(jnp.where(row > col, ratios * kk, 0.0) * strength)
            info.append((q, k, v_all[:, j * head : (j + 1) * head], cum_col, strength, qk * ratios))
    inverse = unit_lower_inverse(lower)
    for j, (q, k, v, cum, strength, scores) in enumerate(info):
        decay = jnp.exp(cum)
        right = jnp.concatenate([strength * decay * k, strength * v], axis=1)
        solved = dot_wide(inverse[j], right)
        last = cum[rows - 1 : rows]
        to_end = k * jnp.exp(last - cum)
        update = dot_wide(to_end.T, solved)
        end = jnp.exp(last)
        diag = lax.broadcasted_iota(jnp.int32, (head, head), 0) == lax.broadcasted_iota(jnp.int32, (head, head), 1)
        map_ref[j, :, :head] = jnp.where(diag, end, 0.0) - update[:, :head]
        map_ref[j, :, head:] = update[:, head:]
        read = dot_wide(scores, solved)
        read_ref[j, :, :head] = q * decay - read[:, :head]
        read_ref[j, :, head:] = read[:, head:]


def delta_terms(mixed, before, conv_weight, log_decay, write_strength, head):
    rows, vheads = log_decay.shape
    kheads = (mixed.shape[1] // head - vheads) // 2
    per = vheads // kheads
    together = 2 if kheads % 2 == 0 else 1
    steps = kheads // together
    causal = jnp.tril(jnp.ones((rows, rows), F32))
    cumul = jnp.dot(causal, log_decay, precision=lax.Precision.HIGHEST)
    cols = jnp.stack([cumul.T, write_strength.T], axis=2)
    lines = cumul.T[:, None, :]
    qw, vw = together * head, together * per * head
    k_at, v_at = kheads * head // qw, 2 * kheads * head // vw

    def spec(height, width, at):
        return pl.BlockSpec((height, width), lambda s: (0, s + at))

    n = together * per
    return pl.pallas_call(
        functools.partial(delta_kernel, head=head, per=per),
        grid=(steps,),
        in_specs=[spec(h, w, a) for h in (rows, 8, 4) for w, a in ((qw, 0), (qw, k_at), (vw, v_at))]
        + [
            pl.BlockSpec((n, rows, 2), lambda s: (s, 0, 0)),
            pl.BlockSpec((n, 1, rows), lambda s: (s, 0, 0)),
        ],
        out_specs=[pl.BlockSpec((n, head, 2 * head), lambda s: (s, 0, 0)), pl.BlockSpec((n, rows, 2 * head), lambda s: (s, 0, 0))],
        out_shape=[jax.ShapeDtypeStruct((vheads, head, 2 * head), F32), jax.ShapeDtypeStruct((vheads, rows, 2 * head), F32)],
        compiler_params=pltpu.CompilerParams(vmem_limit_bytes=40 * 2**20),
        name="delta_terms",
    )(mixed, mixed, mixed, before, before, before, conv_weight, conv_weight, conv_weight, cols, lines)


def emit_kernel(read_ref, state_ref, gate_ref, gain_ref, out_ref):
    n, rows, head2 = read_ref.shape
    head = head2 // 2
    for j in range(n):
        out = dot_square(read_ref[j, :, :head], state_ref[j]) + read_ref[j, :, head:]
        normed = out * lax.rsqrt(jnp.mean(out * out, axis=-1, keepdims=True) + EPS)
        gate = gate_ref[:, j * head : (j + 1) * head].astype(F32)
        out_ref[:, j * head : (j + 1) * head] = (normed * gain_ref[...] * (gate / (1.0 + jnp.exp(-gate)))).astype(BF16)


def emit(read, state, output_gate, gain):
    vheads, rows, head2 = read.shape
    head = head2 // 2
    n = 4 if vheads % 4 == 0 else 1
    return pl.pallas_call(
        emit_kernel,
        grid=(vheads // n,),
        in_specs=[
            pl.BlockSpec((n, rows, head2), lambda s: (s, 0, 0)),
            pl.BlockSpec((n, head, head), lambda s: (s, 0, 0)),
            pl.BlockSpec((rows, n * head), lambda s: (0, s)),
            pl.BlockSpec((1, head), lambda s: (0, 0)),
        ],
        out_specs=pl.BlockSpec((rows, n * head), lambda s: (0, s)),
        out_shape=jax.ShapeDtypeStruct((rows, vheads * head), BF16),
        name="emit",
    )(read, state, output_gate, gain[None])


def apply(transform, right):
    return jnp.einsum("hij,hjk->hik", transform, right, precision=lax.Precision.HIGHEST)


def starting_states(block_map, count, place):
    head = block_map.shape[1]
    levels, step = [], 1
    held = block_map
    while count % (2 * step) == 0 and 4 * step < count and held.shape[0] % 2 == 0:
        share = held.shape[0] // 2
        upper = (place // step) % 2 == 1
        keep = jnp.where(upper, held[share:], held[:share])
        give = jnp.where(upper, held[:share], held[share:])
        got = lax.ppermute(give, AXES, [(i, i ^ step) for i in range(count)])
        early, late = jnp.where(upper, got, keep), jnp.where(upper, keep, got)
        merged = apply(late[:, :, :head], early)
        held = jnp.concatenate([merged[:, :, :head], merged[:, :, head:] + late[:, :, head:]], axis=2)
        levels.append((step, upper, early))
        step *= 2
    state = jnp.zeros_like(held[:, :, head:])
    for turn in range(count // step - 1):
        ahead = held[:, :, head:]
        if turn:
            ahead = ahead + apply(held[:, :, :head], state)
        state = lax.ppermute(ahead, AXES, [(i, i + step) for i in range(count - step)])
    for step, upper, early in reversed(levels):
        second = apply(early[:, :, :head], state) + early[:, :, head:]
        mine, other = jnp.where(upper, second, state), jnp.where(upper, state, second)
        got = lax.ppermute(other, AXES, [(i, i ^ step) for i in range(count)])
        state = jnp.where(upper, jnp.concatenate([got, mine], axis=0), jnp.concatenate([mine, got], axis=0))
    return state


def local(
    residual,
    mixed_qkv,
    output_gate,
    log_decay,
    write_strength,
    conv_weight,
    norm_gain,
    out_weight,
    post_gain,
    router_weight,
    expert_ids,
    expert_gate,
    expert_up,
    expert_down,
    shared_gate,
    shared_up,
    shared_down,
    shared_switch,
):
    rows, width = residual.shape
    head = norm_gain.shape[0]
    count = lax.axis_size(AXES)
    place = lax.axis_index(AXES)
    before = lax.ppermute(mixed_qkv[rows - 8 :], AXES, [(i, i + 1) for i in range(count - 1)])
    block_map, read = delta_terms(mixed_qkv, before, conv_weight, log_decay, write_strength, head)
    state = starting_states(block_map, count, place)
    normed = emit(read, state, output_gate, norm_gain)
    projected = jnp.dot(normed, lax.all_gather(out_weight, "exp", axis=1, tiled=True), preferred_element_type=F32)
    after_mix = (residual.astype(F32) + projected).astype(BF16)
    after_wide = after_mix.astype(F32)
    routed_in = (
        after_wide * lax.rsqrt(jnp.mean(after_wide * after_wide, axis=-1, keepdims=True) + EPS) * post_gain
    ).astype(BF16)

    local_count = expert_gate.shape[0]
    experts = local_count * count
    top = expert_ids.shape[1]
    capacity = rows * top * 6 // (experts * 5)
    named = jnp.any(expert_ids[:, :, None] == jnp.arange(experts, dtype=jnp.int32), axis=1)
    earlier = jnp.dot(jnp.tril(jnp.ones((rows, rows), BF16), -1), named.astype(BF16), preferred_element_type=F32)
    slot = jnp.where(named, earlier.astype(jnp.int32), capacity)
    picks = (slot.T[:, None, :] == jnp.arange(capacity, dtype=jnp.int32)[None, :, None]).reshape(experts * capacity, rows)

    logits = jnp.dot(routed_in, router_weight, preferred_element_type=F32)
    chosen = jnp.where(named, jnp.exp(jnp.where(named, logits, 0.0)), 0.0)
    gates = chosen / jnp.sum(chosen, axis=1, keepdims=True)
    outgoing = jnp.dot(picks.astype(BF16), routed_in, preferred_element_type=F32).astype(BF16)
    received = lax.all_to_all(
        outgoing.reshape(count, local_count, capacity, width), AXES, split_axis=0, concat_axis=0, tiled=True
    )
    shared_hidden = (
        jax.nn.silu(jnp.dot(routed_in, shared_gate, preferred_element_type=F32))
        * jnp.dot(routed_in, shared_up, preferred_element_type=F32)
    ).astype(BF16)
    switch = jax.nn.sigmoid(jnp.dot(routed_in, shared_switch, preferred_element_type=F32))
    shared_out = switch[:, None] * jnp.dot(shared_hidden, shared_down, preferred_element_type=F32)

    received = received.transpose(1, 0, 2, 3).reshape(local_count, count * capacity, width)
    gate_part = jnp.einsum("esd,edf->esf", received, expert_gate, preferred_element_type=F32)
    up_part = jnp.einsum("esd,edf->esf", received, expert_up, preferred_element_type=F32)
    hidden = (jax.nn.silu(gate_part) * up_part).astype(BF16)
    result = jnp.einsum("esf,efd->esd", hidden, expert_down, preferred_element_type=F32).astype(BF16)
    result = result.reshape(local_count, count, capacity, width).transpose(1, 0, 2, 3)
    returned = lax.all_to_all(result, AXES, split_axis=0, concat_axis=0, tiled=True)
    spread = jnp.where(slot[:, :, None] == jnp.arange(capacity, dtype=jnp.int32), gates[:, :, None], 0.0)
    spread_hi, spread_lo = halves(spread.reshape(rows, experts * capacity))
    pulled = jnp.dot(
        jnp.concatenate([spread_hi, spread_lo], axis=0),
        returned.reshape(experts * capacity, width),
        preferred_element_type=F32,
    )
    return (after_wide + pulled[:rows] + pulled[rows:] + shared_out).astype(BF16)


def solution(mesh):
    rows = P(AXES, None)
    return jax.shard_map(
        local,
        mesh=mesh,
        in_specs=(rows, rows, rows, rows, rows, P(), P(), P(None, "exp"), P(), P(), rows)
        + (P(AXES, None, None),) * 3
        + (P(),) * 4,
        out_specs=rows,
        check_vma=False,
    )
```

time: 849 us -> 463 us (0.55)
  other arithmetic: 220 us -> 8.7 us
  local copies, waits for them, and re-layouts: 120 us -> 17.5 us
  blocking collectives: 179 us -> 143 us
  matrix products: 80.9 us -> 45.8 us
  waiting for transfers between devices: 217 us -> 189 us
  Pallas kernels: 0 us -> 18 us
  starting transfers between devices: 10.6 us -> 26.7 us
    another operation x9 -> x1, other arithmetic: 193 us -> 0.75 us  [delta_terms(): cols = jnp.stack([cumul.T, write_strength.T], axis=2)]
    ppermute x1 -> x10, waiting for transfers between devices: 0.01 us -> 52.6 us  [the longest x3 33.2 us: starting_states(): got = lax.ppermute(give, AXES, [(i, i ^ step) for i in range(count)])]
    all_gather x2 -> x0, waiting for transfers between devices: 49.1 us -> none  [entering(): gathered = jax.tree.map(lambda a: lax.all_gather(a, axis), part)]
    all_to_all x3 -> x1, blocking collectives: 179 us -> 143 us  [local(): lax.all_to_all(outgoing.reshape(count, local_count, capacity, width), AXE...]
    unnamed x48 -> x33, local copies, waits for them, and re-layouts: 42.1 us -> 7.51 us
    gather x6 -> x0, local copies, waits for them, and re-layouts: 32.9 us -> none  [the longest x1 24.2 us: local(): pulled = returned[flat_ids, slot_rank].reshape(row_count, TOP, model_width)]
    dot_general x32 -> x18, matrix products: 73.2 us -> 40.8 us  [the longest x1 12.4 us: local(): jnp.einsum('esf,efd->esd', hidden, expert_down, preferred_element_type=F32)]
    all_gather x1, waiting for transfers between devices: 21.1 us -> 0.01 us  [local(): lax.all_gather(out_weight, 'exp', axis=1, tiled=True)]
  transfers between devices with their start and end apart: 6 -> 12, of which waited for: 4 -> 10; matrix products, arithmetic and copies ran while one was open for 11% -> 4% of each run, Pallas kernels for 0% -> 4%
where the time goes in v1:
time: 463 us
  waiting for transfers between devices  189 us (41%)
  blocking collectives  143 us (31%)
  matrix products  45.8 us (10%)
  starting transfers between devices  26.7 us (6%)
  Pallas kernels  18 us (4%)
  local copies, waits for them, and re-layouts  17.5 us (4%)
  between operations  13.8 us (3%)
  other arithmetic  8.7 us (2%)
    all_to_all x1, blocking collectives, local(): lax.all_to_all(outgoing.reshape(count, local_count, capacity, width), AXE...  143 us
    all_to_all x1, waiting for transfers between devices, local(): lax.all_to_all(result, AXES, split_axis=0, concat_axis=0, tiled=True)  136 us
    ppermute x3, waiting for transfers between devices, starting_states(): got = lax.ppermute(give, AXES, [(i, i ^ step) for i in range(count)])  33.2 us
    ppermute x3, starting transfers between devices, starting_states(): lax.ppermute(ahead, AXES, [(i, i + step) for i in range(count - step)])  13.7 us
    pallas_call x1, Pallas kernels, delta_terms(): pl.pallas_call(functools.partial(delta_kernel, head=head, per=per), grid=...  13.7 us
    dot_general x1, matrix products, local(): jnp.einsum('esf,efd->esd', hidden, expert_down, preferred_element_type=F32)  12.4 us
    ppermute x3, waiting for transfers between devices, starting_states(): got = lax.ppermute(other, AXES, [(i, i ^ step) for i in range(count)])  12.1 us
  transfers between devices with their start and end apart: 12, of which 10 were waited for; matrix products, arithmetic and copies ran while one was open for 4% of the time, Pallas kernels for 4%

profile of v1, /device:TPU:0, one launch (start us, length us, event | category | flops | bytes accessed | tf_op | source)
XLA Modules:
  0.0 462.8 jit_solution(13532348099206478512)
XLA Ops:
  6.5 0.7 all-gather.2.cloned.1.call-update
  7.3 0.8 slice.87
  8.1 2.3 collective-permute-start
  10.5 0.9 fusion.40
  11.4 0.7 pad_maximum_fusion.2
  12.1 1.4 copy.28.cols_ref
  13.5 1.2 copy-done.3
  14.7 13.7 %delta_terms.1 = (f32[16,128,256]{2,1,0:T(8,128)S(1)}, f32[16,128,256]{2,1,0:T(8,128)S(1)}) custom-call(bf16[128,4096]{1,0:T(8,128)(2,1)S(1)} %copy-done.1, bf16[128,4096]{1,0:T(8,128)(2,1)S(1)} %copy-done.1, bf16[128,4096]{1,0:T(8,128)(2,1)S(1)} %copy-done.1, bf16[8,4096]{1,0:T(8,128)(2,1)S(1)} %collective-permute-done.qb_ref.kb_ref.vb_ref, ...), custom_call_target="tpu_custom_call" | custom-call | tf_op jit(solution)/shard_map/delta_terms/pallas_call | solution.py:132
  28.4 1.3 copy-done.2
  29.9 0.5 copy-done.4
  30.5 2.6 collective-permute-start.1
  33.0 2.4 collective-permute-done.1
  35.5 2.1 broadcast_select_fusion.1
  37.6 1.0 fusion.22
  38.7 0.9 broadcast_select_fusion.4
  39.6 1.4 collective-permute-start.2
  41.0 24.7 %collective-permute-done.2 = f32[4,128,256]{2,1,0:T(8,128)} collective-permute-done((f32[4,128,256]{2,1,0:T(8,128)}, f32[4,128,256]{2,1,0:T(8,128)}, u32[]{:S(2)}, u32[]{:S(2)}) %collective-permute-start.2) | collective-permute-done | bytes 524320 | tf_op jit(solution)/shard_map/ppermute | solution.py:189
  65.7 1.2 broadcast_select_fusion.3
  66.9 0.6 fusion.27
  67.6 1.7 collective-permute-start.3
  69.3 6.1 %collective-permute-done.3 = f32[2,128,256]{2,1,0:T(8,128)S(1)} collective-permute-done((f32[2,128,256]{2,1,0:T(8,128)S(1)}, f32[2,128,256]{2,1,0:T(8,128)S(1)}, u32[]{:S(2)}, u32[]{:S(2)}) %collective-permute-start.3) | collective-permute-done | bytes 262176 | tf_op jit(solution)/shard_map/ppermute | solution.py:189
  75.8 4.8 %collective-permute-start.4 = (f32[2,128,128]{2,1,0:T(8,128)S(1)}, f32[2,128,128]{2,1,0:T(8,128)S(1)}, u32[]{:S(2)}, u32[]{:S(2)}) collective-permute-start(f32[2,128,128]{2,1,0:T(8,128)S(1)} %slice_add_fusion.4), channel_id=1, source_target_pairs={{0,8},{1,9},{2,10},{3,11},{4,12},{5,13},{6,14},{7,15},{8,16},{9,17... | collective-permute-start | bytes 393224 | tf_op jit(solution)/shard_map/ppermute | solution.py:200
  80.6 2.5 collective-permute-done.4
  83.4 4.4 collective-permute-start.5
  87.8 2.5 collective-permute-done.5
  90.5 4.5 collective-permute-start.6
  95.1 2.3 collective-permute-done.6
  98.0 4.7 %collective-permute-done.7 = f32[2,128,128]{2,1,0:T(8,128)S(1)} collective-permute-done((f32[2,128,128]{2,1,0:T(8,128)S(1)}, f32[2,128,128]{2,1,0:T(8,128)S(1)}, u32[]{:S(2)}, u32[]{:S(2)}) %collective-permute-start.7) | collective-permute-done | bytes 131104 | tf_op jit(solution)/shard_map/ppermute | solution.py:204
  103.6 6.0 %collective-permute-done.8 = f32[4,128,128]{2,1,0:T(8,128)S(1)} collective-permute-done((f32[4,128,128]{2,1,0:T(8,128)S(1)}, f32[4,128,128]{2,1,0:T(8,128)S(1)}, u32[]{:S(2)}, u32[]{:S(2)}) %collective-permute-start.8) | collective-permute-done | bytes 262176 | tf_op jit(solution)/shard_map/ppermute | solution.py:204
  109.6 1.5 broadcast_select_fusion.7
  111.7 1.4 collective-permute-done.9
  113.2 0.8 copy-done.11
  114.0 2.3 maximum_select_fusion.state_ref
  116.3 4.4 emit.1
  120.7 5.0 %multiply_reduce_fusion = (f32[128]{0:T(128)S(1)}, f32[128,2048]{1,0:T(8,128)S(1)}) fusion(bf16[128,2048]{1,0:T(8,128)(2,1)} %emit.1, bf16[2048,2048]{1,0:T(8,128)(2,1)} %all-gather.2.cloned.1.call-done, bf16[128,2048]{1,0:T(8,128)(2,1)S(1)} %copy-done.10), kind=kOutput, calls=%fused_computation.34 | convolution fusion | flops 1075314560 | bytes 10486272 | tf_op jit(solution)/shard_map/dot_general | solution.py:237
  125.7 1.0 copy-done.6
  126.8 1.8 convolution_convert_fusion
  128.6 143.2 %all_to_all.10 = bf16[32,2,24,2048]{3,2,1,0:T(8,128)(2,1)S(1)} all-to-all(bf16[32,2,24,2048]{3,2,1,0:T(8,128)(2,1)S(1)} %bitcast.77), channel_id=1, replica_groups=mesh['ctx'=8,'exp'=4] {'ctx','exp'}, dimensions={0} | all-to-all | bytes 12582912 | tf_op jit(solution)/shard_map/all_to_all | solution.py:257
  271.8 1.1 copy.29
  273.0 2.6 copy-done.7
  275.6 7.2 %fusion.61 = f32[2,768,512]{2,1,0:T(8,128)} fusion(bf16[2,768,2048]{2,1,0:T(8,128)(2,1)S(1)} %bitcast.80, bf16[2,2048,512]{2,1,0:T(8,128)(2,1)} %param.29), kind=kOutput, calls=%fused_computation.119 | convolution fusion | flops 3221225472 | bytes 13631488 | tf_op jit(solution)/shard_map/esd,edf->esf/dot_general | solution.py:268
  282.8 12.4 %convolution_convert_fusion.1 = bf16[2,768,2048]{2,1,0:T(8,128)(2,1)} fusion(bf16[2,512,2048]{2,1,0:T(8,128)(2,1)} %param.31, f32[2,768,512]{2,1,0:T(8,128)} %fusion.61, bf16[2,768,2048]{2,1,0:T(8,128)(2,1)} %bitcast.81, bf16[2,2048,512]{2,1,0:T(8,128)(2,1)} %param.30), kind=kOutput, calls=%fused_computation.2 | convolution fusion | flops 6450315264 | bytes 24117248 | tf_op jit(solution)/shard_map/esf,efd->esd/dot_general | solution.py:271
  295.2 6.5 %copy.32 = bf16[2,32,24,2048]{3,2,0,1:T(8,128)(2,1)} copy(bf16[2,32,24,2048]{3,2,1,0:T(8,128)(2,1)} %bitcast.82) | data formatting | bytes 12582912 | tf_op jit(solution)/shard_map/reshape | solution.py:272
  301.7 4.1 all-to-all-start.1
  307.0 2.8 fusion.62
  309.8 135.9 %all-to-all-done.1 = bf16[32,2,24,2048]{3,2,1,0:T(8,128)(2,1)} async-done(((bf16[32,2,24,2048]{3,2,1,0:T(8,128)(2,1)}), bf16[32,2,24,2048]{3,2,1,0:T(8,128)(2,1)}, u32[]{:S(2)}, u32[]{:S(2)}) %all-to-all-start.1) | async-done | bytes 6291488 | tf_op jit(solution)/shard_map/all_to_all | solution.py:273
  445.6 6.0 %fusion.13 = f32[256,2048]{1,0:T(8,128)} fusion(bf16[1536,2048]{1,0:T(8,128)(2,1)} %bitcast.15, bf16[128,1536]{0,1:T(8,128)(2,1)S(1)} %fusion.19, bf16[128,1536]{0,1:T(8,128)(2,1)S(1)} %fusion.18), kind=kOutput, calls=%fused_computation.37 | convolution fusion | flops 1612185600 | bytes 9175040 | tf_op jit(solution)/shard_map/dot_general | solution.py:276
  451.6 4.3 fusion.3
  (57 shorter events, 4.8 us)
Async XLA Ops:
  6.5 445.1 %copy-start = (bf16[512,2048]{1,0:T(8,128)(2,1)S(1)}, bf16[512,2048]{1,0:T(8,128)(2,1)}, u32[]{:S(2)}) copy-start(bf16[512,2048]{1,0:T(8,128)(2,1)} %param.34) | copy-start | bytes 6291460
  6.5 7.0 %copy-start.1 = (bf16[128,4096]{1,0:T(8,128)(2,1)S(1)}, bf16[128,4096]{1,0:T(8,128)(2,1)}, u32[]{:S(2)}) copy-start(bf16[128,4096]{1,0:T(8,128)(2,1)} %v_ref.1) | copy-start | bytes 3145732
  6.5 7.0 %copy-start.5 = (f32[4,4096]{1,0:T(4,128)S(1)}, f32[4,4096]{1,0:T(4,128)}, u32[]{:S(2)}) copy-start(f32[4,4096]{1,0:T(4,128)} %vw_ref.1) | copy-start | bytes 196612
  6.5 114.1 %all-gather.2.cloned.1.call-start = ((), (), s32[]{:S(2)}) async-start(), calls=%async_computation.2 | async-start | bytes 10485760 | tf_op jit(solution)/shard_map/all_gather | solution.py:237
  8.1 5.4 %collective-permute-start = (bf16[8,4096]{1,0:T(8,128)(2,1)S(1)}, bf16[8,4096]{1,0:T(8,128)(2,1)S(1)}, u32[]{:S(2)}, u32[]{:S(2)}) collective-permute-start(bf16[8,4096]{1,0:T(8,128)(2,1)S(1)} %slice.87), channel_id=1, source_target_pairs={{0,1},{1,2},{2,3},{3,4},{4,5},{5,6},{6,7},{7,8},{8,9},{9,10},{10,1... | collective-permute-start | bytes 196616 | tf_op jit(solution)/shard_map/ppermute | solution.py:233
  13.5 1.2 copy-start.3
  28.4 1.4 copy-start.2
  28.4 2.0 copy-start.4
  30.5 5.0 %collective-permute-start.1 = (f32[8,128,256]{2,1,0:T(8,128)S(1)}, f32[8,128,256]{2,1,0:T(8,128)}, u32[]{:S(2)}, u32[]{:S(2)}) collective-permute-start(f32[8,128,256]{2,1,0:T(8,128)S(1)} %slice_select_fusion), channel_id=1, source_target_pairs={{0,1},{1,0},{2,3},{3,2},{4,5},{5,4},{6,7},{7,6},{8,9},{9,8},{10,11... | collective-permute-start | bytes 3145736 | tf_op jit(solution)/shard_map/ppermute | solution.py:189
  37.6 2.0 copy-start.8
  39.6 26.1 %collective-permute-start.2 = (f32[4,128,256]{2,1,0:T(8,128)}, f32[4,128,256]{2,1,0:T(8,128)}, u32[]{:S(2)}, u32[]{:S(2)}) collective-permute-start(f32[4,128,256]{2,1,0:T(8,128)} %broadcast_select_fusion.4), channel_id=1, source_target_pairs={{0,2},{1,3},{2,0},{3,1},{4,6},{5,7},{6,4},{7,5},{8,10},{9,11},{10,... | collective-permute-start | bytes 1572872 | tf_op jit(solution)/shard_map/ppermute | solution.py:189
  67.5 42.0 %copy-start.9 = (f32[8,128,256]{2,1,0:T(8,128)S(1)}, f32[8,128,256]{2,1,0:T(8,128)}, u32[]{:S(2)}) copy-start(f32[8,128,256]{2,1,0:T(8,128)} %copy-done.8) | copy-start | bytes 3145732
  67.6 7.8 %collective-permute-start.3 = (f32[2,128,256]{2,1,0:T(8,128)S(1)}, f32[2,128,256]{2,1,0:T(8,128)S(1)}, u32[]{:S(2)}, u32[]{:S(2)}) collective-permute-start(f32[2,128,256]{2,1,0:T(8,128)S(1)} %broadcast_select_fusion.10), channel_id=1, source_target_pairs={{0,4},{1,5},{2,6},{3,7},{4,0},{5,1},{6,2},{7,3},{8,12},{9,13},{10,... | collective-permute-start | bytes 786440 | tf_op jit(solution)/shard_map/ppermute | solution.py:189
  75.8 35.4 %copy-start.14 = (s32[128,10]{0,1:T(8,128)S(1)}, s32[128,10]{0,1:T(8,128)}, u32[]{:S(2)}) copy-start(s32[128,10]{0,1:T(8,128)} %param.28) | copy-start | bytes 15364
  75.8 7.3 %collective-permute-start.4 = (f32[2,128,128]{2,1,0:T(8,128)S(1)}, f32[2,128,128]{2,1,0:T(8,128)S(1)}, u32[]{:S(2)}, u32[]{:S(2)}) collective-permute-start(f32[2,128,128]{2,1,0:T(8,128)S(1)} %slice_add_fusion.4), channel_id=1, source_target_pairs={{0,8},{1,9},{2,10},{3,11},{4,12},{5,13},{6,14},{7,15},{8,16},{9,17... | collective-permute-start | bytes 393224 | tf_op jit(solution)/shard_map/ppermute | solution.py:200
  83.4 6.9 %collective-permute-start.5 = (f32[2,128,128]{2,1,0:T(8,128)S(1)}, f32[2,128,128]{2,1,0:T(8,128)S(1)}, u32[]{:S(2)}, u32[]{:S(2)}) collective-permute-start(f32[2,128,128]{2,1,0:T(8,128)S(1)} %convolution_add_fusion.5), channel_id=1, source_target_pairs={{0,8},{1,9},{2,10},{3,11},{4,12},{5,13},{6,14},{7,15},{8,16},{9,17... | collective-permute-start | bytes 393224 | tf_op jit(solution)/shard_map/ppermute | solution.py:200
  90.5 6.9 %collective-permute-start.6 = (f32[2,128,128]{2,1,0:T(8,128)S(1)}, f32[2,128,128]{2,1,0:T(8,128)S(1)}, u32[]{:S(2)}, u32[]{:S(2)}) collective-permute-start(f32[2,128,128]{2,1,0:T(8,128)S(1)} %convolution_add_fusion.4), channel_id=1, source_target_pairs={{0,8},{1,9},{2,10},{3,11},{4,12},{5,13},{6,14},{7,15},{8,16},{9,17... | collective-permute-start | bytes 393224 | tf_op jit(solution)/shard_map/ppermute | solution.py:200
  97.7 5.0 %collective-permute-start.7 = (f32[2,128,128]{2,1,0:T(8,128)S(1)}, f32[2,128,128]{2,1,0:T(8,128)S(1)}, u32[]{:S(2)}, u32[]{:S(2)}) collective-permute-start(f32[2,128,128]{2,1,0:T(8,128)S(1)} %get-tuple-element.23), channel_id=1, source_target_pairs={{0,4},{1,5},{2,6},{3,7},{4,0},{5,1},{6,2},{7,3},{8,12},{9,13},{10,... | collective-permute-start | bytes 393224 | tf_op jit(solution)/shard_map/ppermute | solution.py:204
  103.1 6.4 %collective-permute-start.8 = (f32[4,128,128]{2,1,0:T(8,128)S(1)}, f32[4,128,128]{2,1,0:T(8,128)S(1)}, u32[]{:S(2)}, u32[]{:S(2)}) collective-permute-start(f32[4,128,128]{2,1,0:T(8,128)S(1)} %get-tuple-element.19), channel_id=1, source_target_pairs={{0,2},{1,3},{2,0},{3,1},{4,6},{5,7},{6,4},{7,5},{8,10},{9,11},{10,... | collective-permute-start | bytes 786440 | tf_op jit(solution)/shard_map/ppermute | solution.py:204
  111.1 2.1 collective-permute-start.9
  113.2 0.8 copy-start.11
  114.0 6.7 %copy-start.10 = (bf16[128,2048]{1,0:T(8,128)(2,1)S(1)}, bf16[128,2048]{1,0:T(8,128)(2,1)}, u32[]{:S(2)}) copy-start(bf16[128,2048]{1,0:T(8,128)(2,1)} %param.18) | copy-start | bytes 1572868
  120.7 6.0 %copy-start.13 = (f32[2048]{0:T(1024)S(1)}, f32[2048]{0:T(1024)}, u32[]{:S(2)}) copy-start(f32[2048]{0:T(1024)} %param.26) | copy-start | bytes 24580
  125.7 1.0 copy-start.6
  272.9 2.6 copy-start.7
  301.7 4.1 copy-start.15
  301.7 4.1 copy-start.12
  301.7 143.9 %all-to-all-start.1 = ((bf16[32,2,24,2048]{3,2,1,0:T(8,128)(2,1)}), bf16[32,2,24,2048]{3,2,1,0:T(8,128)(2,1)}, u32[]{:S(2)}, u32[]{:S(2)}) async-start(bf16[32,2,24,2048]{3,2,1,0:T(8,128)(2,1)} %bitcast.78), calls=%async_computation.1 | async-start | bytes 12582912 | tf_op jit(solution)/shard_map/all_to_all | solution.py:273
Sparse Core Ops, SparseCore 0:
  8.9 72.2 all-gather.1

commit v2 on v1

--- a/solution.py
+++ b/solution.py
@@ -186,7 +186,8 @@
         upper = (place // step) % 2 == 1
         keep = jnp.where(upper, held[share:], held[:share])
         give = jnp.where(upper, held[:share], held[share:])
-        got = lax.ppermute(give, AXES, [(i, i ^ step) for i in range(count)])
+        kind = F32 if step == 1 else BF16
+        got = lax.ppermute(give.astype(kind), AXES, [(i, i ^ step) for i in range(count)]).astype(F32)
         early, late = jnp.where(upper, got, keep), jnp.where(upper, keep, got)
         merged = apply(late[:, :, :head], early)
         held = jnp.concatenate([merged[:, :, :head], merged[:, :, head:] + late[:, :, head:]], axis=2)
@@ -197,16 +198,219 @@
         ahead = held[:, :, head:]
         if turn:
             ahead = ahead + apply(held[:, :, :head], state)
-        state = lax.ppermute(ahead, AXES, [(i, i + step) for i in range(count - step)])
+        state = lax.ppermute(ahead.astype(BF16), AXES, [(i, i + step) for i in range(count - step)]).astype(F32)
     for step, upper, early in reversed(levels):
         second = apply(early[:, :, :head], state) + early[:, :, head:]
         mine, other = jnp.where(upper, second, state), jnp.where(upper, state, second)
-        got = lax.ppermute(other, AXES, [(i, i ^ step) for i in range(count)])
+        got = lax.ppermute(other.astype(BF16), AXES, [(i, i ^ step) for i in range(count)]).astype(F32)
         state = jnp.where(upper, jnp.concatenate([got, mine], axis=0), jnp.concatenate([mine, got], axis=0))
     return state
 
 
+def places(mesh):
+    at = {(*d.coords, d.core_on_chip): i for i, d in enumerate(mesh.devices.flat)}
+    return at, tuple(max(c[k] for c in at) + 1 for k in range(4))
+
+
+def moves(layout, x=0, y=0, z=0, core=0):
+    at, size = layout
+    shift = (x, y, z, core)
+    return [(i, at[tuple((c + s) % n for c, s, n in zip(spot, shift, size))]) for spot, i in at.items()]
+
+
+def expert_kernel(*refs, width, capacity, local_count):
+    shards, (chosen_ref, *weights), outs = refs[:8], refs[8:15], refs[15:23]
+    sel_ref, pick_ref, gate_ref, back_ref = refs[23:]
+    step = pl.program_id(0)
+    steps = 2 * local_count
+    rows = shards[0].shape[0]
+    pair_rows, slots = 2 * rows, 2 * capacity
+    tile = width // 4
+    pairs = [(shards[i], shards[i + 1]) for i in range(0, 8, 2)]
+
+    def read(pair, lo, hi):
+        return jnp.concatenate([r[:, lo:hi] for r in pair], axis=0)
+
+    @pl.when(step == 0)
+    def _():
+        before = lax.broadcasted_iota(jnp.int32, (pair_rows, pair_rows), 0)
+        after = lax.broadcasted_iota(jnp.int32, (pair_rows, pair_rows), 1)
+        earlier = jnp.where((before < after) & (before // rows == after // rows), 1.0, 0.0).astype(BF16)
+        second = lax.broadcasted_iota(jnp.int32, (1, pair_rows), 1) // rows
+        slot = lax.broadcasted_iota(jnp.int32, (slots, pair_rows), 0)
+        for p, pair in enumerate(pairs):
+            gates = dot(chosen_ref[...], read(pair, width, pair[0].shape[1]), ((1,), (1,)))
+            named = jnp.where(gates != 0.0, 1.0, 0.0)
+            rank = dot(named.astype(BF16), earlier).astype(jnp.int32)
+            spot = jnp.where(gates != 0.0, rank + second * capacity, -1)
+            for e in range(steps):
+                hit = slot == spot[e : e + 1]
+                pick_ref[p, e * slots : (e + 1) * slots, :] = jnp.where(hit, 1.0, 0.0).astype(BF16)
+                gate = jnp.sum(jnp.where(hit, gates[e : e + 1], 0.0), axis=1, keepdims=True)
+                gate_ref[e, p * slots : (p + 1) * slots, :] = jnp.broadcast_to(gate, (slots, 128))
+            for n in range(4):
+                taken = dot(pick_ref[p], read(pair, n * tile, (n + 1) * tile)).astype(BF16)
+                for e in range(steps):
+                    sel_ref[e, p * slots : (p + 1) * slots, n * tile : (n + 1) * tile] = taken[e * slots : (e + 1) * slots]
+
+    def run(g_ref, u_ref, d_ref):
+        rows_in = sel_ref[step]
+        gate, up = dot(rows_in, g_ref[0]), dot(rows_in, u_ref[0])
+        hidden = (gate / (1.0 + jnp.exp(-gate)) * up).astype(BF16)
+        weight = gate_ref[step][:, 0:1]
+        at = pl.multiple_of(step * slots, slots)
+        for n in range(4):
+            result = (dot(hidden, d_ref[0, :, n * tile : (n + 1) * tile]) * weight).astype(BF16)
+            for p in range(len(pairs)):
+                back_ref[p, pl.ds(at, slots), n * tile : (n + 1) * tile] = result[p * slots : (p + 1) * slots]
+
+    @pl.when(step < local_count)
+    def _():
+        run(*weights[:3])
+
+    @pl.when(step >= local_count)
+    def _():
+        run(*weights[3:])
+
+    @pl.when(step == steps - 1)
+    def _():
+        for p in range(len(pairs)):
+            spread = pick_ref[p].astype(F32).T.astype(BF16)
+            for n in range(4):
+                cut = slice(n * tile, (n + 1) * tile)
+                total = dot(spread, back_ref[p, :, cut]).astype(BF16)
+                outs[2 * p][:, cut] = total[:rows]
+                outs[2 * p + 1][:, cut] = total[rows:]
+
+
+def run_experts(shards, chosen, mine, other, width, capacity):
+    local_count, _, hidden = mine[0].shape
+    steps = 2 * local_count
+    slots = 2 * capacity
+    rows = shards[0].shape[0]
+    whole = lambda a: pl.BlockSpec(a.shape, lambda s: (0,) * a.ndim)
+    first = lambda a: pl.BlockSpec((1, *a.shape[1:]), lambda s: (jnp.minimum(s, local_count - 1), 0, 0))
+    then = lambda a: pl.BlockSpec((1, *a.shape[1:]), lambda s: (jnp.maximum(s - local_count, 0), 0, 0))
+    shapes = [jax.ShapeDtypeStruct((rows, width), BF16)] * 8
+    return pl.pallas_call(
+        functools.partial(expert_kernel, width=width, capacity=capacity, local_count=local_count),
+        grid=(steps,),
+        in_specs=[whole(a) for a in (*shards, chosen)] + [first(a) for a in mine] + [then(a) for a in other],
+        out_specs=[whole(a) for a in shapes],
+        out_shape=shapes,
+        scratch_shapes=[
+            pltpu.VMEM((steps, 4 * slots, width), BF16),
+            pltpu.VMEM((4, steps * slots, 2 * rows), BF16),
+            pltpu.VMEM((steps, 4 * slots, 128), F32),
+            pltpu.VMEM((4, steps * slots, width), BF16),
+        ],
+        cost_estimate=pl.CostEstimate(
+            flops=steps * 4 * slots * (6 * width * hidden + 8 * width * rows),
+            bytes_accessed=6 * width * hidden * steps + 32 * rows * width,
+            transcendentals=0,
+        ),
+        compiler_params=pltpu.CompilerParams(vmem_limit_bytes=58 * 2**20),
+        name="experts",
+    )(*shards, chosen, *mine, *other)
+
+
+def tie(value, *after):
+    return lax.optimization_barrier((value, *after))[0]
+
+
+def plus(*parts):
+    return sum(p.astype(F32) for p in parts[1:]) + parts[0].astype(F32)
+
+
+def routed_by_gather(layout, place, routed_in, gates, weights, other, capacity):
+    rows, width = routed_in.shape
+    experts = gates.shape[1]
+    local_count = weights[0].shape[0]
+    deep = layout[1][2]
+    send = lambda a, **by: lax.ppermute(a, AXES, moves(layout, **by))
+    partner = jnp.asarray([j for _, j in sorted(moves(layout, core=1))], jnp.int32)[place]
+    ids = jnp.concatenate([p * local_count + jnp.arange(local_count, dtype=jnp.int32) for p in (place, partner)])
+    ids = jnp.pad(ids, (0, -ids.shape[0] % 8), constant_values=experts)
+    chosen = (ids[:, None] == jnp.arange(experts, dtype=jnp.int32)).astype(BF16)
+    pad = -(2 * experts) % 128
+    chosen = jnp.pad(jnp.concatenate([chosen, chosen], axis=1), ((0, 0), (0, pad)))
+    gates_hi, gates_lo = halves(gates)
+    packet = jnp.concatenate([routed_in, gates_hi, gates_lo, jnp.zeros((rows, pad), BF16)], axis=1)
+
+    turns = [0, 1]
+    for i in range(2, deep // 2 + 1):
+        turns += [deep + 1 - i, i]
+    turns = turns[:deep]
+    across = [("x", "y"), ("y", "x")]
+    arrived = {0: packet}
+    hops = {}
+    ready = packet
+    for at, turn in enumerate(turns):
+        if turn:
+            arrived[turn] = send(ready, z=-turn)
+            if at == 2:
+                ready = tie(packet, arrived[turns[1]])
+    sums = {}
+    gone = ()
+    for at in range(0, deep, 2):
+        pair = turns[at : at + 2]
+        for turn in pair:
+            hops[turn] = {"x": send(arrived[turn], x=1), "y": send(arrived[turn], y=1)}
+        far = [
+            send(tie(hops[turn][first], *gone) if gone else hops[turn][first], **{second: 1})
+            for turn, (first, second) in zip(pair, across)
+        ]
+        shards = [arrived[t] for t in pair] + [hops[t]["x"] for t in pair] + [hops[t]["y"] for t in pair] + far
+        done = run_experts(shards, chosen, weights, other, width, capacity)
+        gone = (done[0],)
+        for i, turn in enumerate(pair):
+            sums[turn] = (done[i], {"x": done[2 + i], "y": done[4 + i]}, done[6 + i], across[i])
+    total = []
+    late = ()
+    for turn in turns[1:] + [0]:
+        own, to, far, (first, second) = sums[turn]
+        if turn == 0 and late:
+            far = tie(far, *late)
+        back = send(far, **{second: 1})
+        late = (back,)
+        to[first] = plus(to[first], back).astype(BF16)
+        got = [send(to[second], **{second: 1}), send(to[first], **{first: 1})]
+        part = plus(own, *got)
+        total.append(send(part.astype(BF16), z=turn).astype(F32) if turn else part)
+    return plus(*total)
+
+
+def routed_by_exchange(routed_in, gates, named, weights, capacity):
+    rows, width = routed_in.shape
+    expert_gate, expert_up, expert_down = weights
+    local_count, experts = expert_gate.shape[0], gates.shape[1]
+    count = experts // local_count
+    earlier = jnp.dot(jnp.tril(jnp.ones((rows, rows), BF16), -1), named.astype(BF16), preferred_element_type=F32)
+    slot = jnp.where(named, earlier.astype(jnp.int32), capacity)
+    picks = (slot.T[:, None, :] == jnp.arange(capacity, dtype=jnp.int32)[None, :, None]).reshape(experts * capacity, rows)
+    outgoing = jnp.dot(picks.astype(BF16), routed_in, preferred_element_type=F32).astype(BF16)
+    received = lax.all_to_all(
+        outgoing.reshape(count, local_count, capacity, width), AXES, split_axis=0, concat_axis=0, tiled=True
+    )
+    received = received.transpose(1, 0, 2, 3).reshape(local_count, count * capacity, width)
+    gate_part = jnp.einsum("esd,edf->esf", received, expert_gate, preferred_element_type=F32)
+    up_part = jnp.einsum("esd,edf->esf", received, expert_up, preferred_element_type=F32)
+    hidden = (jax.nn.silu(gate_part) * up_part).astype(BF16)
+    result = jnp.einsum("esf,efd->esd", hidden, expert_down, preferred_element_type=F32).astype(BF16)
+    result = result.reshape(local_count, count, capacity, width).transpose(1, 0, 2, 3)
+    returned = lax.all_to_all(result, AXES, split_axis=0, concat_axis=0, tiled=True)
+    spread = jnp.where(slot[:, :, None] == jnp.arange(capacity, dtype=jnp.int32), gates[:, :, None], 0.0)
+    spread_hi, spread_lo = halves(spread.reshape(rows, experts * capacity))
+    pulled = jnp.dot(
+        jnp.concatenate([spread_hi, spread_lo], axis=0),
+        returned.reshape(experts * capacity, width),
+        preferred_element_type=F32,
+    )
+    return pulled[:rows] + pulled[rows:]
+
+
 def local(
+    layout,
     residual,
     mixed_qkv,
     output_gate,
@@ -231,60 +435,58 @@
     count = lax.axis_size(AXES)
     place = lax.axis_index(AXES)
     before = lax.ppermute(mixed_qkv[rows - 8 :], AXES, [(i, i + 1) for i in range(count - 1)])
+    weights = (expert_gate, expert_up, expert_down)
+    x, y, z, cores = layout[1]
+    paired = (x, y, cores) == (2, 2, 2) and z % 2 == 0
+    across_y, across_core = moves(layout, y=1), moves(layout, core=1)
+    columns = lax.axis_size("exp")
+    near = columns == 4 and all(i // columns == j // columns for i, j in across_y + across_core)
+    if near:
+        out_parts = [out_weight, lax.ppermute(out_weight, AXES, across_y)]
+        out_parts += [lax.ppermute(w, AXES, across_core) for w in out_parts]
+        twin, facing = (jnp.asarray([j for _, j in sorted(pairs)], jnp.int32) for pairs in (across_core, across_y))
+        owners = [p % columns for p in (place, facing[place], twin[place], facing[twin[place]])]
+    if paired:
+        other = [lax.ppermute(w, AXES, across_core) for w in weights]
     block_map, read = delta_terms(mixed_qkv, before, conv_weight, log_decay, write_strength, head)
     state = starting_states(block_map, count, place)
     normed = emit(read, state, output_gate, norm_gain)
-    projected = jnp.dot(normed, lax.all_gather(out_weight, "exp", axis=1, tiled=True), preferred_element_type=F32)
+    if near:
+        products = [jnp.dot(normed, w, preferred_element_type=F32) for w in out_parts]
+        projected = jnp.concatenate(
+            [sum(jnp.where(o == e, p, 0.0) for o, p in zip(owners, products)) for e in range(columns)], axis=1
+        )
+    else:
+        projected = jnp.dot(normed, lax.all_gather(out_weight, "exp", axis=1, tiled=True), preferred_element_type=F32)
     after_mix = (residual.astype(F32) + projected).astype(BF16)
     after_wide = after_mix.astype(F32)
     routed_in = (
         after_wide * lax.rsqrt(jnp.mean(after_wide * after_wide, axis=-1, keepdims=True) + EPS) * post_gain
     ).astype(BF16)
 
-    local_count = expert_gate.shape[0]
-    experts = local_count * count
-    top = expert_ids.shape[1]
-    capacity = rows * top * 6 // (experts * 5)
+    experts = expert_gate.shape[0] * count
+    capacity = rows * expert_ids.shape[1] * 6 // (experts * 5)
     named = jnp.any(expert_ids[:, :, None] == jnp.arange(experts, dtype=jnp.int32), axis=1)
-    earlier = jnp.dot(jnp.tril(jnp.ones((rows, rows), BF16), -1), named.astype(BF16), preferred_element_type=F32)
-    slot = jnp.where(named, earlier.astype(jnp.int32), capacity)
-    picks = (slot.T[:, None, :] == jnp.arange(capacity, dtype=jnp.int32)[None, :, None]).reshape(experts * capacity, rows)
-
     logits = jnp.dot(routed_in, router_weight, preferred_element_type=F32)
     chosen = jnp.where(named, jnp.exp(jnp.where(named, logits, 0.0)), 0.0)
     gates = chosen / jnp.sum(chosen, axis=1, keepdims=True)
-    outgoing = jnp.dot(picks.astype(BF16), routed_in, preferred_element_type=F32).astype(BF16)
-    received = lax.all_to_all(
-        outgoing.reshape(count, local_count, capacity, width), AXES, split_axis=0, concat_axis=0, tiled=True
-    )
+    if paired:
+        routed = routed_by_gather(layout, place, routed_in, gates, weights, other, capacity)
+    else:
+        routed = routed_by_exchange(routed_in, gates, named, weights, capacity)
     shared_hidden = (
         jax.nn.silu(jnp.dot(routed_in, shared_gate, preferred_element_type=F32))
         * jnp.dot(routed_in, shared_up, preferred_element_type=F32)
     ).astype(BF16)
     switch = jax.nn.sigmoid(jnp.dot(routed_in, shared_switch, preferred_element_type=F32))
     shared_out = switch[:, None] * jnp.dot(shared_hidden, shared_down, preferred_element_type=F32)
-
-    received = received.transpose(1, 0, 2, 3).reshape(local_count, count * capacity, width)
-    gate_part = jnp.einsum("esd,edf->esf", received, expert_gate, preferred_element_type=F32)
-    up_part = jnp.einsum("esd,edf->esf", received, expert_up, preferred_element_type=F32)
-    hidden = (jax.nn.silu(gate_part) * up_part).astype(BF16)
-    result = jnp.einsum("esf,efd->esd", hidden, expert_down, preferred_element_type=F32).astype(BF16)
-    result = result.reshape(local_count, count, capacity, width).transpose(1, 0, 2, 3)
-    returned = lax.all_to_all(result, AXES, split_axis=0, concat_axis=0, tiled=True)
-    spread = jnp.where(slot[:, :, None] == jnp.arange(capacity, dtype=jnp.int32), gates[:, :, None], 0.0)
-    spread_hi, spread_lo = halves(spread.reshape(rows, experts * capacity))
-    pulled = jnp.dot(
-        jnp.concatenate([spread_hi, spread_lo], axis=0),
-        returned.reshape(experts * capacity, width),
-        preferred_element_type=F32,
-    )
-    return (after_wide + pulled[:rows] + pulled[rows:] + shared_out).astype(BF16)
+    return (after_wide + routed + shared_out).astype(BF16)
 
 
 def solution(mesh):
     rows = P(AXES, None)
     return jax.shard_map(
-        local,
+        functools.partial(local, places(mesh)),
         mesh=mesh,
         in_specs=(rows, rows, rows, rows, rows, P(), P(), P(None, "exp"), P(), P(), rows)
         + (P(AXES, None, None),) * 3

time: 463 us -> 363 us (0.78); the launches traced: 463 us -> 357 us
  blocking collectives: 143 us -> 0 us
  Pallas kernels: 18 us -> 57 us
  starting transfers between devices: 26.7 us -> 58.8 us
  matrix products: 45.8 us -> 17.7 us
  other arithmetic: 8.7 us -> 18 us
  local copies, waits for them, and re-layouts: 17.5 us -> 10.6 us
  between operations: 13.8 us -> 8.11 us
    all_to_all x1 -> x0, blocking collectives: 143 us -> none  [local(): lax.all_to_all(outgoing.reshape(count, local_count, capacity, width), AXE...]
    all_to_all x1 -> x0, waiting for transfers between devices: 136 us -> none  [local(): lax.all_to_all(result, AXES, split_axis=0, concat_axis=0, tiled=True)]
    ppermute x9 -> x45, waiting for transfers between devices: 52.6 us -> 187 us  [the longest x30 139 us: routed_by_gather(): send = lambda a, **by: lax.ppermute(a, AXES, moves(layout, **by))]
    pallas_call x0 -> x2, Pallas kernels: none -> 38.9 us  [run_experts(): pl.pallas_call(functools.partial(expert_kernel, width=width, capacity=cap...]
    ppermute x9 -> x45, starting transfers between devices: 20.2 us -> 56.5 us  [the longest x30 32.8 us: routed_by_gather(): send = lambda a, **by: lax.ppermute(a, AXES, moves(layout, **by))]
    dot_general x6 -> x4, matrix products: 32.5 us -> 8.51 us  [local(): jnp.dot(normed, w, preferred_element_type=F32)]
    convert_element_type x1 -> x17, other arithmetic: 0.27 us -> 12 us  [the longest x3 4.32 us: routed_by_gather(): total.append(send(part.astype(BF16), z=turn).astype(F32) if turn else part)]
    reshape x1 -> x0, local copies, waits for them, and re-layouts: 6.54 us -> none  [local(): result.reshape(local_count, count, capacity, width).transpose(1, 0, 2, 3)]
  transfers between devices with their start and end apart: 12 -> 46, of which waited for: 10 -> 27; matrix products, arithmetic and copies ran while one was open for 4% -> 8% of each run, Pallas kernels for 4% -> 12%
where the time goes in v2:
time: 363 us; the launch traced here: 357 us
  waiting for transfers between devices  187 us (52%)
  starting transfers between devices  58.8 us (16%)
  Pallas kernels  57 us (16%)
  other arithmetic  18 us (5%)
  matrix products  17.7 us (5%)
  local copies, waits for them, and re-layouts  10.6 us (3%)
  between operations  8.11 us (2%)
    ppermute x30, waiting for transfers between devices, routed_by_gather(): send = lambda a, **by: lax.ppermute(a, AXES, moves(layout, **by))  139 us
    pallas_call x2, Pallas kernels, run_experts(): pl.pallas_call(functools.partial(expert_kernel, width=width, capacity=cap...  38.9 us
    ppermute x30, starting transfers between devices, routed_by_gather(): send = lambda a, **by: lax.ppermute(a, AXES, moves(layout, **by))  32.8 us
    ppermute x1, waiting for transfers between devices, local(): out_parts = [out_weight, lax.ppermute(out_weight, AXES, across_y)]  18.8 us
    pallas_call x1, Pallas kernels, delta_terms(): pl.pallas_call(functools.partial(delta_kernel, head=head, per=per), grid=...  13.7 us
    ppermute x3, starting transfers between devices, starting_states(): lax.ppermute(ahead.astype(BF16), AXES, [(i, i + step) for i in range(coun...  13.6 us
    ppermute x3, waiting for transfers between devices, starting_states(): lax.ppermute(other.astype(BF16), AXES, [(i, i ^ step) for i in range(coun...  12.2 us
    ppermute x3, waiting for transfers between devices, starting_states(): lax.ppermute(give.astype(kind), AXES, [(i, i ^ step) for i in range(count)])  11.6 us
  transfers between devices with their start and end apart: 46, of which 27 were waited for; matrix products, arithmetic and copies ran while one was open for 8% of the time, Pallas kernels for 12%

profile of v2, /device:TPU:0, one launch (start us, length us, event | category | flops | bytes accessed | tf_op | source)
XLA Modules:
  0.0 357.3 jit_solution(10740394511268522718)
XLA Ops:
  1.0 2.3 collective-permute-start
  7.5 13.7 %delta_terms.1 = (f32[16,128,256]{2,1,0:T(8,128)S(1)}, f32[16,128,256]{2,1,0:T(8,128)S(1)}) custom-call(bf16[128,4096]{1,0:T(8,128)(2,1)S(1)} %copy-done.1, bf16[128,4096]{1,0:T(8,128)(2,1)S(1)} %copy-done.1, bf16[128,4096]{1,0:T(8,128)(2,1)S(1)} %copy-done.1, bf16[8,4096]{1,0:T(8,128)(2,1)S(1)} %collective-permute-done.qb_ref.kb_ref.vb_ref, ...), custom_call_target="tpu_custom_call" | custom-call | tf_op jit(solution)/shard_map/delta_terms/pallas_call | solution.py:132
  23.2 2.6 collective-permute-start.1
  25.8 2.4 collective-permute-done.1
  28.2 2.1 broadcast_select_fusion.1
  32.2 1.9 collective-permute-start.2
  34.1 6.9 %collective-permute-done.2 = bf16[4,128,256]{2,1,0:T(8,128)(2,1)S(1)} collective-permute-done((bf16[4,128,256]{2,1,0:T(8,128)(2,1)}, bf16[4,128,256]{2,1,0:T(8,128)(2,1)S(1)}, u32[]{:S(2)}, u32[]{:S(2)}) %collective-permute-start.2) | collective-permute-done | bytes 262176 | tf_op jit(solution)/shard_map/ppermute | solution.py:190
  41.8 2.6 collective-permute-start.3
  45.1 2.3 collective-permute-done.3
  47.9 5.0 %collective-permute-start.4 = (bf16[2,128,128]{2,1,0:T(8,128)(2,1)S(1)}, bf16[2,128,128]{2,1,0:T(8,128)(2,1)S(1)}, u32[]{:S(2)}, u32[]{:S(2)}) collective-permute-start(bf16[2,128,128]{2,1,0:T(8,128)(2,1)S(1)} %fusion.46), channel_id=1, source_target_pairs={{0,8},{1,9},{2,10},{3,11},{4,12},{5,13},{6,14},{7,15},{8,16},{9,17... | collective-permute-start | bytes 196616 | tf_op jit(solution)/shard_map/ppermute | solution.py:201
  52.9 1.9 collective-permute-done.4
  55.0 4.3 %collective-permute-start.5 = (bf16[2,128,128]{2,1,0:T(8,128)(2,1)S(1)}, bf16[2,128,128]{2,1,0:T(8,128)(2,1)S(1)}, u32[]{:S(2)}, u32[]{:S(2)}) collective-permute-start(bf16[2,128,128]{2,1,0:T(8,128)(2,1)S(1)} %fusion.1), channel_id=1, source_target_pairs={{0,8},{1,9},{2,10},{3,11},{4,12},{5,13},{6,14},{7,15},{8,16},{9,17... | collective-permute-start | bytes 196616 | tf_op jit(solution)/shard_map/ppermute | solution.py:201
  59.3 1.9 collective-permute-done.5
  61.4 4.3 %collective-permute-start.6 = (bf16[2,128,128]{2,1,0:T(8,128)(2,1)S(1)}, bf16[2,128,128]{2,1,0:T(8,128)(2,1)S(1)}, u32[]{:S(2)}, u32[]{:S(2)}) collective-permute-start(bf16[2,128,128]{2,1,0:T(8,128)(2,1)S(1)} %fusion.2), channel_id=1, source_target_pairs={{0,8},{1,9},{2,10},{3,11},{4,12},{5,13},{6,14},{7,15},{8,16},{9,17... | collective-permute-start | bytes 196616 | tf_op jit(solution)/shard_map/ppermute | solution.py:201
  65.6 1.9 collective-permute-done.6
  68.4 3.7 %collective-permute-done.7 = bf16[2,128,128]{2,1,0:T(8,128)(2,1)S(1)} collective-permute-done((bf16[2,128,128]{2,1,0:T(8,128)(2,1)S(1)}, bf16[2,128,128]{2,1,0:T(8,128)(2,1)S(1)}, u32[]{:S(2)}, u32[]{:S(2)}) %collective-permute-start.7) | collective-permute-done | bytes 65568 | tf_op jit(solution)/shard_map/ppermute | solution.py:205
  72.5 18.8 %collective-permute-done.10 = bf16[2048,512]{1,0:T(8,128)(2,1)} collective-permute-done((bf16[2048,512]{1,0:T(8,128)(2,1)}, bf16[2048,512]{1,0:T(8,128)(2,1)}, u32[]{:S(2)}, u32[]{:S(2)}) %collective-permute-start.10) | collective-permute-done | bytes 2097184 | tf_op jit(solution)/shard_map/ppermute | solution.py:445
  92.3 5.0 %collective-permute-done.8 = bf16[4,128,128]{2,1,0:T(8,128)(2,1)S(1)} collective-permute-done((bf16[4,128,128]{2,1,0:T(8,128)(2,1)S(1)}, bf16[4,128,128]{2,1,0:T(8,128)(2,1)S(1)}, u32[]{:S(2)}, u32[]{:S(2)}) %collective-permute-start.8) | collective-permute-done | bytes 131104 | tf_op jit(solution)/shard_map/ppermute | solution.py:205
  98.8 3.4 collective-permute-done.9
  111.8 4.3 %emit.1 = bf16[128,2048]{1,0:T(8,128)(2,1)} custom-call(f32[16,128,256]{2,1,0:T(8,128)} %copy-done.3, f32[16,128,128]{2,1,0:T(8,128)} %maximum_select_fusion.state_ref, bf16[128,2048]{1,0:T(8,128)(2,1)} %gate_ref.1, f32[1,128]{1,0:T(1,128)} %bitcast.50), custom_call_target="tpu_custom_call" | custom-call | tf_op jit(solution)/shard_map/emit/pallas_call | solution.py:161
  116.1 2.3 fusion.52
  118.4 2.0 fusion.53
  120.4 2.0 fusion.54
  122.5 2.2 select_add_fusion.3
  127.1 3.6 %collective-permute-start.14 = (bf16[128,2176]{1,0:T(8,128)(2,1)}, bf16[128,2176]{1,0:T(8,128)(2,1)}, u32[]{:S(2)}, u32[]{:S(2)}) collective-permute-start(bf16[128,2176]{1,0:T(8,128)(2,1)} %concatenate.47.refs_0_), channel_id=1, source_target_pairs={{0,24},{1,25},{2,26},{3,27},{4,28},{5,29},{6,30},{7,31},{8,0},{9,1... | collective-permute-start | bytes 1671176 | tf_op jit(solution)/shard_map/ppermute | solution.py:330
  132.8 10.7 %collective-permute-done.14.refs_1_ = bf16[128,2176]{1,0:T(8,128)(2,1)} collective-permute-done((bf16[128,2176]{1,0:T(8,128)(2,1)}, bf16[128,2176]{1,0:T(8,128)(2,1)}, u32[]{:S(2)}, u32[]{:S(2)}) %collective-permute-start.14) | collective-permute-done | bytes 557088 | tf_op jit(solution)/shard_map/ppermute | solution.py:330
  145.2 4.4 %collective-permute-start.15 = (bf16[128,2176]{1,0:T(8,128)(2,1)}, bf16[128,2176]{1,0:T(8,128)(2,1)}, u32[]{:S(2)}, u32[]{:S(2)}) collective-permute-start(bf16[128,2176]{1,0:T(8,128)(2,1)} %concatenate.47.refs_0_), channel_id=1, source_target_pairs={{0,16},{1,17},{2,18},{3,19},{4,20},{5,21},{6,22},{7,23},{8,24},{9,... | collective-permute-start | bytes 1671176 | tf_op jit(solution)/shard_map/ppermute | solution.py:330
  152.5 7.1 %collective-permute-done.23.refs_5_ = bf16[128,2176]{1,0:T(8,128)(2,1)} collective-permute-done((bf16[128,2176]{1,0:T(8,128)(2,1)}, bf16[128,2176]{1,0:T(8,128)(2,1)}, u32[]{:S(2)}, u32[]{:S(2)}) %collective-permute-start.23) | collective-permute-done | bytes 557088 | tf_op jit(solution)/shard_map/ppermute | solution.py:330
  164.3 21.0 %collective-permute-done.15.refs_1_ = bf16[128,2176]{1,0:T(8,128)(2,1)} collective-permute-done((bf16[128,2176]{1,0:T(8,128)(2,1)}, bf16[128,2176]{1,0:T(8,128)(2,1)}, u32[]{:S(2)}, u32[]{:S(2)}) %collective-permute-start.15) | collective-permute-done | bytes 557088 | tf_op jit(solution)/shard_map/ppermute | solution.py:330
  188.6 19.4 %experts.2 = (bf16[128,2048]{1,0:T(8,128)(2,1)}, bf16[128,2048]{1,0:T(8,128)(2,1)}, bf16[128,2048]{1,0:T(8,128)(2,1)}, bf16[128,2048]{1,0:T(8,128)(2,1)}, bf16[1...) custom-call(bf16[128,2176]{1,0:T(8,128)(2,1)} %concatenate.47.refs_0_, ...), custom_call_target="tpu_custom_call" | custom-call | flops 6442450944 | bytes 33554432 | tf_op jit(solution)/shard_map/experts/pallas_call | solution.py:295
  213.6 9.5 %collective-permute-done.43 = bf16[128,2048]{1,0:T(8,128)(2,1)S(1)} collective-permute-done((bf16[128,2048]{1,0:T(8,128)(2,1)}, bf16[128,2048]{1,0:T(8,128)(2,1)S(1)}, u32[]{:S(2)}, u32[]{:S(2)}) %collective-permute-start.43) | collective-permute-done | bytes 524320 | tf_op jit(solution)/shard_map/ppermute | solution.py:330
  224.6 2.0 add_convert_fusion.1
  228.0 7.2 %collective-permute-done.17.refs_3_ = bf16[128,2176]{1,0:T(8,128)(2,1)} collective-permute-done((bf16[128,2176]{1,0:T(8,128)(2,1)}, bf16[128,2176]{1,0:T(8,128)(2,1)}, u32[]{:S(2)}, u32[]{:S(2)}) %collective-permute-start.17) | collective-permute-done | bytes 557088 | tf_op jit(solution)/shard_map/ppermute | solution.py:330
  235.2 2.0 collective-permute-done.29.refs_6_
  237.1 10.0 %collective-permute-done.30.refs_7_ = bf16[128,2176]{1,0:T(8,128)(2,1)} collective-permute-done((bf16[128,2176]{1,0:T(8,128)(2,1)}, bf16[128,2176]{1,0:T(8,128)(2,1)}, u32[]{:S(2)}, u32[]{:S(2)}) %collective-permute-start.30) | collective-permute-done | bytes 557088 | tf_op jit(solution)/shard_map/ppermute | solution.py:330
  247.1 19.5 %experts.3 = (bf16[128,2048]{1,0:T(8,128)(2,1)}, bf16[128,2048]{1,0:T(8,128)(2,1)}, bf16[128,2048]{1,0:T(8,128)(2,1)}, bf16[128,2048]{1,0:T(8,128)(2,1)}, bf16[1...) custom-call(bf16[128,2176]{1,0:T(8,128)(2,1)} %copy-done.9, ...), custom_call_target="tpu_custom_call" | custom-call | flops 6442450944 | bytes 33554432 | tf_op jit(solution)/shard_map/experts/pallas_call | solution.py:295
  271.9 2.2 add_convert_fusion
  274.2 7.6 %collective-permute-done.36 = bf16[128,2048]{1,0:T(8,128)(2,1)S(1)} collective-permute-done((bf16[128,2048]{1,0:T(8,128)(2,1)}, bf16[128,2048]{1,0:T(8,128)(2,1)S(1)}, u32[]{:S(2)}, u32[]{:S(2)}) %collective-permute-start.36) | collective-permute-done | bytes 524320 | tf_op jit(solution)/shard_map/ppermute | solution.py:330
  282.5 12.5 %collective-permute-done.32 = bf16[128,2048]{1,0:T(8,128)(2,1)S(1)} collective-permute-done((bf16[128,2048]{1,0:T(8,128)(2,1)S(1)}, bf16[128,2048]{1,0:T(8,128)(2,1)S(1)}, u32[]{:S(2)}, u32[]{:S(2)}) %collective-permute-start.32) | collective-permute-done | bytes 524320 | tf_op jit(solution)/shard_map/ppermute | solution.py:330
  295.7 21.8 %collective-permute-done.40 = bf16[128,2048]{1,0:T(8,128)(2,1)S(1)} collective-permute-done((bf16[128,2048]{1,0:T(8,128)(2,1)S(1)}, bf16[128,2048]{1,0:T(8,128)(2,1)S(1)}, u32[]{:S(2)}, u32[]{:S(2)}) %collective-permute-start.40) | collective-permute-done | bytes 524320 | tf_op jit(solution)/shard_map/ppermute | solution.py:330
  319.0 5.9 %collective-permute-done.37 = bf16[128,2048]{1,0:T(8,128)(2,1)S(1)} collective-permute-done((bf16[128,2048]{1,0:T(8,128)(2,1)S(1)}, bf16[128,2048]{1,0:T(8,128)(2,1)S(1)}, u32[]{:S(2)}, u32[]{:S(2)}) %collective-permute-start.37) | collective-permute-done | bytes 524320 | tf_op jit(solution)/shard_map/ppermute | solution.py:330
  326.6 2.6 collective-permute-done.33
  330.5 3.5 convolution_multiply_fusion
  333.9 2.1 collective-permute-done.45
  336.1 1.9 collective-permute-done.41
  338.0 12.7 %collective-permute-done.38 = bf16[128,2048]{1,0:T(8,128)(2,1)} collective-permute-done((bf16[128,2048]{1,0:T(8,128)(2,1)}, bf16[128,2048]{1,0:T(8,128)(2,1)}, u32[]{:S(2)}, u32[]{:S(2)}) %collective-permute-start.38) | collective-permute-done | bytes 524320 | tf_op jit(solution)/shard_map/ppermute | solution.py:330
  350.7 3.1 collective-permute-done.34
  353.8 3.6 fusion.13
  (170 shorter events, 53.6 us)
Async XLA Ops:
  0.0 330.5 %copy-start = (bf16[512,2048]{1,0:T(8,128)(2,1)S(1)}, bf16[512,2048]{1,0:T(8,128)(2,1)}, u32[]{:S(2)}) copy-start(bf16[512,2048]{1,0:T(8,128)(2,1)} %param.37) | copy-start | bytes 6291460
  1.0 4.4 %collective-permute-start = (bf16[8,4096]{1,0:T(8,128)(2,1)S(1)}, bf16[8,4096]{1,0:T(8,128)(2,1)S(1)}, u32[]{:S(2)}, u32[]{:S(2)}) collective-permute-start(bf16[8,4096]{1,0:T(8,128)(2,1)S(1)} %slice.81), channel_id=1, source_target_pairs={{0,1},{1,2},{2,3},{3,4},{4,5},{5,6},{6,7},{7,8},{8,9},{9,10},{10,1... | collective-permute-start | bytes 196616 | tf_op jit(solution)/shard_map/ppermute | solution.py:437
  23.2 5.0 %collective-permute-start.1 = (f32[8,128,256]{2,1,0:T(8,128)S(1)}, f32[8,128,256]{2,1,0:T(8,128)}, u32[]{:S(2)}, u32[]{:S(2)}) collective-permute-start(f32[8,128,256]{2,1,0:T(8,128)S(1)} %slice_select_fusion), channel_id=1, source_target_pairs={{0,1},{1,0},{2,3},{3,2},{4,5},{5,4},{6,7},{7,6},{8,9},{9,8},{10,11... | collective-permute-start | bytes 3145736 | tf_op jit(solution)/shard_map/ppermute | solution.py:190
  32.2 8.8 %collective-permute-start.2 = (bf16[4,128,256]{2,1,0:T(8,128)(2,1)}, bf16[4,128,256]{2,1,0:T(8,128)(2,1)S(1)}, u32[]{:S(2)}, u32[]{:S(2)}) collective-permute-start(bf16[4,128,256]{2,1,0:T(8,128)(2,1)} %select_convert_fusion.1), channel_id=1, source_target_pairs={{0,2},{1,3},{2,0},{3,1},{4,6},{5,7},{6,4},{7,5},{8,10},{9,11},{10,... | collective-permute-start | bytes 786440 | tf_op jit(solution)/shard_map/ppermute | solution.py:190
  41.8 5.6 %collective-permute-start.3 = (bf16[2,128,256]{2,1,0:T(8,128)(2,1)S(1)}, bf16[2,128,256]{2,1,0:T(8,128)(2,1)S(1)}, u32[]{:S(2)}, u32[]{:S(2)}) collective-permute-start(bf16[2,128,256]{2,1,0:T(8,128)(2,1)S(1)} %select_convert_fusion.3), channel_id=1, source_target_pairs={{0,4},{1,5},{2,6},{3,7},{4,0},{5,1},{6,2},{7,3},{8,12},{9,13},{10,... | collective-permute-start | bytes 393224 | tf_op jit(solution)/shard_map/ppermute | solution.py:190
  44.4 46.9 %collective-permute-start.10 = (bf16[2048,512]{1,0:T(8,128)(2,1)}, bf16[2048,512]{1,0:T(8,128)(2,1)}, u32[]{:S(2)}, u32[]{:S(2)}) collective-permute-start(bf16[2048,512]{1,0:T(8,128)(2,1)} %param.28), channel_id=1, source_target_pairs={{0,2},{1,3},{2,0},{3,1},{4,6},{5,7},{6,4},{7,5},{8,10},{9,11},{10,... | collective-permute-start | bytes 6291464 | tf_op jit(solution)/shard_map/ppermute | solution.py:445
  47.9 6.9 %collective-permute-start.4 = (bf16[2,128,128]{2,1,0:T(8,128)(2,1)S(1)}, bf16[2,128,128]{2,1,0:T(8,128)(2,1)S(1)}, u32[]{:S(2)}, u32[]{:S(2)}) collective-permute-start(bf16[2,128,128]{2,1,0:T(8,128)(2,1)S(1)} %fusion.46), channel_id=1, source_target_pairs={{0,8},{1,9},{2,10},{3,11},{4,12},{5,13},{6,14},{7,15},{8,16},{9,17... | collective-permute-start | bytes 196616 | tf_op jit(solution)/shard_map/ppermute | solution.py:201
  55.0 6.2 %collective-permute-start.5 = (bf16[2,128,128]{2,1,0:T(8,128)(2,1)S(1)}, bf16[2,128,128]{2,1,0:T(8,128)(2,1)S(1)}, u32[]{:S(2)}, u32[]{:S(2)}) collective-permute-start(bf16[2,128,128]{2,1,0:T(8,128)(2,1)S(1)} %fusion.1), channel_id=1, source_target_pairs={{0,8},{1,9},{2,10},{3,11},{4,12},{5,13},{6,14},{7,15},{8,16},{9,17... | collective-permute-start | bytes 196616 | tf_op jit(solution)/shard_map/ppermute | solution.py:201
  61.4 6.2 %collective-permute-start.6 = (bf16[2,128,128]{2,1,0:T(8,128)(2,1)S(1)}, bf16[2,128,128]{2,1,0:T(8,128)(2,1)S(1)}, u32[]{:S(2)}, u32[]{:S(2)}) collective-permute-start(bf16[2,128,128]{2,1,0:T(8,128)(2,1)S(1)} %fusion.2), channel_id=1, source_target_pairs={{0,8},{1,9},{2,10},{3,11},{4,12},{5,13},{6,14},{7,15},{8,16},{9,17... | collective-permute-start | bytes 196616 | tf_op jit(solution)/shard_map/ppermute | solution.py:201
  67.8 4.3 %collective-permute-start.7 = (bf16[2,128,128]{2,1,0:T(8,128)(2,1)S(1)}, bf16[2,128,128]{2,1,0:T(8,128)(2,1)S(1)}, u32[]{:S(2)}, u32[]{:S(2)}) collective-permute-start(bf16[2,128,128]{2,1,0:T(8,128)(2,1)S(1)} %fusion.29), channel_id=1, source_target_pairs={{0,4},{1,5},{2,6},{3,7},{4,0},{5,1},{6,2},{7,3},{8,12},{9,13},{10,... | collective-permute-start | bytes 196616 | tf_op jit(solution)/shard_map/ppermute | solution.py:205
  68.4 52.0 %collective-permute-start.11 = (bf16[2048,512]{1,0:T(8,128)(2,1)}, bf16[2048,512]{1,0:T(8,128)(2,1)}, u32[]{:S(2)}, u32[]{:S(2)}) collective-permute-start(bf16[2048,512]{1,0:T(8,128)(2,1)} %param.28), channel_id=1, source_target_pairs={{0,1},{1,0},{2,3},{3,2},{4,5},{5,4},{6,7},{7,6},{8,9},{9,8},{10,11... | collective-permute-start | bytes 6291464 | tf_op jit(solution)/shard_map/ppermute | solution.py:446
  91.3 31.2 %collective-permute-start.12 = (bf16[2048,512]{1,0:T(8,128)(2,1)}, bf16[2048,512]{1,0:T(8,128)(2,1)}, u32[]{:S(2)}, u32[]{:S(2)}) collective-permute-start(bf16[2048,512]{1,0:T(8,128)(2,1)} %collective-permute-done.10), channel_id=1, source_target_pairs={{0,1},{1,0},{2,3},{3,2},{4,5},{5,4},{6,7},{7,6},{8,9},{9,8},{10,11... | collective-permute-start | bytes 6291464 | tf_op jit(solution)/shard_map/ppermute | solution.py:446
  91.4 6.0 %collective-permute-start.8 = (bf16[4,128,128]{2,1,0:T(8,128)(2,1)S(1)}, bf16[4,128,128]{2,1,0:T(8,128)(2,1)S(1)}, u32[]{:S(2)}, u32[]{:S(2)}) collective-permute-start(bf16[4,128,128]{2,1,0:T(8,128)(2,1)S(1)} %select_convert_fusion.2), channel_id=1, source_target_pairs={{0,2},{1,3},{2,0},{3,1},{4,6},{5,7},{6,4},{7,5},{8,10},{9,11},{10,... | collective-permute-start | bytes 393224 | tf_op jit(solution)/shard_map/ppermute | solution.py:205
  92.1 40.1 %collective-permute-start.26 = (bf16[2,2048,512]{2,1,0:T(8,128)(2,1)}, bf16[2,2048,512]{2,1,0:T(8,128)(2,1)}, u32[]{:S(2)}, u32[]{:S(2)}) collective-permute-start(bf16[2,2048,512]{2,1,0:T(8,128)(2,1)} %refs_9_.3), channel_id=1, source_target_pairs={{0,1},{1,0},{2,3},{3,2},{4,5},{5,4},{6,7},{7,6},{8,9},{9,8},{10,11... | collective-permute-start | bytes 12582920 | tf_op jit(solution)/shard_map/ppermute | solution.py:450
  98.2 4.0 %collective-permute-start.9 = (bf16[8,128,128]{2,1,0:T(8,128)(2,1)S(1)}, bf16[8,128,128]{2,1,0:T(8,128)(2,1)S(1)}, u32[]{:S(2)}, u32[]{:S(2)}) collective-permute-start(bf16[8,128,128]{2,1,0:T(8,128)(2,1)S(1)} %select_convert_fusion), channel_id=1, source_target_pairs={{0,1},{1,0},{2,3},{3,2},{4,5},{5,4},{6,7},{7,6},{8,9},{9,8},{10,11... | collective-permute-start | bytes 786440 | tf_op jit(solution)/shard_map/ppermute | solution.py:205
  98.3 46.5 %collective-permute-start.27 = (bf16[2,2048,512]{2,1,0:T(8,128)(2,1)}, bf16[2,2048,512]{2,1,0:T(8,128)(2,1)}, u32[]{:S(2)}, u32[]{:S(2)}) collective-permute-start(bf16[2,2048,512]{2,1,0:T(8,128)(2,1)} %refs_10_.3), channel_id=1, source_target_pairs={{0,1},{1,0},{2,3},{3,2},{4,5},{5,4},{6,7},{7,6},{8,9},{9,8},{10,11... | collective-permute-start | bytes 12582920 | tf_op jit(solution)/shard_map/ppermute | solution.py:450
  102.2 43.0 %collective-permute-start.28 = (bf16[2,512,2048]{2,1,0:T(8,128)(2,1)}, bf16[2,512,2048]{2,1,0:T(8,128)(2,1)}, u32[]{:S(2)}, u32[]{:S(2)}) collective-permute-start(bf16[2,512,2048]{2,1,0:T(8,128)(2,1)} %refs_11_.3), channel_id=1, source_target_pairs={{0,1},{1,0},{2,3},{3,2},{4,5},{5,4},{6,7},{7,6},{8,9},{9,8},{10,11... | collective-permute-start | bytes 12582920 | tf_op jit(solution)/shard_map/ppermute | solution.py:450
  127.1 16.4 %collective-permute-start.14 = (bf16[128,2176]{1,0:T(8,128)(2,1)}, bf16[128,2176]{1,0:T(8,128)(2,1)}, u32[]{:S(2)}, u32[]{:S(2)}) collective-permute-start(bf16[128,2176]{1,0:T(8,128)(2,1)} %concatenate.47.refs_0_), channel_id=1, source_target_pairs={{0,24},{1,25},{2,26},{3,27},{4,28},{5,29},{6,30},{7,31},{8,0},{9,1... | collective-permute-start | bytes 1671176 | tf_op jit(solution)/shard_map/ppermute | solution.py:330
  130.7 18.9 %collective-permute-start.20 = (bf16[128,2176]{1,0:T(8,128)(2,1)}, bf16[128,2176]{1,0:T(8,128)(2,1)}, u32[]{:S(2)}, u32[]{:S(2)}) collective-permute-start(bf16[128,2176]{1,0:T(8,128)(2,1)} %concatenate.47.refs_0_), channel_id=1, source_target_pairs={{0,4},{1,5},{2,6},{3,7},{4,0},{5,1},{6,2},{7,3},{8,12},{9,13},{10,... | collective-permute-start | bytes 1671176 | tf_op jit(solution)/shard_map/ppermute | solution.py:330
  132.2 18.9 %collective-permute-start.22 = (bf16[128,2176]{1,0:T(8,128)(2,1)}, bf16[128,2176]{1,0:T(8,128)(2,1)}, u32[]{:S(2)}, u32[]{:S(2)}) collective-permute-start(bf16[128,2176]{1,0:T(8,128)(2,1)} %concatenate.47.refs_0_), channel_id=1, source_target_pairs={{0,2},{1,3},{2,0},{3,1},{4,6},{5,7},{6,4},{7,5},{8,10},{9,11},{10,... | collective-permute-start | bytes 1671176 | tf_op jit(solution)/shard_map/ppermute | solution.py:330
  143.5 16.1 %collective-permute-start.23 = (bf16[128,2176]{1,0:T(8,128)(2,1)}, bf16[128,2176]{1,0:T(8,128)(2,1)}, u32[]{:S(2)}, u32[]{:S(2)}) collective-permute-start(bf16[128,2176]{1,0:T(8,128)(2,1)} %collective-permute-done.14.refs_1_), channel_id=1, source_target_pairs={{0,2},{1,3},{2,0},{3,1},{4,6},{5,7},{6,4},{7,5},{8,10},{9,11},{10,... | collective-permute-start | bytes 1671176 | tf_op jit(solution)/shard_map/ppermute | solution.py:330
  144.7 18.2 %collective-permute-start.13 = (bf16[128,2176]{1,0:T(8,128)(2,1)}, bf16[128,2176]{1,0:T(8,128)(2,1)S(1)}, u32[]{:S(2)}, u32[]{:S(2)}) collective-permute-start(bf16[128,2176]{1,0:T(8,128)(2,1)} %concatenate.47.refs_0_), channel_id=1, source_target_pairs={{0,8},{1,9},{2,10},{3,11},{4,12},{5,13},{6,14},{7,15},{8,16},{9,17... | collective-permute-start | bytes 1671176 | tf_op jit(solution)/shard_map/ppermute | solution.py:330
  145.2 40.1 %collective-permute-start.15 = (bf16[128,2176]{1,0:T(8,128)(2,1)}, bf16[128,2176]{1,0:T(8,128)(2,1)}, u32[]{:S(2)}, u32[]{:S(2)}) collective-permute-start(bf16[128,2176]{1,0:T(8,128)(2,1)} %concatenate.47.refs_0_), channel_id=1, source_target_pairs={{0,16},{1,17},{2,18},{3,19},{4,20},{5,21},{6,22},{7,23},{8,24},{9,... | collective-permute-start | bytes 1671176 | tf_op jit(solution)/shard_map/ppermute | solution.py:330
  149.6 37.1 %collective-permute-start.21 = (bf16[128,2176]{1,0:T(8,128)(2,1)}, bf16[128,2176]{1,0:T(8,128)(2,1)S(1)}, u32[]{:S(2)}, u32[]{:S(2)}) collective-permute-start(bf16[128,2176]{1,0:T(8,128)(2,1)} %collective-permute-done.14.refs_1_), channel_id=1, source_target_pairs={{0,4},{1,5},{2,6},{3,7},{4,0},{5,1},{6,2},{7,3},{8,12},{9,13},{10,... | collective-permute-start | bytes 1671176 | tf_op jit(solution)/shard_map/ppermute | solution.py:330
  151.1 35.7 %collective-permute-start.24 = (bf16[128,2176]{1,0:T(8,128)(2,1)}, bf16[128,2176]{1,0:T(8,128)(2,1)S(1)}, u32[]{:S(2)}, u32[]{:S(2)}) collective-permute-start(bf16[128,2176]{1,0:T(8,128)(2,1)} %collective-permute-done.20.refs_2_), channel_id=1, source_target_pairs={{0,2},{1,3},{2,0},{3,1},{4,6},{5,7},{6,4},{7,5},{8,10},{9,11},{10,... | collective-permute-start | bytes 1671176 | tf_op jit(solution)/shard_map/ppermute | solution.py:330
  159.6 27.2 %collective-permute-start.25 = (bf16[128,2176]{1,0:T(8,128)(2,1)}, bf16[128,2176]{1,0:T(8,128)(2,1)S(1)}, u32[]{:S(2)}, u32[]{:S(2)}) collective-permute-start(bf16[128,2176]{1,0:T(8,128)(2,1)} %collective-permute-done.23.refs_5_), channel_id=1, source_target_pairs={{0,4},{1,5},{2,6},{3,7},{4,0},{5,1},{6,2},{7,3},{8,12},{9,13},{10,... | collective-permute-start | bytes 1671176 | tf_op jit(solution)/shard_map/ppermute | solution.py:330
  161.6 52.0 %copy-start.24 = (bf16[2048]{0:T(1024)(128)(2,1)S(1)}, bf16[2048]{0:T(1024)(128)(2,1)}, u32[]{:S(2)}) copy-start(bf16[2048]{0:T(1024)(128)(2,1)} %param.38) | copy-start | bytes 12292
  162.9 47.8 %collective-permute-start.16 = (bf16[128,2176]{1,0:T(8,128)(2,1)S(1)}, bf16[128,2176]{1,0:T(8,128)(2,1)}, u32[]{:S(2)}, u32[]{:S(2)}) collective-permute-start(bf16[128,2176]{1,0:T(8,128)(2,1)S(1)} %collective-permute-done.13.refs_0_), channel_id=1, source_target_pairs={{0,4},{1,5},{2,6},{3,7},{4,0},{5,1},{6,2},{7,3},{8,12},{9,13},{10,... | collective-permute-start | bytes 1671176 | tf_op jit(solution)/shard_map/ppermute | solution.py:330
  185.3 26.8 %collective-permute-start.19 = (bf16[128,2176]{1,0:T(8,128)(2,1)}, bf16[128,2176]{1,0:T(8,128)(2,1)}, u32[]{:S(2)}, u32[]{:S(2)}) collective-permute-start(bf16[128,2176]{1,0:T(8,128)(2,1)} %collective-permute-done.15.refs_1_), channel_id=1, source_target_pairs={{0,2},{1,3},{2,0},{3,1},{4,6},{5,7},{6,4},{7,5},{8,10},{9,11},{10,... | collective-permute-start | bytes 1671176 | tf_op jit(solution)/shard_map/ppermute | solution.py:330
  208.0 15.1 %collective-permute-start.43 = (bf16[128,2048]{1,0:T(8,128)(2,1)}, bf16[128,2048]{1,0:T(8,128)(2,1)S(1)}, u32[]{:S(2)}, u32[]{:S(2)}) collective-permute-start(bf16[128,2048]{1,0:T(8,128)(2,1)} %get-tuple-element.46), channel_id=1, source_target_pairs={{0,4},{1,5},{2,6},{3,7},{4,0},{5,1},{6,2},{7,3},{8,12},{9,13},{10,... | collective-permute-start | bytes 1572872 | tf_op jit(solution)/shard_map/ppermute | solution.py:330
  209.5 17.0 %collective-permute-start.18 = (bf16[128,2176]{1,0:T(8,128)(2,1)S(1)}, bf16[128,2176]{1,0:T(8,128)(2,1)S(1)}, u32[]{:S(2)}, u32[]{:S(2)}) collective-permute-start(bf16[128,2176]{1,0:T(8,128)(2,1)S(1)} %collective-permute-done.13.refs_0_), channel_id=1, source_target_pairs={{0,2},{1,3},{2,0},{3,1},{4,6},{5,7},{6,4},{7,5},{8,10},{9,11},{10,... | collective-permute-start | bytes 1671176 | tf_op jit(solution)/shard_map/ppermute | solution.py:330
  210.1 25.1 %collective-permute-start.17 = (bf16[128,2176]{1,0:T(8,128)(2,1)}, bf16[128,2176]{1,0:T(8,128)(2,1)}, u32[]{:S(2)}, u32[]{:S(2)}) collective-permute-start(bf16[128,2176]{1,0:T(8,128)(2,1)} %collective-permute-done.15.refs_1_), channel_id=1, source_target_pairs={{0,4},{1,5},{2,6},{3,7},{4,0},{5,1},{6,2},{7,3},{8,12},{9,13},{10,... | collective-permute-start | bytes 1671176 | tf_op jit(solution)/shard_map/ppermute | solution.py:330
  210.7 26.4 %collective-permute-start.29 = (bf16[128,2176]{1,0:T(8,128)(2,1)}, bf16[128,2176]{1,0:T(8,128)(2,1)}, u32[]{:S(2)}, u32[]{:S(2)}) collective-permute-start(bf16[128,2176]{1,0:T(8,128)(2,1)} %collective-permute-done.16.refs_2_), channel_id=1, source_target_pairs={{0,2},{1,3},{2,0},{3,1},{4,6},{5,7},{6,4},{7,5},{8,10},{9,11},{10,... | collective-permute-start | bytes 1671176 | tf_op jit(solution)/shard_map/ppermute | solution.py:330
  212.1 35.0 %collective-permute-start.30 = (bf16[128,2176]{1,0:T(8,128)(2,1)}, bf16[128,2176]{1,0:T(8,128)(2,1)}, u32[]{:S(2)}, u32[]{:S(2)}) collective-permute-start(bf16[128,2176]{1,0:T(8,128)(2,1)} %collective-permute-done.19.refs_5_), channel_id=1, source_target_pairs={{0,4},{1,5},{2,6},{3,7},{4,0},{5,1},{6,2},{7,3},{8,12},{9,13},{10,... | collective-permute-start | bytes 1671176 | tf_op jit(solution)/shard_map/ppermute | solution.py:330
  223.1 46.8 %collective-permute-start.42 = (bf16[128,2048]{1,0:T(8,128)(2,1)}, bf16[128,2048]{1,0:T(8,128)(2,1)}, u32[]{:S(2)}, u32[]{:S(2)}) collective-permute-start(bf16[128,2048]{1,0:T(8,128)(2,1)} %get-tuple-element.45), channel_id=1, source_target_pairs={{0,4},{1,5},{2,6},{3,7},{4,0},{5,1},{6,2},{7,3},{8,12},{9,13},{10,... | collective-permute-start | bytes 1572872 | tf_op jit(solution)/shard_map/ppermute | solution.py:330
  227.4 43.9 %collective-permute-start.44 = (bf16[128,2048]{1,0:T(8,128)(2,1)}, bf16[128,2048]{1,0:T(8,128)(2,1)}, u32[]{:S(2)}, u32[]{:S(2)}) collective-permute-start(bf16[128,2048]{1,0:T(8,128)(2,1)} %add_convert_fusion.1), channel_id=1, source_target_pairs={{0,2},{1,3},{2,0},{3,1},{4,6},{5,7},{6,4},{7,5},{8,10},{9,11},{10,... | collective-permute-start | bytes 1572872 | tf_op jit(solution)/shard_map/ppermute | solution.py:330
  266.6 15.1 %collective-permute-start.36 = (bf16[128,2048]{1,0:T(8,128)(2,1)}, bf16[128,2048]{1,0:T(8,128)(2,1)S(1)}, u32[]{:S(2)}, u32[]{:S(2)}) collective-permute-start(bf16[128,2048]{1,0:T(8,128)(2,1)} %get-tuple-element.38), channel_id=1, source_target_pairs={{0,4},{1,5},{2,6},{3,7},{4,0},{5,1},{6,2},{7,3},{8,12},{9,13},{10,... | collective-permute-start | bytes 1572872 | tf_op jit(solution)/shard_map/ppermute | solution.py:330
  268.6 65.3 %collective-permute-start.39 = (bf16[128,2048]{1,0:T(8,128)(2,1)}, bf16[128,2048]{1,0:T(8,128)(2,1)}, u32[]{:S(2)}, u32[]{:S(2)}) collective-permute-start(bf16[128,2048]{1,0:T(8,128)(2,1)} %get-tuple-element.41), channel_id=1, source_target_pairs={{0,2},{1,3},{2,0},{3,1},{4,6},{5,7},{6,4},{7,5},{8,10},{9,11},{10,... | collective-permute-start | bytes 1572872 | tf_op jit(solution)/shard_map/ppermute | solution.py:330
  269.3 49.7 %collective-permute-start.35 = (bf16[128,2048]{1,0:T(8,128)(2,1)S(1)}, bf16[128,2048]{1,0:T(8,128)(2,1)S(1)}, u32[]{:S(2)}, u32[]{:S(2)}) collective-permute-start(bf16[128,2048]{1,0:T(8,128)(2,1)S(1)} %copy-done.28), channel_id=1, source_target_pairs={{0,4},{1,5},{2,6},{3,7},{4,0},{5,1},{6,2},{7,3},{8,12},{9,13},{10,... | collective-permute-start | bytes 1572872 | tf_op jit(solution)/shard_map/ppermute | solution.py:330
  269.9 25.1 %collective-permute-start.32 = (bf16[128,2048]{1,0:T(8,128)(2,1)S(1)}, bf16[128,2048]{1,0:T(8,128)(2,1)S(1)}, u32[]{:S(2)}, u32[]{:S(2)}) collective-permute-start(bf16[128,2048]{1,0:T(8,128)(2,1)S(1)} %copy-done.29), channel_id=1, source_target_pairs={{0,2},{1,3},{2,0},{3,1},{4,6},{5,7},{6,4},{7,5},{8,10},{9,11},{10,... | collective-permute-start | bytes 1572872 | tf_op jit(solution)/shard_map/ppermute | solution.py:330
  271.3 55.3 %collective-permute-start.31 = (bf16[128,2048]{1,0:T(8,128)(2,1)S(1)}, bf16[128,2048]{1,0:T(8,128)(2,1)S(1)}, u32[]{:S(2)}, u32[]{:S(2)}) collective-permute-start(bf16[128,2048]{1,0:T(8,128)(2,1)S(1)} %copy-done.27), channel_id=1, source_target_pairs={{0,2},{1,3},{2,0},{3,1},{4,6},{5,7},{6,4},{7,5},{8,10},{9,11},{10,... | collective-permute-start | bytes 1572872 | tf_op jit(solution)/shard_map/ppermute | solution.py:330
  281.8 35.7 %collective-permute-start.40 = (bf16[128,2048]{1,0:T(8,128)(2,1)S(1)}, bf16[128,2048]{1,0:T(8,128)(2,1)S(1)}, u32[]{:S(2)}, u32[]{:S(2)}) collective-permute-start(bf16[128,2048]{1,0:T(8,128)(2,1)S(1)} %copy-done.26), channel_id=1, source_target_pairs={{0,2},{1,3},{2,0},{3,1},{4,6},{5,7},{6,4},{7,5},{8,10},{9,11},{10,... | collective-permute-start | bytes 1572872 | tf_op jit(solution)/shard_map/ppermute | solution.py:330
  295.0 29.9 %collective-permute-start.37 = (bf16[128,2048]{1,0:T(8,128)(2,1)S(1)}, bf16[128,2048]{1,0:T(8,128)(2,1)S(1)}, u32[]{:S(2)}, u32[]{:S(2)}) collective-permute-start(bf16[128,2048]{1,0:T(8,128)(2,1)S(1)} %add_convert_fusion.4), channel_id=1, source_target_pairs={{0,2},{1,3},{2,0},{3,1},{4,6},{5,7},{6,4},{7,5},{8,10},{9,11},{10,... | collective-permute-start | bytes 1572872 | tf_op jit(solution)/shard_map/ppermute | solution.py:330
  317.5 11.7 %collective-permute-start.33 = (bf16[128,2048]{1,0:T(8,128)(2,1)S(1)}, bf16[128,2048]{1,0:T(8,128)(2,1)S(1)}, u32[]{:S(2)}, u32[]{:S(2)}) collective-permute-start(bf16[128,2048]{1,0:T(8,128)(2,1)S(1)} %add_convert_fusion.6), channel_id=1, source_target_pairs={{0,4},{1,5},{2,6},{3,7},{4,0},{5,1},{6,2},{7,3},{8,12},{9,13},{10,... | collective-permute-start | bytes 1572872 | tf_op jit(solution)/shard_map/ppermute | solution.py:330
  319.0 17.1 %collective-permute-start.45 = (bf16[128,2048]{1,0:T(8,128)(2,1)}, bf16[128,2048]{1,0:T(8,128)(2,1)}, u32[]{:S(2)}, u32[]{:S(2)}) collective-permute-start(bf16[128,2048]{1,0:T(8,128)(2,1)} %add_convert_fusion), channel_id=1, source_target_pairs={{0,8},{1,9},{2,10},{3,11},{4,12},{5,13},{6,14},{7,15},{8,16},{9,17... | collective-permute-start | bytes 1572872 | tf_op jit(solution)/shard_map/ppermute | solution.py:330
  324.9 13.1 %collective-permute-start.41 = (bf16[128,2048]{1,0:T(8,128)(2,1)}, bf16[128,2048]{1,0:T(8,128)(2,1)}, u32[]{:S(2)}, u32[]{:S(2)}) collective-permute-start(bf16[128,2048]{1,0:T(8,128)(2,1)} %add_convert_fusion.2), channel_id=1, source_target_pairs={{0,4},{1,5},{2,6},{3,7},{4,0},{5,1},{6,2},{7,3},{8,12},{9,13},{10,... | collective-permute-start | bytes 1572872 | tf_op jit(solution)/shard_map/ppermute | solution.py:330
  326.6 24.0 %collective-permute-start.38 = (bf16[128,2048]{1,0:T(8,128)(2,1)}, bf16[128,2048]{1,0:T(8,128)(2,1)}, u32[]{:S(2)}, u32[]{:S(2)}) collective-permute-start(bf16[128,2048]{1,0:T(8,128)(2,1)} %add_convert_fusion.3), channel_id=1, source_target_pairs={{0,16},{1,17},{2,18},{3,19},{4,20},{5,21},{6,22},{7,23},{8,24},{9,... | collective-permute-start | bytes 1572872 | tf_op jit(solution)/shard_map/ppermute | solution.py:330
  330.2 23.6 %collective-permute-start.34 = (bf16[128,2048]{1,0:T(8,128)(2,1)}, bf16[128,2048]{1,0:T(8,128)(2,1)}, u32[]{:S(2)}, u32[]{:S(2)}) collective-permute-start(bf16[128,2048]{1,0:T(8,128)(2,1)} %add_convert_fusion.5), channel_id=1, source_target_pairs={{0,24},{1,25},{2,26},{3,27},{4,28},{5,29},{6,30},{7,31},{8,0},{9,1... | collective-permute-start | bytes 1572872 | tf_op jit(solution)/shard_map/ppermute | solution.py:330
  (29 other events, 384.1 us)

commit v3 on v2

--- a/solution.py
+++ b/solution.py
@@ -139,6 +139,7 @@
         ],
         out_specs=[pl.BlockSpec((n, head, 2 * head), lambda s: (s, 0, 0)), pl.BlockSpec((n, rows, 2 * head), lambda s: (s, 0, 0))],
         out_shape=[jax.ShapeDtypeStruct((vheads, head, 2 * head), F32), jax.ShapeDtypeStruct((vheads, rows, 2 * head), F32)],
+        cost_estimate=pl.CostEstimate(flops=rows * head * head * vheads, bytes_accessed=rows * head * vheads, transcendentals=0),
         compiler_params=pltpu.CompilerParams(vmem_limit_bytes=40 * 2**20),
         name="delta_terms",
     )(mixed, mixed, mixed, before, before, before, conv_weight, conv_weight, conv_weight, cols, lines)
@@ -173,14 +174,18 @@
     )(read, state, output_gate, gain[None])
 
 
+def tie(value, *after):
+    return lax.optimization_barrier((value, *after))[0]
+
+
 def apply(transform, right):
     return jnp.einsum("hij,hjk->hik", transform, right, precision=lax.Precision.HIGHEST)
 
 
-def starting_states(block_map, count, place):
+def starting_states(block_map, count, place, first_half):
     head = block_map.shape[1]
     levels, step = [], 1
-    held = block_map
+    held, some = block_map, None
     while count % (2 * step) == 0 and 4 * step < count and held.shape[0] % 2 == 0:
         share = held.shape[0] // 2
         upper = (place // step) % 2 == 1
@@ -188,6 +193,8 @@
         give = jnp.where(upper, held[:share], held[share:])
         kind = F32 if step == 1 else BF16
         got = lax.ppermute(give.astype(kind), AXES, [(i, i ^ step) for i in range(count)]).astype(F32)
+        if step == 2 and first_half is not None:
+            some = first_half(got)
         early, late = jnp.where(upper, got, keep), jnp.where(upper, keep, got)
         merged = apply(late[:, :, :head], early)
         held = jnp.concatenate([merged[:, :, :head], merged[:, :, head:] + late[:, :, head:]], axis=2)
@@ -199,17 +206,23 @@
         if turn:
             ahead = ahead + apply(held[:, :, :head], state)
         state = lax.ppermute(ahead.astype(BF16), AXES, [(i, i + step) for i in range(count - step)]).astype(F32)
+    middle = state
     for step, upper, early in reversed(levels):
         second = apply(early[:, :, :head], state) + early[:, :, head:]
         mine, other = jnp.where(upper, second, state), jnp.where(upper, state, second)
         got = lax.ppermute(other.astype(BF16), AXES, [(i, i ^ step) for i in range(count)]).astype(F32)
         state = jnp.where(upper, jnp.concatenate([got, mine], axis=0), jnp.concatenate([mine, got], axis=0))
-    return state
+    return state, some, middle
 
 
 def places(mesh):
     at = {(*d.coords, d.core_on_chip): i for i, d in enumerate(mesh.devices.flat)}
     return at, tuple(max(c[k] for c in at) + 1 for k in range(4))
+
+
+def moves_to(layout, target):
+    at, _ = layout
+    return [(i, at[target(spot)]) for spot, i in at.items()]
 
 
 def moves(layout, x=0, y=0, z=0, core=0):
@@ -218,166 +231,194 @@
     return [(i, at[tuple((c + s) % n for c, s, n in zip(spot, shift, size))]) for spot, i in at.items()]
 
 
+def flip(layout, **by):
+    masks = {i ^ j for i, j in moves(layout, **by)}
+    return masks.pop() if len(masks) == 1 else None
+
+
 def expert_kernel(*refs, width, capacity, local_count):
     shards, (chosen_ref, *weights), outs = refs[:8], refs[8:15], refs[15:23]
-    sel_ref, pick_ref, gate_ref, back_ref = refs[23:]
-    step = pl.program_id(0)
+    block_ref, gate_w, up_w, down_w, sel_ref, pick_ref, gate_ref, back_ref, out_ref, in_sem, w_sem, out_sem = refs[23:]
     steps = 2 * local_count
     rows = shards[0].shape[0]
     pair_rows, slots = 2 * rows, 2 * capacity
     tile = width // 4
-    pairs = [(shards[i], shards[i + 1]) for i in range(0, 8, 2)]
-
-    def read(pair, lo, hi):
-        return jnp.concatenate([r[:, lo:hi] for r in pair], axis=0)
-
-    @pl.when(step == 0)
-    def _():
-        before = lax.broadcasted_iota(jnp.int32, (pair_rows, pair_rows), 0)
-        after = lax.broadcasted_iota(jnp.int32, (pair_rows, pair_rows), 1)
-        earlier = jnp.where((before < after) & (before // rows == after // rows), 1.0, 0.0).astype(BF16)
-        second = lax.broadcasted_iota(jnp.int32, (1, pair_rows), 1) // rows
-        slot = lax.broadcasted_iota(jnp.int32, (slots, pair_rows), 0)
-        for p, pair in enumerate(pairs):
-            gates = dot(chosen_ref[...], read(pair, width, pair[0].shape[1]), ((1,), (1,)))
-            named = jnp.where(gates != 0.0, 1.0, 0.0)
-            rank = dot(named.astype(BF16), earlier).astype(jnp.int32)
-            spot = jnp.where(gates != 0.0, rank + second * capacity, -1)
+    packet = shards[0].shape[1]
+
+    loads = [pltpu.make_async_copy(r, block_ref.at[i], in_sem.at[i]) for i, r in enumerate(shards)]
+    fills = []
+    for e in range(steps):
+        part = weights[:3] if e < local_count else weights[3:]
+        fills.append(
+            [
+                pltpu.make_async_copy(r.at[e % local_count], w.at[e], w_sem.at[e, k])
+                for k, (r, w) in enumerate(zip(part, (gate_w, up_w, down_w)))
+            ]
+        )
+    for copy in loads + sum(fills, []):
+        copy.start()
+
+    before = lax.broadcasted_iota(jnp.int32, (pair_rows, pair_rows), 0)
+    after = lax.broadcasted_iota(jnp.int32, (pair_rows, pair_rows), 1)
+    earlier = jnp.where((before < after) & (before // rows == after // rows), 1.0, 0.0).astype(BF16)
+    second = lax.broadcasted_iota(jnp.int32, (1, pair_rows), 1) // rows
+    slot = lax.broadcasted_iota(jnp.int32, (slots, pair_rows), 0)
+    for p in range(4):
+        loads[2 * p].wait()
+        loads[2 * p + 1].wait()
+        marks = block_ref[2 * p : 2 * p + 2, :, width:].reshape(pair_rows, packet - width)
+        gates = dot(chosen_ref[...], marks, ((1,), (1,)))
+        named = jnp.where(gates != 0.0, 1.0, 0.0)
+        rank = dot(named.astype(BF16), earlier).astype(jnp.int32)
+        spot = jnp.where(gates != 0.0, rank + second * capacity, -1)
+        for e in range(steps):
+            hit = slot == spot[e : e + 1]
+            pick_ref[p, e * slots : (e + 1) * slots, :] = jnp.where(hit, 1.0, 0.0).astype(BF16)
+            gate = jnp.sum(jnp.where(hit, gates[e : e + 1], 0.0), axis=1, keepdims=True)
+            gate_ref[e, p * slots : (p + 1) * slots, :] = jnp.broadcast_to(gate, (slots, 128))
+        for n in range(4):
+            cut = slice(n * tile, (n + 1) * tile)
+            taken = dot(pick_ref[p], block_ref[2 * p : 2 * p + 2, :, cut].reshape(pair_rows, tile)).astype(BF16)
             for e in range(steps):
-                hit = slot == spot[e : e + 1]
-                pick_ref[p, e * slots : (e + 1) * slots, :] = jnp.where(hit, 1.0, 0.0).astype(BF16)
-                gate = jnp.sum(jnp.where(hit, gates[e : e + 1], 0.0), axis=1, keepdims=True)
-                gate_ref[e, p * slots : (p + 1) * slots, :] = jnp.broadcast_to(gate, (slots, 128))
-            for n in range(4):
-                taken = dot(pick_ref[p], read(pair, n * tile, (n + 1) * tile)).astype(BF16)
-                for e in range(steps):
-                    sel_ref[e, p * slots : (p + 1) * slots, n * tile : (n + 1) * tile] = taken[e * slots : (e + 1) * slots]
-
-    def run(g_ref, u_ref, d_ref):
-        rows_in = sel_ref[step]
-        gate, up = dot(rows_in, g_ref[0]), dot(rows_in, u_ref[0])
+                sel_ref[e, p * slots : (p + 1) * slots, cut] = taken[e * slots : (e + 1) * slots]
+
+    for e in range(steps):
+        for copy in fills[e]:
+            copy.wait()
+        rows_in = sel_ref[e]
+        gate, up = dot(rows_in, gate_w[e]), dot(rows_in, up_w[e])
         hidden = (gate / (1.0 + jnp.exp(-gate)) * up).astype(BF16)
-        weight = gate_ref[step][:, 0:1]
-        at = pl.multiple_of(step * slots, slots)
+        weight = gate_ref[e][:, 0:1]
         for n in range(4):
-            result = (dot(hidden, d_ref[0, :, n * tile : (n + 1) * tile]) * weight).astype(BF16)
-            for p in range(len(pairs)):
-                back_ref[p, pl.ds(at, slots), n * tile : (n + 1) * tile] = result[p * slots : (p + 1) * slots]
-
-    @pl.when(step < local_count)
-    def _():
-        run(*weights[:3])
-
-    @pl.when(step >= local_count)
-    def _():
-        run(*weights[3:])
-
-    @pl.when(step == steps - 1)
-    def _():
-        for p in range(len(pairs)):
-            spread = pick_ref[p].astype(F32).T.astype(BF16)
-            for n in range(4):
-                cut = slice(n * tile, (n + 1) * tile)
-                total = dot(spread, back_ref[p, :, cut]).astype(BF16)
-                outs[2 * p][:, cut] = total[:rows]
-                outs[2 * p + 1][:, cut] = total[rows:]
+            cut = slice(n * tile, (n + 1) * tile)
+            result = (dot(hidden, down_w[e, :, cut]) * weight).astype(BF16)
+            for p in range(4):
+                back_ref[p, e * slots : (e + 1) * slots, cut] = result[p * slots : (p + 1) * slots]
+
+    stores = [pltpu.make_async_copy(out_ref.at[i], r, out_sem.at[i]) for i, r in enumerate(outs)]
+    for p in range(4):
+        spread = pick_ref[p].astype(F32).T.astype(BF16)
+        for n in range(4):
+            cut = slice(n * tile, (n + 1) * tile)
+            total = dot(spread, back_ref[p, :, cut]).astype(BF16)
+            out_ref[2 * p : 2 * p + 2, :, cut] = total.reshape(2, rows, tile)
+        stores[2 * p].start()
+        stores[2 * p + 1].start()
+    for copy in stores:
+        copy.wait()
 
 
 def run_experts(shards, chosen, mine, other, width, capacity):
     local_count, _, hidden = mine[0].shape
     steps = 2 * local_count
     slots = 2 * capacity
-    rows = shards[0].shape[0]
-    whole = lambda a: pl.BlockSpec(a.shape, lambda s: (0,) * a.ndim)
-    first = lambda a: pl.BlockSpec((1, *a.shape[1:]), lambda s: (jnp.minimum(s, local_count - 1), 0, 0))
-    then = lambda a: pl.BlockSpec((1, *a.shape[1:]), lambda s: (jnp.maximum(s - local_count, 0), 0, 0))
-    shapes = [jax.ShapeDtypeStruct((rows, width), BF16)] * 8
+    rows, packet = shards[0].shape
+    anywhere = pl.BlockSpec(memory_space=pl.ANY)
     return pl.pallas_call(
         functools.partial(expert_kernel, width=width, capacity=capacity, local_count=local_count),
-        grid=(steps,),
-        in_specs=[whole(a) for a in (*shards, chosen)] + [first(a) for a in mine] + [then(a) for a in other],
-        out_specs=[whole(a) for a in shapes],
-        out_shape=shapes,
+        in_specs=[anywhere] * 8 + [pl.BlockSpec(memory_space=pltpu.VMEM)] + [anywhere] * 6,
+        out_specs=[anywhere] * 8,
+        out_shape=[jax.ShapeDtypeStruct((rows, width), BF16)] * 8,
         scratch_shapes=[
+            pltpu.VMEM((8, rows, packet), BF16),
+            pltpu.VMEM((steps, width, hidden), BF16),
+            pltpu.VMEM((steps, width, hidden), BF16),
+            pltpu.VMEM((steps, hidden, width), BF16),
             pltpu.VMEM((steps, 4 * slots, width), BF16),
             pltpu.VMEM((4, steps * slots, 2 * rows), BF16),
             pltpu.VMEM((steps, 4 * slots, 128), F32),
             pltpu.VMEM((4, steps * slots, width), BF16),
+            pltpu.VMEM((8, rows, width), BF16),
+            pltpu.SemaphoreType.DMA((8,)),
+            pltpu.SemaphoreType.DMA((steps, 3)),
+            pltpu.SemaphoreType.DMA((8,)),
         ],
         cost_estimate=pl.CostEstimate(
             flops=steps * 4 * slots * (6 * width * hidden + 8 * width * rows),
             bytes_accessed=6 * width * hidden * steps + 32 * rows * width,
             transcendentals=0,
         ),
-        compiler_params=pltpu.CompilerParams(vmem_limit_bytes=58 * 2**20),
+        compiler_params=pltpu.CompilerParams(vmem_limit_bytes=56 * 2**20),
         name="experts",
     )(*shards, chosen, *mine, *other)
 
 
-def tie(value, *after):
-    return lax.optimization_barrier((value, *after))[0]
-
-
 def plus(*parts):
     return sum(p.astype(F32) for p in parts[1:]) + parts[0].astype(F32)
 
 
-def routed_by_gather(layout, place, routed_in, gates, weights, other, capacity):
+class Links:
+    def __init__(self, layout):
+        self.layout, self.sent = layout, {}
+
+    def send(self, value, link, turn=1):
+        queue = self.sent.setdefault(link, [])
+        if len(queue) >= 2:
+            value = tie(value, queue[-2])
+        queue.append(lax.ppermute(value, AXES, moves(self.layout, **{link: turn})))
+        return queue[-1]
+
+
+def routed_by_gather(layout, place, twin, routed_in, gates, weights, other, capacity):
     rows, width = routed_in.shape
     experts = gates.shape[1]
     local_count = weights[0].shape[0]
     deep = layout[1][2]
-    send = lambda a, **by: lax.ppermute(a, AXES, moves(layout, **by))
-    partner = jnp.asarray([j for _, j in sorted(moves(layout, core=1))], jnp.int32)[place]
-    ids = jnp.concatenate([p * local_count + jnp.arange(local_count, dtype=jnp.int32) for p in (place, partner)])
+    ids = jnp.concatenate([p * local_count + jnp.arange(local_count, dtype=jnp.int32) for p in (place, place ^ twin)])
     ids = jnp.pad(ids, (0, -ids.shape[0] % 8), constant_values=experts)
     chosen = (ids[:, None] == jnp.arange(experts, dtype=jnp.int32)).astype(BF16)
     pad = -(2 * experts) % 128
     chosen = jnp.pad(jnp.concatenate([chosen, chosen], axis=1), ((0, 0), (0, pad)))
     gates_hi, gates_lo = halves(gates)
     packet = jnp.concatenate([routed_in, gates_hi, gates_lo, jnp.zeros((rows, pad), BF16)], axis=1)
-
-    turns = [0, 1]
-    for i in range(2, deep // 2 + 1):
-        turns += [deep + 1 - i, i]
-    turns = turns[:deep]
-    across = [("x", "y"), ("y", "x")]
-    arrived = {0: packet}
-    hops = {}
-    ready = packet
-    for at, turn in enumerate(turns):
-        if turn:
-            arrived[turn] = send(ready, z=-turn)
-            if at == 2:
-                ready = tie(packet, arrived[turns[1]])
-    sums = {}
-    gone = ()
-    for at in range(0, deep, 2):
-        pair = turns[at : at + 2]
-        for turn in pair:
-            hops[turn] = {"x": send(arrived[turn], x=1), "y": send(arrived[turn], y=1)}
-        far = [
-            send(tie(hops[turn][first], *gone) if gone else hops[turn][first], **{second: 1})
-            for turn, (first, second) in zip(pair, across)
-        ]
-        shards = [arrived[t] for t in pair] + [hops[t]["x"] for t in pair] + [hops[t]["y"] for t in pair] + far
-        done = run_experts(shards, chosen, weights, other, width, capacity)
-        gone = (done[0],)
-        for i, turn in enumerate(pair):
-            sums[turn] = (done[i], {"x": done[2 + i], "y": done[4 + i]}, done[6 + i], across[i])
-    total = []
-    late = ()
-    for turn in turns[1:] + [0]:
-        own, to, far, (first, second) = sums[turn]
-        if turn == 0 and late:
-            far = tie(far, *late)
-        back = send(far, **{second: 1})
-        late = (back,)
-        to[first] = plus(to[first], back).astype(BF16)
-        got = [send(to[second], **{second: 1}), send(to[first], **{first: 1})]
-        part = plus(own, *got)
-        total.append(send(part.astype(BF16), z=turn).astype(F32) if turn else part)
-    return plus(*total)
+    packet = tie(packet, *other)
+
+    links = Links(layout)
+    here = {0: packet}
+    by_x, by_y, far, sums = {}, {}, {}, {}
+    pairs = [(t, t + 1) for t in range(0, deep, 2)]
+
+    def spread(t):
+        by_x[t], by_y[t] = links.send(here[t], "x"), links.send(here[t], "y")
+        if t + 1 < deep:
+            here[t + 1] = links.send(here[t], "z", -1)
+
+    for a, b in pairs:
+        if a == 0:
+            spread(a)
+            spread(b)
+        far[a], far[b] = links.send(by_x[a], "y"), links.send(by_y[b], "x")
+        ahead = [sums[a - 1][0]] if a else []
+        if b + 1 < deep:
+            spread(b + 1)
+            spread(b + 2)
+            ahead += [by_x[b + 2], by_y[b + 2]]
+        shards = [d[t] for d in (here, by_x, by_y, far) for t in (a, b)]
+        done = run_experts([tie(shards[0], *ahead), *shards[1:]], chosen, weights, other, width, capacity)
+        sums[a], sums[b] = done[0::2], done[1::2]
+    links = Links(layout)
+
+    def own_turn(t, straight, with_far):
+        part = plus(sums[t][0], straight, with_far)
+        return lax.ppermute(part.astype(BF16), AXES, moves(layout, z=t)) if t else part
+
+    def added(block, back):
+        return plus(block, back).astype(BF16)
+
+    back1 = links.send(sums[1][3], "x")
+    back0 = links.send(sums[0][3], "y")
+    straight1 = links.send(sums[1][1], "x")
+    last1 = links.send(added(sums[1][2], back1), "y")
+    total = [own_turn(1, straight1, last1)]
+    for a, b in pairs[1:]:
+        back_b, back_a = links.send(sums[b][3], "x"), links.send(sums[a][3], "y")
+        last_a, straight_a = links.send(added(sums[a][1], back_a), "x"), links.send(sums[a][2], "y")
+        total.append(own_turn(a, straight_a, last_a))
+        straight_b, last_b = links.send(sums[b][1], "x"), links.send(added(sums[b][2], back_b), "y")
+        total.append(own_turn(b, straight_b, last_b))
+    last0 = links.send(added(tie(sums[0][1], total[0]), back0), "x")
+    straight0 = links.send(tie(sums[0][2], total[0]), "y")
+    return plus(own_turn(0, straight0, last0), *total)
 
 
 def routed_by_exchange(routed_in, gates, named, weights, capacity):
@@ -437,22 +478,35 @@
     before = lax.ppermute(mixed_qkv[rows - 8 :], AXES, [(i, i + 1) for i in range(count - 1)])
     weights = (expert_gate, expert_up, expert_down)
     x, y, z, cores = layout[1]
-    paired = (x, y, cores) == (2, 2, 2) and z % 2 == 0
-    across_y, across_core = moves(layout, y=1), moves(layout, core=1)
+    twin, facing = flip(layout, core=1), flip(layout, y=1)
+    paired = (x, y, cores) == (2, 2, 2) and z % 2 == 0 and twin is not None
     columns = lax.axis_size("exp")
-    near = columns == 4 and all(i // columns == j // columns for i, j in across_y + across_core)
+    beside = {i ^ j for i, j in moves_to(layout, lambda c: (c[0], c[1], c[2] ^ 1, c[3]))} if z % 2 == 0 else set()
+    near = columns == 4 and None not in (twin, facing) and twin | facing == columns - 1 and len(beside) == 1
+    if paired:
+        other = [lax.ppermute(w, AXES, moves(layout, core=1)) for w in weights]
+    block_map, read = delta_terms(mixed_qkv, before, conv_weight, log_decay, write_strength, head)
+    half = out_weight.shape[0] // 2
+    odd = (place & min(beside)) != 0 if near else None
+
+    def first_half(done):
+        mine = tie(jnp.where(odd, out_weight[half:], out_weight[:half]), done)
+        return lax.ppermute(mine, AXES, moves(layout, y=1))
+
+    state, some, middle = starting_states(block_map, count, place, first_half if near else None)
     if near:
-        out_parts = [out_weight, lax.ppermute(out_weight, AXES, across_y)]
-        out_parts += [lax.ppermute(w, AXES, across_core) for w in out_parts]
-        twin, facing = (jnp.asarray([j for _, j in sorted(pairs)], jnp.int32) for pairs in (across_core, across_y))
-        owners = [p % columns for p in (place, facing[place], twin[place], facing[twin[place]])]
-    if paired:
-        other = [lax.ppermute(w, AXES, across_core) for w in weights]
-    block_map, read = delta_terms(mixed_qkv, before, conv_weight, log_decay, write_strength, head)
-    state = starting_states(block_map, count, place)
+        rest = lax.ppermute(tie(some, middle), AXES, moves_to(layout, lambda c: (c[0], c[1], c[2] ^ 1, c[3])))
+        out_parts = [[out_weight], [some, rest]]
+        out_parts += [[lax.ppermute(w, AXES, moves(layout, core=1)) for w in part] for part in out_parts]
+        owners = [(place ^ mask) % columns for mask in (0, facing, twin, facing | twin)]
     normed = emit(read, state, output_gate, norm_gain)
     if near:
-        products = [jnp.dot(normed, w, preferred_element_type=F32) for w in out_parts]
+        mine = jnp.where(odd, normed[:, half:], normed[:, :half])
+        others = jnp.where(odd, normed[:, :half], normed[:, half:])
+        products = []
+        for part in out_parts:
+            by = [normed] if len(part) == 1 else [mine, others]
+            products.append(sum(jnp.dot(n, w, preferred_element_type=F32) for n, w in zip(by, part)))
         projected = jnp.concatenate(
             [sum(jnp.where(o == e, p, 0.0) for o, p in zip(owners, products)) for e in range(columns)], axis=1
         )
@@ -471,7 +525,7 @@
     chosen = jnp.where(named, jnp.exp(jnp.where(named, logits, 0.0)), 0.0)
     gates = chosen / jnp.sum(chosen, axis=1, keepdims=True)
     if paired:
-        routed = routed_by_gather(layout, place, routed_in, gates, weights, other, capacity)
+        routed = routed_by_gather(layout, place, twin, routed_in, gates, weights, other, capacity)
     else:
         routed = routed_by_exchange(routed_in, gates, named, weights, capacity)
     shared_hidden = (

time: 363 us -> 314 us (0.87); the launches traced: 357 us -> 313 us
  waiting for transfers between devices: 187 us -> 144 us
  between operations: 8.11 us -> 0.69 us
  starting transfers between devices: 58.8 us -> 63.2 us
  other arithmetic: 18 us -> 22 us
    ppermute x36 -> x38, waiting for transfers between devices: 158 us -> 123 us  [the longest x27 90.6 us: send(): queue.append(lax.ppermute(value, AXES, moves(self.layout, **{link: turn})))]
    ppermute x3, waiting for transfers between devices: 12.2 us -> 5.05 us  [starting_states(): lax.ppermute(other.astype(BF16), AXES, [(i, i ^ step) for i in range(coun...]
    ppermute x36 -> x38, starting transfers between devices: 34.3 us -> 38.5 us  [the longest x27 35.3 us: send(): queue.append(lax.ppermute(value, AXES, moves(self.layout, **{link: turn})))]
    dot_general x4 -> x6, matrix products: 8.51 us -> 9.11 us  [local(): jnp.dot(n, w, preferred_element_type=F32)]
  transfers between devices with their start and end apart: 46 -> 48, of which waited for: 27 -> 25; matrix products, arithmetic and copies ran while one was open for 8% -> 11% of each run, Pallas kernels for 12% -> 13%
where the time goes in v3:
time: 314 us; the launch traced here: 313 us
  waiting for transfers between devices  144 us (46%)
  starting transfers between devices  63.2 us (20%)
  Pallas kernels  55.9 us (18%)
  other arithmetic  22 us (7%)
  matrix products  19 us (6%)
  local copies, waits for them, and re-layouts  7.96 us (3%)
    ppermute x27, waiting for transfers between devices, send(): queue.append(lax.ppermute(value, AXES, moves(self.layout, **{link: turn})))  90.6 us
    pallas_call x2, Pallas kernels, run_experts(): pl.pallas_call(functools.partial(expert_kernel, width=width, capacity=cap...  37.9 us
    ppermute x27, starting transfers between devices, send(): queue.append(lax.ppermute(value, AXES, moves(self.layout, **{link: turn})))  35.3 us
    pallas_call x1, Pallas kernels, delta_terms(): pl.pallas_call(functools.partial(delta_kernel, head=head, per=per), grid=...  13.7 us
    ppermute x3, starting transfers between devices, starting_states(): lax.ppermute(ahead.astype(BF16), AXES, [(i, i + step) for i in range(coun...  13.6 us
    ppermute x1, waiting for transfers between devices, local(): lax.ppermute(tie(some, middle), AXES, moves_to(layout, lambda c: (c[0], c...  13.3 us
    ppermute x3, waiting for transfers between devices, starting_states(): lax.ppermute(give.astype(kind), AXES, [(i, i ^ step) for i in range(count)])  12.3 us
    ppermute x3, waiting for transfers between devices, own_turn(): lax.ppermute(part.astype(BF16), AXES, moves(layout, z=t))  10.2 us
  transfers between devices with their start and end apart: 48, of which 25 were waited for; matrix products, arithmetic and copies ran while one was open for 11% of the time, Pallas kernels for 13%

profile of v3, /device:TPU:0, one launch (start us, length us, event | category | flops | bytes accessed | tf_op | source)
XLA Modules:
  0.0 313.0 jit_solution(3238684554062247457)
XLA Ops:
  1.0 2.3 collective-permute-start
  7.4 13.7 %delta_terms.1 = (f32[16,128,256]{2,1,0:T(8,128)S(1)}, f32[16,128,256]{2,1,0:T(8,128)S(1)}) custom-call(bf16[128,4096]{1,0:T(8,128)(2,1)S(1)} %copy-done.1, bf16[128,4096]{1,0:T(8,128)(2,1)S(1)} %copy-done.1, bf16[128,4096]{1,0:T(8,128)(2,1)S(1)} %copy-done.1, bf16[8,4096]{1,0:T(8,128)(2,1)S(1)} %collective-permute-done.qb_ref.kb_ref.vb_ref, ...), custom_call_target="tpu_custom_call" | custom-call | flops 33554432 | bytes 262144 | tf_op jit(solution)/shard_map/delta_terms/pallas_call | solution.py:132
  23.1 2.6 collective-permute-start.1
  25.8 2.4 collective-permute-done.1
  28.2 2.1 broadcast_select_fusion.1
  32.2 1.9 collective-permute-start.2
  34.1 6.9 %collective-permute-done.2 = bf16[4,128,256]{2,1,0:T(8,128)(2,1)S(1)} collective-permute-done((bf16[4,128,256]{2,1,0:T(8,128)(2,1)}, bf16[4,128,256]{2,1,0:T(8,128)(2,1)S(1)}, u32[]{:S(2)}, u32[]{:S(2)}) %collective-permute-start.2) | collective-permute-done | bytes 262176 | tf_op jit(solution)/shard_map/ppermute | solution.py:195
  42.0 2.6 collective-permute-start.3
  44.6 3.0 collective-permute-done.3
  48.0 5.0 %collective-permute-start.4 = (bf16[2,128,128]{2,1,0:T(8,128)(2,1)S(1)}, bf16[2,128,128]{2,1,0:T(8,128)(2,1)S(1)}, u32[]{:S(2)}, u32[]{:S(2)}) collective-permute-start(bf16[2,128,128]{2,1,0:T(8,128)(2,1)S(1)} %fusion.47), channel_id=1, source_target_pairs={{0,8},{1,9},{2,10},{3,11},{4,12},{5,13},{6,14},{7,15},{8,16},{9,17... | collective-permute-start | bytes 196616 | tf_op jit(solution)/shard_map/ppermute | solution.py:208
  53.1 1.7 slice_select_fusion
  55.3 4.1 %collective-permute-start.5 = (bf16[2,128,128]{2,1,0:T(8,128)(2,1)S(1)}, bf16[2,128,128]{2,1,0:T(8,128)(2,1)S(1)}, u32[]{:S(2)}, u32[]{:S(2)}) collective-permute-start(bf16[2,128,128]{2,1,0:T(8,128)(2,1)S(1)} %fusion.1), channel_id=1, source_target_pairs={{0,8},{1,9},{2,10},{3,11},{4,12},{5,13},{6,14},{7,15},{8,16},{9,17... | collective-permute-start | bytes 196616 | tf_op jit(solution)/shard_map/ppermute | solution.py:208
  59.4 1.9 collective-permute-done.5
  61.5 4.4 %collective-permute-start.6 = (bf16[2,128,128]{2,1,0:T(8,128)(2,1)S(1)}, bf16[2,128,128]{2,1,0:T(8,128)(2,1)S(1)}, u32[]{:S(2)}, u32[]{:S(2)}) collective-permute-start(bf16[2,128,128]{2,1,0:T(8,128)(2,1)S(1)} %fusion.2), channel_id=1, source_target_pairs={{0,8},{1,9},{2,10},{3,11},{4,12},{5,13},{6,14},{7,15},{8,16},{9,17... | collective-permute-start | bytes 196616 | tf_op jit(solution)/shard_map/ppermute | solution.py:208
  66.1 1.6 collective-permute-done.6
  68.6 9.2 %collective-permute-done.10 = bf16[1024,512]{1,0:T(8,128)(2,1)S(1)} collective-permute-done((bf16[1024,512]{1,0:T(8,128)(2,1)S(1)}, bf16[1024,512]{1,0:T(8,128)(2,1)S(1)}, u32[]{:S(2)}, u32[]{:S(2)}) %collective-permute-start.10) | collective-permute-done | bytes 1048608 | tf_op jit(solution)/shard_map/ppermute | solution.py:494
  81.3 3.5 %collective-permute-done.8 = bf16[4,128,128]{2,1,0:T(8,128)(2,1)S(1)} collective-permute-done((bf16[4,128,128]{2,1,0:T(8,128)(2,1)S(1)}, bf16[4,128,128]{2,1,0:T(8,128)(2,1)S(1)}, u32[]{:S(2)}, u32[]{:S(2)}) %collective-permute-start.8) | collective-permute-done | bytes 131104 | tf_op jit(solution)/shard_map/ppermute | solution.py:213
  86.4 13.3 %collective-permute-done.11 = bf16[1024,512]{1,0:T(8,128)(2,1)S(1)} collective-permute-done((bf16[1024,512]{1,0:T(8,128)(2,1)S(1)}, bf16[1024,512]{1,0:T(8,128)(2,1)S(1)}, u32[]{:S(2)}, u32[]{:S(2)}) %collective-permute-start.11) | collective-permute-done | bytes 1048608 | tf_op jit(solution)/shard_map/ppermute | solution.py:498
  103.5 2.3 maximum_select_fusion.state_ref
  105.8 4.3 %emit.1 = bf16[128,2048]{1,0:T(8,128)(2,1)} custom-call(f32[16,128,256]{2,1,0:T(8,128)} %copy-done.3, f32[16,128,128]{2,1,0:T(8,128)} %maximum_select_fusion.state_ref, bf16[128,2048]{1,0:T(8,128)(2,1)} %gate_ref.1, f32[1,128]{1,0:T(1,128)} %bitcast.46), custom_call_target="tpu_custom_call" | custom-call | tf_op jit(solution)/shard_map/emit/pallas_call | solution.py:162
  110.2 1.7 fusion.38
  113.7 2.0 fusion.52
  115.8 2.0 fusion.53
  122.3 2.4 collective-permute-start.18
  126.2 11.1 %collective-permute-done.18.refs_1_ = bf16[128,2176]{1,0:T(8,128)(2,1)S(1)} collective-permute-done((bf16[128,2176]{1,0:T(8,128)(2,1)}, bf16[128,2176]{1,0:T(8,128)(2,1)S(1)}, u32[]{:S(2)}, u32[]{:S(2)}) %collective-permute-start.18) | collective-permute-done | bytes 557088 | tf_op jit(solution)/shard_map/ppermute | solution.py:358
  137.3 4.1 %collective-permute-start.19 = (bf16[128,2176]{1,0:T(8,128)(2,1)S(1)}, bf16[128,2176]{1,0:T(8,128)(2,1)}, u32[]{:S(2)}, u32[]{:S(2)}) collective-permute-start(bf16[128,2176]{1,0:T(8,128)(2,1)S(1)} %collective-permute-done.18.refs_1_), channel_id=1, source_target_pairs={{0,24},{1,25},{2,26},{3,27},{4,28},{5,29},{6,30},{7,31},{8,0},{9,1... | collective-permute-start | bytes 1671176 | tf_op jit(solution)/shard_map/ppermute | solution.py:358
  143.5 9.3 %collective-permute-done.19.refs_0_ = bf16[128,2176]{1,0:T(8,128)(2,1)} collective-permute-done((bf16[128,2176]{1,0:T(8,128)(2,1)S(1)}, bf16[128,2176]{1,0:T(8,128)(2,1)}, u32[]{:S(2)}, u32[]{:S(2)}) %collective-permute-start.19) | collective-permute-done | bytes 557088 | tf_op jit(solution)/shard_map/ppermute | solution.py:358
  152.7 4.4 %collective-permute-start.20 = (bf16[128,2176]{1,0:T(8,128)(2,1)}, bf16[128,2176]{1,0:T(8,128)(2,1)}, u32[]{:S(2)}, u32[]{:S(2)}) collective-permute-start(bf16[128,2176]{1,0:T(8,128)(2,1)} %collective-permute-done.19.refs_0_), channel_id=1, source_target_pairs={{0,24},{1,25},{2,26},{3,27},{4,28},{5,29},{6,30},{7,31},{8,0},{9,1... | collective-permute-start | bytes 1671176 | tf_op jit(solution)/shard_map/ppermute | solution.py:358
  159.2 7.8 %collective-permute-done.26.refs_6_ = bf16[128,2176]{1,0:T(8,128)(2,1)} collective-permute-done((bf16[128,2176]{1,0:T(8,128)(2,1)}, bf16[128,2176]{1,0:T(8,128)(2,1)}, u32[]{:S(2)}, u32[]{:S(2)}) %collective-permute-start.26) | collective-permute-done | bytes 557088 | tf_op jit(solution)/shard_map/ppermute | solution.py:358
  169.4 3.6 %collective-permute-done.23.refs_7_ = bf16[128,2176]{1,0:T(8,128)(2,1)} collective-permute-done((bf16[128,2176]{1,0:T(8,128)(2,1)}, bf16[128,2176]{1,0:T(8,128)(2,1)}, u32[]{:S(2)}, u32[]{:S(2)}) %collective-permute-start.23) | collective-permute-done | bytes 557088 | tf_op jit(solution)/shard_map/ppermute | solution.py:358
  174.4 10.4 %collective-permute-done.28.refs_3_ = bf16[128,2176]{1,0:T(8,128)(2,1)S(1)} collective-permute-done((bf16[128,2176]{1,0:T(8,128)(2,1)}, bf16[128,2176]{1,0:T(8,128)(2,1)S(1)}, u32[]{:S(2)}, u32[]{:S(2)}) %collective-permute-start.28) | collective-permute-done | bytes 557088 | tf_op jit(solution)/shard_map/ppermute | solution.py:358
  186.3 10.4 %collective-permute-done.24.refs_3_ = bf16[128,2176]{1,0:T(8,128)(2,1)S(1)} collective-permute-done((bf16[128,2176]{1,0:T(8,128)(2,1)}, bf16[128,2176]{1,0:T(8,128)(2,1)S(1)}, u32[]{:S(2)}, u32[]{:S(2)}) %collective-permute-start.24) | collective-permute-done | bytes 557088 | tf_op jit(solution)/shard_map/ppermute | solution.py:358
  196.8 18.9 %experts.2 = (bf16[128,2048]{1,0:T(8,128)(2,1)}, bf16[128,2048]{1,0:T(8,128)(2,1)}, bf16[128,2048]{1,0:T(8,128)(2,1)}, bf16[128,2048]{1,0:T(8,128)(2,1)}, bf16[1...) custom-call(bf16[128,2176]{1,0:T(8,128)(2,1)} %concatenate.47.refs_0_, ...), custom_call_target="tpu_custom_call" | custom-call | flops 6442450944 | bytes 33554432 | tf_op jit(solution)/shard_map/experts/pallas_call | solution.py:317
  217.4 2.0 collective-permute-start.36
  220.6 10.3 %collective-permute-done.30 = bf16[128,2048]{1,0:T(8,128)(2,1)S(1)} collective-permute-done((bf16[128,2048]{1,0:T(8,128)(2,1)}, bf16[128,2048]{1,0:T(8,128)(2,1)S(1)}, u32[]{:S(2)}, u32[]{:S(2)}) %collective-permute-start.30) | collective-permute-done | bytes 524320 | tf_op jit(solution)/shard_map/ppermute | solution.py:358
  230.8 2.0 add_convert_fusion.6
  234.3 7.4 %collective-permute-done.36.refs_7_ = bf16[128,2176]{1,0:T(8,128)(2,1)} collective-permute-done((bf16[128,2176]{1,0:T(8,128)(2,1)S(1)}, bf16[128,2176]{1,0:T(8,128)(2,1)}, u32[]{:S(2)}, u32[]{:S(2)}) %collective-permute-start.36) | collective-permute-done | bytes 557088 | tf_op jit(solution)/shard_map/ppermute | solution.py:358
  241.7 19.0 %experts.3 = (bf16[128,2048]{1,0:T(8,128)(2,1)}, bf16[128,2048]{1,0:T(8,128)(2,1)}, bf16[128,2048]{1,0:T(8,128)(2,1)}, bf16[128,2048]{1,0:T(8,128)(2,1)}, bf16[1...) custom-call(bf16[128,2176]{1,0:T(8,128)(2,1)} %collective-permute-done.1, ...), custom_call_target="tpu_custom_call" | custom-call | flops 6442450944 | bytes 33554432 | tf_op jit(solution)/shard_map/experts/pallas_call | solution.py:317
  265.6 10.4 %collective-permute-done.39 = bf16[128,2048]{1,0:T(8,128)(2,1)S(1)} collective-permute-done((bf16[128,2048]{1,0:T(8,128)(2,1)}, bf16[128,2048]{1,0:T(8,128)(2,1)S(1)}, u32[]{:S(2)}, u32[]{:S(2)}) %collective-permute-start.39) | collective-permute-done | bytes 524320 | tf_op jit(solution)/shard_map/ppermute | solution.py:358
  279.8 2.4 collective-permute-done.32
  282.3 2.7 collective-permute-done.37
  286.4 2.0 add_convert_fusion
  288.4 1.7 collective-permute-done.40
  291.2 4.6 %collective-permute-done.43 = bf16[128,2048]{1,0:T(8,128)(2,1)S(1)} collective-permute-done((bf16[128,2048]{1,0:T(8,128)(2,1)S(1)}, bf16[128,2048]{1,0:T(8,128)(2,1)S(1)}, u32[]{:S(2)}, u32[]{:S(2)}) %collective-permute-start.43) | collective-permute-done | bytes 524320 | tf_op jit(solution)/shard_map/ppermute | solution.py:358
  298.2 3.4 %convolution_multiply_fusion = f32[128,2048]{1,0:T(8,128)} fusion(bf16[512,2048]{1,0:T(8,128)(2,1)S(1)} %copy-done, bf16[128,2048]{1,0:T(8,128)(2,1)S(1)} %fusion.11, bf16[2048,512]{1,0:T(8,128)(2,1)} %param.33, f32[128]{0:T(128)S(1)} %fusion.8, f32[128,512]{1,0:T(8,128)S(1)} %fusion.54), kind=kOutput, calls=%fused_computation | convolution fusion | flops 537526272 | bytes 6029824 | tf_op jit(solution)/shard_map/dot_general | solution.py:536
  301.7 2.3 collective-permute-done.41
  303.9 5.5 %collective-permute-done.45 = bf16[128,2048]{1,0:T(8,128)(2,1)} collective-permute-done((bf16[128,2048]{1,0:T(8,128)(2,1)}, bf16[128,2048]{1,0:T(8,128)(2,1)}, u32[]{:S(2)}, u32[]{:S(2)}) %collective-permute-start.45) | collective-permute-done | bytes 524320 | tf_op jit(solution)/shard_map/ppermute | solution.py:403
  309.5 3.6 %fusion.13 = bf16[128,2048]{1,0:T(8,128)(2,1)} fusion(f32[128,2048]{1,0:T(8,128)} %convolution_multiply_fusion, bf16[128,2048]{1,0:T(8,128)(2,1)S(1)} %get-tuple-element.90, bf16[128,2048]{1,0:T(8,128)(2,1)} %get-tuple-element.88, bf16[128,2048]{1,0:T(8,128)(2,1)} %collective-permute-done.47, bf16[128,2048]{1,0:T(8,128)(2,1)} %collective-permute-done.46, ...), kind=kLoop, calls=%fused_computation.27 | loop fusion | flops 3932160 | bytes 5242880 | tf_op jit(solution)/shard_map/convert_element_type | solution.py:537
  (183 shorter events, 55.9 us)
Async XLA Ops:
  1.0 4.4 %collective-permute-start = (bf16[8,4096]{1,0:T(8,128)(2,1)S(1)}, bf16[8,4096]{1,0:T(8,128)(2,1)S(1)}, u32[]{:S(2)}, u32[]{:S(2)}) collective-permute-start(bf16[8,4096]{1,0:T(8,128)(2,1)S(1)} %slice.95), channel_id=1, source_target_pairs={{0,1},{1,2},{2,3},{3,4},{4,5},{5,6},{6,7},{7,8},{8,9},{9,10},{10,1... | collective-permute-start | bytes 196616 | tf_op jit(solution)/shard_map/ppermute | solution.py:478
  23.1 5.0 %collective-permute-start.1 = (f32[8,128,256]{2,1,0:T(8,128)S(1)}, f32[8,128,256]{2,1,0:T(8,128)}, u32[]{:S(2)}, u32[]{:S(2)}) collective-permute-start(f32[8,128,256]{2,1,0:T(8,128)S(1)} %slice_select_fusion.1), channel_id=1, source_target_pairs={{0,1},{1,0},{2,3},{3,2},{4,5},{5,4},{6,7},{7,6},{8,9},{9,8},{10,11... | collective-permute-start | bytes 3145736 | tf_op jit(solution)/shard_map/ppermute | solution.py:195
  32.2 8.8 %collective-permute-start.2 = (bf16[4,128,256]{2,1,0:T(8,128)(2,1)}, bf16[4,128,256]{2,1,0:T(8,128)(2,1)S(1)}, u32[]{:S(2)}, u32[]{:S(2)}) collective-permute-start(bf16[4,128,256]{2,1,0:T(8,128)(2,1)} %select_convert_fusion.1), channel_id=1, source_target_pairs={{0,2},{1,3},{2,0},{3,1},{4,6},{5,7},{6,4},{7,5},{8,10},{9,11},{10,... | collective-permute-start | bytes 786440 | tf_op jit(solution)/shard_map/ppermute | solution.py:195
  42.0 5.6 %collective-permute-start.3 = (bf16[2,128,256]{2,1,0:T(8,128)(2,1)S(1)}, bf16[2,128,256]{2,1,0:T(8,128)(2,1)S(1)}, u32[]{:S(2)}, u32[]{:S(2)}) collective-permute-start(bf16[2,128,256]{2,1,0:T(8,128)(2,1)S(1)} %select_convert_fusion.3), channel_id=1, source_target_pairs={{0,4},{1,5},{2,6},{3,7},{4,0},{5,1},{6,2},{7,3},{8,12},{9,13},{10,... | collective-permute-start | bytes 393224 | tf_op jit(solution)/shard_map/ppermute | solution.py:195
  48.0 7.1 %collective-permute-start.4 = (bf16[2,128,128]{2,1,0:T(8,128)(2,1)S(1)}, bf16[2,128,128]{2,1,0:T(8,128)(2,1)S(1)}, u32[]{:S(2)}, u32[]{:S(2)}) collective-permute-start(bf16[2,128,128]{2,1,0:T(8,128)(2,1)S(1)} %fusion.47), channel_id=1, source_target_pairs={{0,8},{1,9},{2,10},{3,11},{4,12},{5,13},{6,14},{7,15},{8,16},{9,17... | collective-permute-start | bytes 196616 | tf_op jit(solution)/shard_map/ppermute | solution.py:208
  54.7 23.0 %collective-permute-start.10 = (bf16[1024,512]{1,0:T(8,128)(2,1)S(1)}, bf16[1024,512]{1,0:T(8,128)(2,1)S(1)}, u32[]{:S(2)}, u32[]{:S(2)}) collective-permute-start(bf16[1024,512]{1,0:T(8,128)(2,1)S(1)} %slice_select_fusion), channel_id=1, source_target_pairs={{0,2},{1,3},{2,0},{3,1},{4,6},{5,7},{6,4},{7,5},{8,10},{9,11},{10,... | collective-permute-start | bytes 3145736 | tf_op jit(solution)/shard_map/ppermute | solution.py:494
  55.3 6.0 %collective-permute-start.5 = (bf16[2,128,128]{2,1,0:T(8,128)(2,1)S(1)}, bf16[2,128,128]{2,1,0:T(8,128)(2,1)S(1)}, u32[]{:S(2)}, u32[]{:S(2)}) collective-permute-start(bf16[2,128,128]{2,1,0:T(8,128)(2,1)S(1)} %fusion.1), channel_id=1, source_target_pairs={{0,8},{1,9},{2,10},{3,11},{4,12},{5,13},{6,14},{7,15},{8,16},{9,17... | collective-permute-start | bytes 196616 | tf_op jit(solution)/shard_map/ppermute | solution.py:208
  61.5 6.2 %collective-permute-start.6 = (bf16[2,128,128]{2,1,0:T(8,128)(2,1)S(1)}, bf16[2,128,128]{2,1,0:T(8,128)(2,1)S(1)}, u32[]{:S(2)}, u32[]{:S(2)}) collective-permute-start(bf16[2,128,128]{2,1,0:T(8,128)(2,1)S(1)} %fusion.2), channel_id=1, source_target_pairs={{0,8},{1,9},{2,10},{3,11},{4,12},{5,13},{6,14},{7,15},{8,16},{9,17... | collective-permute-start | bytes 196616 | tf_op jit(solution)/shard_map/ppermute | solution.py:208
  66.0 46.0 %collective-permute-start.12 = (bf16[2048,512]{1,0:T(8,128)(2,1)}, bf16[2048,512]{1,0:T(8,128)(2,1)}, u32[]{:S(2)}, u32[]{:S(2)}) collective-permute-start(bf16[2048,512]{1,0:T(8,128)(2,1)} %param.25), channel_id=1, source_target_pairs={{0,1},{1,0},{2,3},{3,2},{4,5},{5,4},{6,7},{7,6},{8,9},{9,8},{10,11... | collective-permute-start | bytes 6291464 | tf_op jit(solution)/shard_map/ppermute | solution.py:500
  67.9 11.4 %collective-permute-start.7 = (bf16[2,128,128]{2,1,0:T(8,128)(2,1)S(1)}, bf16[2,128,128]{2,1,0:T(8,128)(2,1)S(1)}, u32[]{:S(2)}, u32[]{:S(2)}) collective-permute-start(bf16[2,128,128]{2,1,0:T(8,128)(2,1)S(1)} %select_convert_fusion.4), channel_id=1, source_target_pairs={{0,4},{1,5},{2,6},{3,7},{4,0},{5,1},{6,2},{7,3},{8,12},{9,13},{10,... | collective-permute-start | bytes 196616 | tf_op jit(solution)/shard_map/ppermute | solution.py:213
  77.7 22.0 %collective-permute-start.11 = (bf16[1024,512]{1,0:T(8,128)(2,1)S(1)}, bf16[1024,512]{1,0:T(8,128)(2,1)S(1)}, u32[]{:S(2)}, u32[]{:S(2)}) collective-permute-start(bf16[1024,512]{1,0:T(8,128)(2,1)S(1)} %collective-permute-done.10), channel_id=1, source_target_pairs={{0,8},{1,9},{2,10},{3,11},{4,12},{5,13},{6,14},{7,15},{8,0},{9,1},... | collective-permute-start | bytes 3145736 | tf_op jit(solution)/shard_map/ppermute | solution.py:498
  79.8 5.0 %collective-permute-start.8 = (bf16[4,128,128]{2,1,0:T(8,128)(2,1)S(1)}, bf16[4,128,128]{2,1,0:T(8,128)(2,1)S(1)}, u32[]{:S(2)}, u32[]{:S(2)}) collective-permute-start(bf16[4,128,128]{2,1,0:T(8,128)(2,1)S(1)} %select_convert_fusion.2), channel_id=1, source_target_pairs={{0,2},{1,3},{2,0},{3,1},{4,6},{5,7},{6,4},{7,5},{8,10},{9,11},{10,... | collective-permute-start | bytes 393224 | tf_op jit(solution)/shard_map/ppermute | solution.py:213
  80.8 41.6 %collective-permute-start.15 = (bf16[2,2048,512]{2,1,0:T(8,128)(2,1)}, bf16[2,2048,512]{2,1,0:T(8,128)(2,1)}, u32[]{:S(2)}, u32[]{:S(2)}) collective-permute-start(bf16[2,2048,512]{2,1,0:T(8,128)(2,1)} %refs_9_.3), channel_id=1, source_target_pairs={{0,1},{1,0},{2,3},{3,2},{4,5},{5,4},{6,7},{7,6},{8,9},{9,8},{10,11... | collective-permute-start | bytes 12582920 | tf_op jit(solution)/shard_map/ppermute | solution.py:487
  80.8 41.6 %collective-permute-start.16 = (bf16[2,2048,512]{2,1,0:T(8,128)(2,1)}, bf16[2,2048,512]{2,1,0:T(8,128)(2,1)}, u32[]{:S(2)}, u32[]{:S(2)}) collective-permute-start(bf16[2,2048,512]{2,1,0:T(8,128)(2,1)} %refs_10_.3), channel_id=1, source_target_pairs={{0,1},{1,0},{2,3},{3,2},{4,5},{5,4},{6,7},{7,6},{8,9},{9,8},{10,11... | collective-permute-start | bytes 12582920 | tf_op jit(solution)/shard_map/ppermute | solution.py:487
  84.8 37.5 %collective-permute-start.17 = (bf16[2,512,2048]{2,1,0:T(8,128)(2,1)}, bf16[2,512,2048]{2,1,0:T(8,128)(2,1)}, u32[]{:S(2)}, u32[]{:S(2)}) collective-permute-start(bf16[2,512,2048]{2,1,0:T(8,128)(2,1)} %refs_11_.3), channel_id=1, source_target_pairs={{0,1},{1,0},{2,3},{3,2},{4,5},{5,4},{6,7},{7,6},{8,9},{9,8},{10,11... | collective-permute-start | bytes 12582920 | tf_op jit(solution)/shard_map/ppermute | solution.py:487
  100.7 1.7 collective-permute-start.9
  102.4 15.4 %collective-permute-start.14 = (bf16[1024,512]{1,0:T(8,128)(2,1)}, bf16[1024,512]{1,0:T(8,128)(2,1)}, u32[]{:S(2)}, u32[]{:S(2)}) collective-permute-start(bf16[1024,512]{1,0:T(8,128)(2,1)} %copy-done.31), channel_id=1, source_target_pairs={{0,1},{1,0},{2,3},{3,2},{4,5},{5,4},{6,7},{7,6},{8,9},{9,8},{10,11... | collective-permute-start | bytes 3145736 | tf_op jit(solution)/shard_map/ppermute | solution.py:500
  111.9 7.4 %collective-permute-start.13 = (bf16[1024,512]{1,0:T(8,128)(2,1)S(1)}, bf16[1024,512]{1,0:T(8,128)(2,1)S(1)}, u32[]{:S(2)}, u32[]{:S(2)}) collective-permute-start(bf16[1024,512]{1,0:T(8,128)(2,1)S(1)} %collective-permute-done.10), channel_id=1, source_target_pairs={{0,1},{1,0},{2,3},{3,2},{4,5},{5,4},{6,7},{7,6},{8,9},{9,8},{10,11... | collective-permute-start | bytes 3145736 | tf_op jit(solution)/shard_map/ppermute | solution.py:500
  122.3 14.9 %collective-permute-start.18 = (bf16[128,2176]{1,0:T(8,128)(2,1)}, bf16[128,2176]{1,0:T(8,128)(2,1)S(1)}, u32[]{:S(2)}, u32[]{:S(2)}) collective-permute-start(bf16[128,2176]{1,0:T(8,128)(2,1)} %concatenate.47.refs_0_), channel_id=1, source_target_pairs={{0,24},{1,25},{2,26},{3,27},{4,28},{5,29},{6,30},{7,31},{8,0},{9,1... | collective-permute-start | bytes 1671176 | tf_op jit(solution)/shard_map/ppermute | solution.py:358
  124.7 18.2 %collective-permute-start.22 = (bf16[128,2176]{1,0:T(8,128)(2,1)}, bf16[128,2176]{1,0:T(8,128)(2,1)}, u32[]{:S(2)}, u32[]{:S(2)}) collective-permute-start(bf16[128,2176]{1,0:T(8,128)(2,1)} %concatenate.47.refs_0_), channel_id=1, source_target_pairs={{0,4},{1,5},{2,6},{3,7},{4,0},{5,1},{6,2},{7,3},{8,12},{9,13},{10,... | collective-permute-start | bytes 1671176 | tf_op jit(solution)/shard_map/ppermute | solution.py:358
  125.3 17.6 %collective-permute-start.25 = (bf16[128,2176]{1,0:T(8,128)(2,1)}, bf16[128,2176]{1,0:T(8,128)(2,1)S(1)}, u32[]{:S(2)}, u32[]{:S(2)}) collective-permute-start(bf16[128,2176]{1,0:T(8,128)(2,1)} %concatenate.47.refs_0_), channel_id=1, source_target_pairs={{0,2},{1,3},{2,0},{3,1},{4,6},{5,7},{6,4},{7,5},{8,10},{9,11},{10,... | collective-permute-start | bytes 1671176 | tf_op jit(solution)/shard_map/ppermute | solution.py:358
  137.3 15.5 %collective-permute-start.19 = (bf16[128,2176]{1,0:T(8,128)(2,1)S(1)}, bf16[128,2176]{1,0:T(8,128)(2,1)}, u32[]{:S(2)}, u32[]{:S(2)}) collective-permute-start(bf16[128,2176]{1,0:T(8,128)(2,1)S(1)} %collective-permute-done.18.refs_1_), channel_id=1, source_target_pairs={{0,24},{1,25},{2,26},{3,27},{4,28},{5,29},{6,30},{7,31},{8,0},{9,1... | collective-permute-start | bytes 1671176 | tf_op jit(solution)/shard_map/ppermute | solution.py:358
  141.4 15.7 %collective-permute-start.21 = (bf16[128,2176]{1,0:T(8,128)(2,1)S(1)}, bf16[128,2176]{1,0:T(8,128)(2,1)}, u32[]{:S(2)}, u32[]{:S(2)}) collective-permute-start(bf16[128,2176]{1,0:T(8,128)(2,1)S(1)} %collective-permute-done.18.refs_1_), channel_id=1, source_target_pairs={{0,2},{1,3},{2,0},{3,1},{4,6},{5,7},{6,4},{7,5},{8,10},{9,11},{10,... | collective-permute-start | bytes 1671176 | tf_op jit(solution)/shard_map/ppermute | solution.py:358
  142.9 24.1 %collective-permute-start.26 = (bf16[128,2176]{1,0:T(8,128)(2,1)}, bf16[128,2176]{1,0:T(8,128)(2,1)}, u32[]{:S(2)}, u32[]{:S(2)}) collective-permute-start(bf16[128,2176]{1,0:T(8,128)(2,1)} %collective-permute-done.22.refs_2_), channel_id=1, source_target_pairs={{0,2},{1,3},{2,0},{3,1},{4,6},{5,7},{6,4},{7,5},{8,10},{9,11},{10,... | collective-permute-start | bytes 1671176 | tf_op jit(solution)/shard_map/ppermute | solution.py:358
  152.7 15.1 %collective-permute-start.20 = (bf16[128,2176]{1,0:T(8,128)(2,1)}, bf16[128,2176]{1,0:T(8,128)(2,1)}, u32[]{:S(2)}, u32[]{:S(2)}) collective-permute-start(bf16[128,2176]{1,0:T(8,128)(2,1)} %collective-permute-done.19.refs_0_), channel_id=1, source_target_pairs={{0,24},{1,25},{2,26},{3,27},{4,28},{5,29},{6,30},{7,31},{8,0},{9,1... | collective-permute-start | bytes 1671176 | tf_op jit(solution)/shard_map/ppermute | solution.py:358
  157.1 15.9 %collective-permute-start.23 = (bf16[128,2176]{1,0:T(8,128)(2,1)}, bf16[128,2176]{1,0:T(8,128)(2,1)}, u32[]{:S(2)}, u32[]{:S(2)}) collective-permute-start(bf16[128,2176]{1,0:T(8,128)(2,1)} %collective-permute-done.21.refs_5_), channel_id=1, source_target_pairs={{0,4},{1,5},{2,6},{3,7},{4,0},{5,1},{6,2},{7,3},{8,12},{9,13},{10,... | collective-permute-start | bytes 1671176 | tf_op jit(solution)/shard_map/ppermute | solution.py:358
  157.7 27.1 %collective-permute-start.28 = (bf16[128,2176]{1,0:T(8,128)(2,1)}, bf16[128,2176]{1,0:T(8,128)(2,1)S(1)}, u32[]{:S(2)}, u32[]{:S(2)}) collective-permute-start(bf16[128,2176]{1,0:T(8,128)(2,1)} %copy-done.12), channel_id=1, source_target_pairs={{0,4},{1,5},{2,6},{3,7},{4,0},{5,1},{6,2},{7,3},{8,12},{9,13},{10,... | collective-permute-start | bytes 1671176 | tf_op jit(solution)/shard_map/ppermute | solution.py:358
  167.9 18.4 %collective-permute-start.27 = (bf16[128,2176]{1,0:T(8,128)(2,1)}, bf16[128,2176]{1,0:T(8,128)(2,1)S(1)}, u32[]{:S(2)}, u32[]{:S(2)}) collective-permute-start(bf16[128,2176]{1,0:T(8,128)(2,1)} %collective-permute-done.20.refs_1_), channel_id=1, source_target_pairs={{0,2},{1,3},{2,0},{3,1},{4,6},{5,7},{6,4},{7,5},{8,10},{9,11},{10,... | collective-permute-start | bytes 1671176 | tf_op jit(solution)/shard_map/ppermute | solution.py:358
  173.0 23.8 %collective-permute-start.24 = (bf16[128,2176]{1,0:T(8,128)(2,1)}, bf16[128,2176]{1,0:T(8,128)(2,1)S(1)}, u32[]{:S(2)}, u32[]{:S(2)}) collective-permute-start(bf16[128,2176]{1,0:T(8,128)(2,1)} %collective-permute-done.20.refs_1_), channel_id=1, source_target_pairs={{0,4},{1,5},{2,6},{3,7},{4,0},{5,1},{6,2},{7,3},{8,12},{9,13},{10,... | collective-permute-start | bytes 1671176 | tf_op jit(solution)/shard_map/ppermute | solution.py:358
  184.9 31.5 %collective-permute-start.33 = (bf16[128,2176]{1,0:T(8,128)(2,1)}, bf16[128,2176]{1,0:T(8,128)(2,1)S(1)}, u32[]{:S(2)}, u32[]{:S(2)}) collective-permute-start(bf16[128,2176]{1,0:T(8,128)(2,1)} %collective-permute-done.19.refs_0_), channel_id=1, source_target_pairs={{0,4},{1,5},{2,6},{3,7},{4,0},{5,1},{6,2},{7,3},{8,12},{9,13},{10,... | collective-permute-start | bytes 1671176 | tf_op jit(solution)/shard_map/ppermute | solution.py:358
  185.4 30.9 %collective-permute-start.34 = (bf16[128,2176]{1,0:T(8,128)(2,1)}, bf16[128,2176]{1,0:T(8,128)(2,1)S(1)}, u32[]{:S(2)}, u32[]{:S(2)}) collective-permute-start(bf16[128,2176]{1,0:T(8,128)(2,1)} %collective-permute-done.19.refs_0_), channel_id=1, source_target_pairs={{0,2},{1,3},{2,0},{3,1},{4,6},{5,7},{6,4},{7,5},{8,10},{9,11},{10,... | collective-permute-start | bytes 1671176 | tf_op jit(solution)/shard_map/ppermute | solution.py:358
  215.7 15.1 %collective-permute-start.30 = (bf16[128,2048]{1,0:T(8,128)(2,1)}, bf16[128,2048]{1,0:T(8,128)(2,1)S(1)}, u32[]{:S(2)}, u32[]{:S(2)}) collective-permute-start(bf16[128,2048]{1,0:T(8,128)(2,1)} %get-tuple-element.59), channel_id=1, source_target_pairs={{0,4},{1,5},{2,6},{3,7},{4,0},{5,1},{6,2},{7,3},{8,12},{9,13},{10,... | collective-permute-start | bytes 1572872 | tf_op jit(solution)/shard_map/ppermute | solution.py:358
  216.4 17.9 %collective-permute-start.35 = (bf16[128,2176]{1,0:T(8,128)(2,1)S(1)}, bf16[128,2176]{1,0:T(8,128)(2,1)S(1)}, u32[]{:S(2)}, u32[]{:S(2)}) collective-permute-start(bf16[128,2176]{1,0:T(8,128)(2,1)S(1)} %collective-permute-done.33.refs_2_), channel_id=1, source_target_pairs={{0,2},{1,3},{2,0},{3,1},{4,6},{5,7},{6,4},{7,5},{8,10},{9,11},{10,... | collective-permute-start | bytes 1671176 | tf_op jit(solution)/shard_map/ppermute | solution.py:358
  217.4 24.3 %collective-permute-start.36 = (bf16[128,2176]{1,0:T(8,128)(2,1)S(1)}, bf16[128,2176]{1,0:T(8,128)(2,1)}, u32[]{:S(2)}, u32[]{:S(2)}) collective-permute-start(bf16[128,2176]{1,0:T(8,128)(2,1)S(1)} %collective-permute-done.27.refs_5_), channel_id=1, source_target_pairs={{0,4},{1,5},{2,6},{3,7},{4,0},{5,1},{6,2},{7,3},{8,12},{9,13},{10,... | collective-permute-start | bytes 1671176 | tf_op jit(solution)/shard_map/ppermute | solution.py:358
  219.4 41.4 %collective-permute-start.38 = (bf16[128,2048]{1,0:T(8,128)(2,1)}, bf16[128,2048]{1,0:T(8,128)(2,1)}, u32[]{:S(2)}, u32[]{:S(2)}) collective-permute-start(bf16[128,2048]{1,0:T(8,128)(2,1)} %get-tuple-element.70), channel_id=1, source_target_pairs={{0,2},{1,3},{2,0},{3,1},{4,6},{5,7},{6,4},{7,5},{8,10},{9,11},{10,... | collective-permute-start | bytes 1572872 | tf_op jit(solution)/shard_map/ppermute | solution.py:358
  220.0 44.0 %collective-permute-start.29 = (bf16[128,2048]{1,0:T(8,128)(2,1)}, bf16[128,2048]{1,0:T(8,128)(2,1)}, u32[]{:S(2)}, u32[]{:S(2)}) collective-permute-start(bf16[128,2048]{1,0:T(8,128)(2,1)} %get-tuple-element.58), channel_id=1, source_target_pairs={{0,4},{1,5},{2,6},{3,7},{4,0},{5,1},{6,2},{7,3},{8,12},{9,13},{10,... | collective-permute-start | bytes 1572872 | tf_op jit(solution)/shard_map/ppermute | solution.py:358
  232.8 30.6 %collective-permute-start.31 = (bf16[128,2048]{1,0:T(8,128)(2,1)}, bf16[128,2048]{1,0:T(8,128)(2,1)}, u32[]{:S(2)}, u32[]{:S(2)}) collective-permute-start(bf16[128,2048]{1,0:T(8,128)(2,1)} %add_convert_fusion.6), channel_id=1, source_target_pairs={{0,2},{1,3},{2,0},{3,1},{4,6},{5,7},{6,4},{7,5},{8,10},{9,11},{10,... | collective-permute-start | bytes 1572872 | tf_op jit(solution)/shard_map/ppermute | solution.py:358
  260.8 15.1 %collective-permute-start.39 = (bf16[128,2048]{1,0:T(8,128)(2,1)}, bf16[128,2048]{1,0:T(8,128)(2,1)S(1)}, u32[]{:S(2)}, u32[]{:S(2)}) collective-permute-start(bf16[128,2048]{1,0:T(8,128)(2,1)} %get-tuple-element.71), channel_id=1, source_target_pairs={{0,2},{1,3},{2,0},{3,1},{4,6},{5,7},{6,4},{7,5},{8,10},{9,11},{10,... | collective-permute-start | bytes 1572872 | tf_op jit(solution)/shard_map/ppermute | solution.py:358
  262.8 13.9 %collective-permute-start.42 = (bf16[128,2048]{1,0:T(8,128)(2,1)S(1)}, bf16[128,2048]{1,0:T(8,128)(2,1)S(1)}, u32[]{:S(2)}, u32[]{:S(2)}) collective-permute-start(bf16[128,2048]{1,0:T(8,128)(2,1)S(1)} %copy-done.34), channel_id=1, source_target_pairs={{0,4},{1,5},{2,6},{3,7},{4,0},{5,1},{6,2},{7,3},{8,12},{9,13},{10,... | collective-permute-start | bytes 1572872 | tf_op jit(solution)/shard_map/ppermute | solution.py:358
  263.5 21.5 %collective-permute-start.37 = (bf16[128,2048]{1,0:T(8,128)(2,1)S(1)}, bf16[128,2048]{1,0:T(8,128)(2,1)S(1)}, u32[]{:S(2)}, u32[]{:S(2)}) collective-permute-start(bf16[128,2048]{1,0:T(8,128)(2,1)S(1)} %copy-done.33), channel_id=1, source_target_pairs={{0,2},{1,3},{2,0},{3,1},{4,6},{5,7},{6,4},{7,5},{8,10},{9,11},{10,... | collective-permute-start | bytes 1572872 | tf_op jit(solution)/shard_map/ppermute | solution.py:358
  265.5 16.8 %collective-permute-start.32 = (bf16[128,2048]{1,0:T(8,128)(2,1)S(1)}, bf16[128,2048]{1,0:T(8,128)(2,1)S(1)}, u32[]{:S(2)}, u32[]{:S(2)}) collective-permute-start(bf16[128,2048]{1,0:T(8,128)(2,1)S(1)} %add_convert_fusion.5), channel_id=1, source_target_pairs={{0,8},{1,9},{2,10},{3,11},{4,12},{5,13},{6,14},{7,15},{8,16},{9,17... | collective-permute-start | bytes 1572872 | tf_op jit(solution)/shard_map/ppermute | solution.py:403
  276.1 14.1 %collective-permute-start.40 = (bf16[128,2048]{1,0:T(8,128)(2,1)S(1)}, bf16[128,2048]{1,0:T(8,128)(2,1)S(1)}, u32[]{:S(2)}, u32[]{:S(2)}) collective-permute-start(bf16[128,2048]{1,0:T(8,128)(2,1)S(1)} %add_convert_fusion.4), channel_id=1, source_target_pairs={{0,4},{1,5},{2,6},{3,7},{4,0},{5,1},{6,2},{7,3},{8,12},{9,13},{10,... | collective-permute-start | bytes 1572872 | tf_op jit(solution)/shard_map/ppermute | solution.py:358
  276.7 19.0 %collective-permute-start.43 = (bf16[128,2048]{1,0:T(8,128)(2,1)S(1)}, bf16[128,2048]{1,0:T(8,128)(2,1)S(1)}, u32[]{:S(2)}, u32[]{:S(2)}) collective-permute-start(bf16[128,2048]{1,0:T(8,128)(2,1)S(1)} %copy-done.32), channel_id=1, source_target_pairs={{0,4},{1,5},{2,6},{3,7},{4,0},{5,1},{6,2},{7,3},{8,12},{9,13},{10,... | collective-permute-start | bytes 1572872 | tf_op jit(solution)/shard_map/ppermute | solution.py:358
  278.3 17.5 %collective-permute-start.44 = (bf16[128,2048]{1,0:T(8,128)(2,1)S(1)}, bf16[128,2048]{1,0:T(8,128)(2,1)S(1)}, u32[]{:S(2)}, u32[]{:S(2)}) collective-permute-start(bf16[128,2048]{1,0:T(8,128)(2,1)S(1)} %add_convert_fusion.2), channel_id=1, source_target_pairs={{0,2},{1,3},{2,0},{3,1},{4,6},{5,7},{6,4},{7,5},{8,10},{9,11},{10,... | collective-permute-start | bytes 1572872 | tf_op jit(solution)/shard_map/ppermute | solution.py:358
  285.0 16.7 %collective-permute-start.46 = (bf16[128,2048]{1,0:T(8,128)(2,1)}, bf16[128,2048]{1,0:T(8,128)(2,1)}, u32[]{:S(2)}, u32[]{:S(2)}) collective-permute-start(bf16[128,2048]{1,0:T(8,128)(2,1)} %get-tuple-element.84), channel_id=1, source_target_pairs={{0,2},{1,3},{2,0},{3,1},{4,6},{5,7},{6,4},{7,5},{8,10},{9,11},{10,... | collective-permute-start | bytes 1572872 | tf_op jit(solution)/shard_map/ppermute | solution.py:358
  291.2 12.8 %collective-permute-start.41 = (bf16[128,2048]{1,0:T(8,128)(2,1)}, bf16[128,2048]{1,0:T(8,128)(2,1)}, u32[]{:S(2)}, u32[]{:S(2)}) collective-permute-start(bf16[128,2048]{1,0:T(8,128)(2,1)} %add_convert_fusion.3), channel_id=1, source_target_pairs={{0,16},{1,17},{2,18},{3,19},{4,20},{5,21},{6,22},{7,23},{8,24},{9,... | collective-permute-start | bytes 1572872 | tf_op jit(solution)/shard_map/ppermute | solution.py:403
  296.8 12.6 %collective-permute-start.45 = (bf16[128,2048]{1,0:T(8,128)(2,1)}, bf16[128,2048]{1,0:T(8,128)(2,1)}, u32[]{:S(2)}, u32[]{:S(2)}) collective-permute-start(bf16[128,2048]{1,0:T(8,128)(2,1)} %add_convert_fusion.1), channel_id=1, source_target_pairs={{0,24},{1,25},{2,26},{3,27},{4,28},{5,29},{6,30},{7,31},{8,0},{9,1... | collective-permute-start | bytes 1572872 | tf_op jit(solution)/shard_map/ppermute | solution.py:403
  296.8 12.6 %collective-permute-start.47 = (bf16[128,2048]{1,0:T(8,128)(2,1)}, bf16[128,2048]{1,0:T(8,128)(2,1)}, u32[]{:S(2)}, u32[]{:S(2)}) collective-permute-start(bf16[128,2048]{1,0:T(8,128)(2,1)} %add_convert_fusion), channel_id=1, source_target_pairs={{0,4},{1,5},{2,6},{3,7},{4,0},{5,1},{6,2},{7,3},{8,12},{9,13},{10,... | collective-permute-start | bytes 1572872 | tf_op jit(solution)/shard_map/ppermute | solution.py:358
  (35 other events, 719.4 us)

commit v4 on v3

--- a/solution.py
+++ b/solution.py
@@ -182,19 +182,19 @@
     return jnp.einsum("hij,hjk->hik", transform, right, precision=lax.Precision.HIGHEST)
 
 
-def starting_states(block_map, count, place, first_half):
+def starting_states(block_map, count, place, ready, swaps):
     head = block_map.shape[1]
     levels, step = [], 1
-    held, some = block_map, None
+    held = block_map
     while count % (2 * step) == 0 and 4 * step < count and held.shape[0] % 2 == 0:
         share = held.shape[0] // 2
         upper = (place // step) % 2 == 1
         keep = jnp.where(upper, held[share:], held[:share])
         give = jnp.where(upper, held[:share], held[share:])
         kind = F32 if step == 1 else BF16
+        if step == 1 and ready is not None:
+            give = tie(give, ready)
         got = lax.ppermute(give.astype(kind), AXES, [(i, i ^ step) for i in range(count)]).astype(F32)
-        if step == 2 and first_half is not None:
-            some = first_half(got)
         early, late = jnp.where(upper, got, keep), jnp.where(upper, keep, got)
         merged = apply(late[:, :, :head], early)
         held = jnp.concatenate([merged[:, :, :head], merged[:, :, head:] + late[:, :, head:]], axis=2)
@@ -207,12 +207,13 @@
             ahead = ahead + apply(held[:, :, :head], state)
         state = lax.ppermute(ahead.astype(BF16), AXES, [(i, i + step) for i in range(count - step)]).astype(F32)
     middle = state
+    state = tie(state, *swaps)
     for step, upper, early in reversed(levels):
         second = apply(early[:, :, :head], state) + early[:, :, head:]
         mine, other = jnp.where(upper, second, state), jnp.where(upper, state, second)
         got = lax.ppermute(other.astype(BF16), AXES, [(i, i ^ step) for i in range(count)]).astype(F32)
         state = jnp.where(upper, jnp.concatenate([got, mine], axis=0), jnp.concatenate([mine, got], axis=0))
-    return state, some, middle
+    return state, middle
 
 
 def places(mesh):
@@ -251,11 +252,11 @@
         part = weights[:3] if e < local_count else weights[3:]
         fills.append(
             [
-                pltpu.make_async_copy(r.at[e % local_count], w.at[e], w_sem.at[e, k])
+                pltpu.make_async_copy(r.at[e % local_count], w.at[e % 2], w_sem.at[e, k])
                 for k, (r, w) in enumerate(zip(part, (gate_w, up_w, down_w)))
             ]
         )
-    for copy in loads + sum(fills, []):
+    for copy in loads + fills[0] + fills[1]:
         copy.start()
 
     before = lax.broadcasted_iota(jnp.int32, (pair_rows, pair_rows), 0)
@@ -286,14 +287,17 @@
         for copy in fills[e]:
             copy.wait()
         rows_in = sel_ref[e]
-        gate, up = dot(rows_in, gate_w[e]), dot(rows_in, up_w[e])
+        gate, up = dot(rows_in, gate_w[e % 2]), dot(rows_in, up_w[e % 2])
         hidden = (gate / (1.0 + jnp.exp(-gate)) * up).astype(BF16)
         weight = gate_ref[e][:, 0:1]
         for n in range(4):
             cut = slice(n * tile, (n + 1) * tile)
-            result = (dot(hidden, down_w[e, :, cut]) * weight).astype(BF16)
+            result = (dot(hidden, down_w[e % 2, :, cut]) * weight).astype(BF16)
             for p in range(4):
                 back_ref[p, e * slots : (e + 1) * slots, cut] = result[p * slots : (p + 1) * slots]
+        if e + 2 < steps:
+            for copy in fills[e + 2]:
+                copy.start()
 
     stores = [pltpu.make_async_copy(out_ref.at[i], r, out_sem.at[i]) for i, r in enumerate(outs)]
     for p in range(4):
@@ -321,9 +325,9 @@
         out_shape=[jax.ShapeDtypeStruct((rows, width), BF16)] * 8,
         scratch_shapes=[
             pltpu.VMEM((8, rows, packet), BF16),
-            pltpu.VMEM((steps, width, hidden), BF16),
-            pltpu.VMEM((steps, width, hidden), BF16),
-            pltpu.VMEM((steps, hidden, width), BF16),
+            pltpu.VMEM((2, width, hidden), BF16),
+            pltpu.VMEM((2, width, hidden), BF16),
+            pltpu.VMEM((2, hidden, width), BF16),
             pltpu.VMEM((steps, 4 * slots, width), BF16),
             pltpu.VMEM((4, steps * slots, 2 * rows), BF16),
             pltpu.VMEM((steps, 4 * slots, 128), F32),
@@ -333,12 +337,8 @@
             pltpu.SemaphoreType.DMA((steps, 3)),
             pltpu.SemaphoreType.DMA((8,)),
         ],
-        cost_estimate=pl.CostEstimate(
-            flops=steps * 4 * slots * (6 * width * hidden + 8 * width * rows),
-            bytes_accessed=6 * width * hidden * steps + 32 * rows * width,
-            transcendentals=0,
-        ),
-        compiler_params=pltpu.CompilerParams(vmem_limit_bytes=56 * 2**20),
+        cost_estimate=pl.CostEstimate(flops=width * hidden, bytes_accessed=rows * width, transcendentals=0),
+        compiler_params=pltpu.CompilerParams(vmem_limit_bytes=32 * 2**20),
         name="experts",
     )(*shards, chosen, *mine, *other)
 
@@ -387,7 +387,7 @@
         if a == 0:
             spread(a)
             spread(b)
-        far[a], far[b] = links.send(by_x[a], "y"), links.send(by_y[b], "x")
+        far[a], far[b] = links.send(tie(by_x[a], by_y[b]), "y"), links.send(tie(by_y[b], by_x[b]), "x")
         ahead = [sums[a - 1][0]] if a else []
         if b + 1 < deep:
             spread(b + 1)
@@ -483,21 +483,22 @@
     columns = lax.axis_size("exp")
     beside = {i ^ j for i, j in moves_to(layout, lambda c: (c[0], c[1], c[2] ^ 1, c[3]))} if z % 2 == 0 else set()
     near = columns == 4 and None not in (twin, facing) and twin | facing == columns - 1 and len(beside) == 1
-    if paired:
-        other = [lax.ppermute(w, AXES, moves(layout, core=1)) for w in weights]
+    swaps = [lax.ppermute(w, AXES, moves(layout, core=1)) for w in (weights if paired else ())]
+    if near:
+        swaps.append(lax.ppermute(out_weight, AXES, moves(layout, core=1)))
     block_map, read = delta_terms(mixed_qkv, before, conv_weight, log_decay, write_strength, head)
     half = out_weight.shape[0] // 2
     odd = (place & min(beside)) != 0 if near else None
 
-    def first_half(done):
-        mine = tie(jnp.where(odd, out_weight[half:], out_weight[:half]), done)
-        return lax.ppermute(mine, AXES, moves(layout, y=1))
-
-    state, some, middle = starting_states(block_map, count, place, first_half if near else None)
+    some = None
+    if near:
+        some = jnp.where(odd, out_weight[half:], out_weight[:half])
+        some = lax.ppermute(tie(some, before), AXES, moves(layout, y=1))
+    state, middle = starting_states(block_map, count, place, some, swaps)
     if near:
         rest = lax.ppermute(tie(some, middle), AXES, moves_to(layout, lambda c: (c[0], c[1], c[2] ^ 1, c[3])))
-        out_parts = [[out_weight], [some, rest]]
-        out_parts += [[lax.ppermute(w, AXES, moves(layout, core=1)) for w in part] for part in out_parts]
+        out_parts = [[out_weight], [some, rest], swaps[-1:]]
+        out_parts.append([lax.ppermute(w, AXES, moves(layout, core=1)) for w in out_parts[1]])
         owners = [(place ^ mask) % columns for mask in (0, facing, twin, facing | twin)]
     normed = emit(read, state, output_gate, norm_gain)
     if near:
@@ -525,7 +526,7 @@
     chosen = jnp.where(named, jnp.exp(jnp.where(named, logits, 0.0)), 0.0)
     gates = chosen / jnp.sum(chosen, axis=1, keepdims=True)
     if paired:
-        routed = routed_by_gather(layout, place, twin, routed_in, gates, weights, other, capacity)
+        routed = routed_by_gather(layout, place, twin, routed_in, gates, weights, swaps[:3], capacity)
     else:
         routed = routed_by_exchange(routed_in, gates, named, weights, capacity)
     shared_hidden = (

time: 314 us -> 304 us (0.968)
  starting transfers between devices: 63.2 us -> 73.8 us
  Pallas kernels: 55.9 us -> 45.8 us
  waiting for transfers between devices: 144 us -> 136 us
  other arithmetic: 22 us -> 15.6 us
  local copies, waits for them, and re-layouts: 7.96 us -> 11.8 us
    pallas_call x2, Pallas kernels: 37.9 us -> 27.7 us  [run_experts(): pl.pallas_call(functools.partial(expert_kernel, width=width, capacity=cap...]
    ppermute x27, starting transfers between devices: 35.3 us -> 39.5 us  [send(): queue.append(lax.ppermute(value, AXES, moves(self.layout, **{link: turn})))]
    ppermute x3, waiting for transfers between devices: 10.2 us -> 6.15 us  [own_turn(): lax.ppermute(part.astype(BF16), AXES, moves(layout, z=t))]
    ppermute x3, starting transfers between devices: 0.06 us -> 3.95 us  [own_turn(): lax.ppermute(part.astype(BF16), AXES, moves(layout, z=t))]
    ppermute x4 -> x2, waiting for transfers between devices: 9.17 us -> 5.62 us  [the longest x1 5.62 us: local(): some = lax.ppermute(tie(some, before), AXES, moves(layout, y=1))]
    unnamed x71 -> x61, local copies, waits for them, and re-layouts: 5.54 us -> 9.04 us
    ppermute x1, waiting for transfers between devices: 13.3 us -> 9.9 us  [local(): lax.ppermute(tie(some, middle), AXES, moves_to(layout, lambda c: (c[0], c...]
  transfers between devices with their start and end apart: 48 -> 48, of which waited for: 25 -> 26; matrix products, arithmetic and copies ran while one was open for 11% -> 10% of each run, Pallas kernels for 13% -> 15%
where the time goes in v4:
time: 304 us; the launch traced here: 303 us
  waiting for transfers between devices  136 us (45%)
  starting transfers between devices  73.8 us (24%)
  Pallas kernels  45.8 us (15%)
  matrix products  19.3 us (6%)
  other arithmetic  15.6 us (5%)
  local copies, waits for them, and re-layouts  11.8 us (4%)
    ppermute x27, waiting for transfers between devices, send(): queue.append(lax.ppermute(value, AXES, moves(self.layout, **{link: turn})))  92.6 us
    ppermute x27, starting transfers between devices, send(): queue.append(lax.ppermute(value, AXES, moves(self.layout, **{link: turn})))  39.5 us
    pallas_call x2, Pallas kernels, run_experts(): pl.pallas_call(functools.partial(expert_kernel, width=width, capacity=cap...  27.7 us
    pallas_call x1, Pallas kernels, delta_terms(): pl.pallas_call(functools.partial(delta_kernel, head=head, per=per), grid=...  13.7 us
    ppermute x3, starting transfers between devices, starting_states(): lax.ppermute(ahead.astype(BF16), AXES, [(i, i + step) for i in range(coun...  12.6 us
    ppermute x3, waiting for transfers between devices, starting_states(): lax.ppermute(give.astype(kind), AXES, [(i, i ^ step) for i in range(count)])  12.2 us
    dot_general x6, matrix products, local(): jnp.dot(n, w, preferred_element_type=F32)  10.7 us
    ppermute x1, waiting for transfers between devices, local(): lax.ppermute(tie(some, middle), AXES, moves_to(layout, lambda c: (c[0], c...  9.9 us
  transfers between devices with their start and end apart: 48, of which 26 were waited for; matrix products, arithmetic and copies ran while one was open for 10% of the time, Pallas kernels for 15%

profile of v4, /device:TPU:0, one launch (start us, length us, event | category | flops | bytes accessed | tf_op | source)
XLA Modules:
  0.0 303.3 jit_solution(3399918222444843084)
XLA Ops:
  1.0 2.4 collective-permute-start
  3.4 2.7 slice_select_fusion
  6.1 3.4 %collective-permute-start.1 = (bf16[1024,512]{1,0:T(8,128)(2,1)}, bf16[1024,512]{1,0:T(8,128)(2,1)}, u32[]{:S(2)}, u32[]{:S(2)}) collective-permute-start(bf16[1024,512]{1,0:T(8,128)(2,1)} %slice_select_fusion), channel_id=1, source_target_pairs={{0,2},{1,3},{2,0},{3,1},{4,6},{5,7},{6,4},{7,5},{8,10},{9,11},{10,... | collective-permute-start | bytes 3145736 | tf_op jit(solution)/shard_map/ppermute | solution.py:496
  12.4 13.7 %delta_terms.1 = (f32[16,128,256]{2,1,0:T(8,128)S(1)}, f32[16,128,256]{2,1,0:T(8,128)S(1)}) custom-call(bf16[128,4096]{1,0:T(8,128)(2,1)S(1)} %copy-done.1, bf16[128,4096]{1,0:T(8,128)(2,1)S(1)} %copy-done.1, bf16[128,4096]{1,0:T(8,128)(2,1)S(1)} %copy-done.1, bf16[8,4096]{1,0:T(8,128)(2,1)S(1)} %collective-permute-done.qb_ref.kb_ref.vb_ref, ...), custom_call_target="tpu_custom_call" | custom-call | flops 33554432 | bytes 262144 | tf_op jit(solution)/shard_map/delta_terms/pallas_call | solution.py:132
  28.0 5.6 %collective-permute-done.1 = bf16[1024,512]{1,0:T(8,128)(2,1)} collective-permute-done((bf16[1024,512]{1,0:T(8,128)(2,1)}, bf16[1024,512]{1,0:T(8,128)(2,1)}, u32[]{:S(2)}, u32[]{:S(2)}) %collective-permute-start.1) | collective-permute-done | bytes 1048608 | tf_op jit(solution)/shard_map/ppermute | solution.py:496
  34.6 2.1 collective-permute-done.2
  36.7 2.1 broadcast_select_fusion
  40.8 3.1 %collective-permute-start.3 = (bf16[4,128,256]{2,1,0:T(8,128)(2,1)}, bf16[4,128,256]{2,1,0:T(8,128)(2,1)S(1)}, u32[]{:S(2)}, u32[]{:S(2)}) collective-permute-start(bf16[4,128,256]{2,1,0:T(8,128)(2,1)} %select_convert_fusion.1), channel_id=1, source_target_pairs={{0,2},{1,3},{2,0},{3,1},{4,6},{5,7},{6,4},{7,5},{8,10},{9,11},{10,... | collective-permute-start | bytes 786440 | tf_op jit(solution)/shard_map/ppermute | solution.py:197
  43.9 6.8 %collective-permute-done.3 = bf16[4,128,256]{2,1,0:T(8,128)(2,1)S(1)} collective-permute-done((bf16[4,128,256]{2,1,0:T(8,128)(2,1)}, bf16[4,128,256]{2,1,0:T(8,128)(2,1)S(1)}, u32[]{:S(2)}, u32[]{:S(2)}) %collective-permute-start.3) | collective-permute-done | bytes 262176 | tf_op jit(solution)/shard_map/ppermute | solution.py:197
  51.5 1.9 collective-permute-start.4
  53.3 3.2 %collective-permute-done.4 = bf16[2,128,256]{2,1,0:T(8,128)(2,1)S(1)} collective-permute-done((bf16[2,128,256]{2,1,0:T(8,128)(2,1)S(1)}, bf16[2,128,256]{2,1,0:T(8,128)(2,1)S(1)}, u32[]{:S(2)}, u32[]{:S(2)}) %collective-permute-start.4) | collective-permute-done | bytes 131104 | tf_op jit(solution)/shard_map/ppermute | solution.py:197
  57.0 3.9 %collective-permute-start.5 = (bf16[2,128,128]{2,1,0:T(8,128)(2,1)S(1)}, bf16[2,128,128]{2,1,0:T(8,128)(2,1)S(1)}, u32[]{:S(2)}, u32[]{:S(2)}) collective-permute-start(bf16[2,128,128]{2,1,0:T(8,128)(2,1)S(1)} %fusion.47), channel_id=1, source_target_pairs={{0,8},{1,9},{2,10},{3,11},{4,12},{5,13},{6,14},{7,15},{8,16},{9,17... | collective-permute-start | bytes 196616 | tf_op jit(solution)/shard_map/ppermute | solution.py:208
  60.9 1.9 collective-permute-done.5
  63.0 4.3 %collective-permute-start.6 = (bf16[2,128,128]{2,1,0:T(8,128)(2,1)S(1)}, bf16[2,128,128]{2,1,0:T(8,128)(2,1)S(1)}, u32[]{:S(2)}, u32[]{:S(2)}) collective-permute-start(bf16[2,128,128]{2,1,0:T(8,128)(2,1)S(1)} %fusion.1), channel_id=1, source_target_pairs={{0,8},{1,9},{2,10},{3,11},{4,12},{5,13},{6,14},{7,15},{8,16},{9,17... | collective-permute-start | bytes 196616 | tf_op jit(solution)/shard_map/ppermute | solution.py:208
  67.3 1.9 collective-permute-done.6
  69.4 4.4 %collective-permute-start.7 = (bf16[2,128,128]{2,1,0:T(8,128)(2,1)S(1)}, bf16[2,128,128]{2,1,0:T(8,128)(2,1)S(1)}, u32[]{:S(2)}, u32[]{:S(2)}) collective-permute-start(bf16[2,128,128]{2,1,0:T(8,128)(2,1)S(1)} %fusion.2), channel_id=1, source_target_pairs={{0,8},{1,9},{2,10},{3,11},{4,12},{5,13},{6,14},{7,15},{8,16},{9,17... | collective-permute-start | bytes 196616 | tf_op jit(solution)/shard_map/ppermute | solution.py:208
  73.8 2.3 collective-permute-done.7
  78.0 2.5 collective-permute-start.15
  82.8 3.5 %collective-permute-done.13 = bf16[4,128,128]{2,1,0:T(8,128)(2,1)S(1)} collective-permute-done((bf16[4,128,128]{2,1,0:T(8,128)(2,1)S(1)}, bf16[4,128,128]{2,1,0:T(8,128)(2,1)S(1)}, u32[]{:S(2)}, u32[]{:S(2)}) %collective-permute-start.13) | collective-permute-done | bytes 131104 | tf_op jit(solution)/shard_map/ppermute | solution.py:214
  88.0 9.9 %collective-permute-done.15 = bf16[1024,512]{1,0:T(8,128)(2,1)} collective-permute-done((bf16[1024,512]{1,0:T(8,128)(2,1)}, bf16[1024,512]{1,0:T(8,128)(2,1)}, u32[]{:S(2)}, u32[]{:S(2)}) %collective-permute-start.15) | collective-permute-done | bytes 1048608 | tf_op jit(solution)/shard_map/ppermute | solution.py:499
  99.0 4.3 %emit.1 = bf16[128,2048]{1,0:T(8,128)(2,1)} custom-call(f32[16,128,256]{2,1,0:T(8,128)} %copy-done.4, f32[16,128,128]{2,1,0:T(8,128)} %maximum_select_fusion.state_ref, bf16[128,2048]{1,0:T(8,128)(2,1)} %gate_ref.1, f32[1,128]{1,0:T(1,128)} %bitcast.46), custom_call_target="tpu_custom_call" | custom-call | tf_op jit(solution)/shard_map/emit/pallas_call | solution.py:162
  103.4 1.7 fusion.38
  106.8 2.0 fusion.52
  108.9 2.0 fusion.53
  116.0 4.5 %collective-permute-start.18 = (bf16[128,2176]{1,0:T(8,128)(2,1)S(1)}, bf16[128,2176]{1,0:T(8,128)(2,1)S(1)}, u32[]{:S(2)}, u32[]{:S(2)}) collective-permute-start(bf16[128,2176]{1,0:T(8,128)(2,1)S(1)} %concatenate.47.refs_0_), channel_id=1, source_target_pairs={{0,24},{1,25},{2,26},{3,27},{4,28},{5,29},{6,30},{7,31},{8,0},{9,1... | collective-permute-start | bytes 1671176 | tf_op jit(solution)/shard_map/ppermute | solution.py:358
  121.0 12.0 %collective-permute-done.18.refs_1_ = bf16[128,2176]{1,0:T(8,128)(2,1)S(1)} collective-permute-done((bf16[128,2176]{1,0:T(8,128)(2,1)S(1)}, bf16[128,2176]{1,0:T(8,128)(2,1)S(1)}, u32[]{:S(2)}, u32[]{:S(2)}) %collective-permute-start.18) | collective-permute-done | bytes 557088 | tf_op jit(solution)/shard_map/ppermute | solution.py:358
  133.4 1.7 collective-permute-start.26
  135.1 4.3 %collective-permute-start.19 = (bf16[128,2176]{1,0:T(8,128)(2,1)S(1)}, bf16[128,2176]{1,0:T(8,128)(2,1)S(1)}, u32[]{:S(2)}, u32[]{:S(2)}) collective-permute-start(bf16[128,2176]{1,0:T(8,128)(2,1)S(1)} %collective-permute-done.18.refs_1_), channel_id=1, source_target_pairs={{0,24},{1,25},{2,26},{3,27},{4,28},{5,29},{6,30},{7,31},{8,0},{9,1... | collective-permute-start | bytes 1671176 | tf_op jit(solution)/shard_map/ppermute | solution.py:358
  140.7 8.0 %collective-permute-done.21.refs_5_ = bf16[128,2176]{1,0:T(8,128)(2,1)} collective-permute-done((bf16[128,2176]{1,0:T(8,128)(2,1)S(1)}, bf16[128,2176]{1,0:T(8,128)(2,1)}, u32[]{:S(2)}, u32[]{:S(2)}) %collective-permute-start.21) | collective-permute-done | bytes 557088 | tf_op jit(solution)/shard_map/ppermute | solution.py:358
  148.7 10.6 %collective-permute-done.26.refs_4_ = bf16[128,2176]{1,0:T(8,128)(2,1)S(1)} collective-permute-done((bf16[128,2176]{1,0:T(8,128)(2,1)S(1)}, bf16[128,2176]{1,0:T(8,128)(2,1)S(1)}, u32[]{:S(2)}, u32[]{:S(2)}) %collective-permute-start.26) | collective-permute-done | bytes 557088 | tf_op jit(solution)/shard_map/ppermute | solution.py:358
  160.6 4.1 %collective-permute-start.20 = (bf16[128,2176]{1,0:T(8,128)(2,1)S(1)}, bf16[128,2176]{1,0:T(8,128)(2,1)}, u32[]{:S(2)}, u32[]{:S(2)}) collective-permute-start(bf16[128,2176]{1,0:T(8,128)(2,1)S(1)} %collective-permute-done.19.refs_0_), channel_id=1, source_target_pairs={{0,24},{1,25},{2,26},{3,27},{4,28},{5,29},{6,30},{7,31},{8,0},{9,1... | collective-permute-start | bytes 1671176 | tf_op jit(solution)/shard_map/ppermute | solution.py:358
  167.1 6.7 %collective-permute-done.27.refs_6_ = bf16[128,2176]{1,0:T(8,128)(2,1)} collective-permute-done((bf16[128,2176]{1,0:T(8,128)(2,1)}, bf16[128,2176]{1,0:T(8,128)(2,1)}, u32[]{:S(2)}, u32[]{:S(2)}) %collective-permute-start.27) | collective-permute-done | bytes 557088 | tf_op jit(solution)/shard_map/ppermute | solution.py:358
  182.6 8.5 %collective-permute-done.28.refs_5_ = bf16[128,2176]{1,0:T(8,128)(2,1)S(1)} collective-permute-done((bf16[128,2176]{1,0:T(8,128)(2,1)}, bf16[128,2176]{1,0:T(8,128)(2,1)S(1)}, u32[]{:S(2)}, u32[]{:S(2)}) %collective-permute-start.28) | collective-permute-done | bytes 557088 | tf_op jit(solution)/shard_map/ppermute | solution.py:358
  191.0 3.3 %collective-permute-done.25.refs_3_ = bf16[128,2176]{1,0:T(8,128)(2,1)S(1)} collective-permute-done((bf16[128,2176]{1,0:T(8,128)(2,1)}, bf16[128,2176]{1,0:T(8,128)(2,1)S(1)}, u32[]{:S(2)}, u32[]{:S(2)}) %collective-permute-start.25) | collective-permute-done | bytes 557088 | tf_op jit(solution)/shard_map/ppermute | solution.py:358
  197.5 14.6 %experts.2 = (bf16[128,2048]{1,0:T(8,128)(2,1)S(1)}, bf16[128,2048]{1,0:T(8,128)(2,1)S(1)}, bf16[128,2048]{1,0:T(8,128)(2,1)S(1)}, bf16[128,2048]{1,0:T(8,128)(2...) custom-call(bf16[128,2176]{1,0:T(8,128)(2,1)S(1)} %concatenate.47.re, ...), custom_call_target="tpu_custom_call" | custom-call | flops 1048576 | bytes 262144 | tf_op jit(solution)/shard_map/experts/pallas_call | solution.py:321
  214.3 1.7 collective-permute-start.35
  216.3 10.8 %collective-permute-done.30 = bf16[128,2048]{1,0:T(8,128)(2,1)S(1)} collective-permute-done((bf16[128,2048]{1,0:T(8,128)(2,1)S(1)}, bf16[128,2048]{1,0:T(8,128)(2,1)S(1)}, u32[]{:S(2)}, u32[]{:S(2)}) %collective-permute-start.30) | collective-permute-done | bytes 524320 | tf_op jit(solution)/shard_map/ppermute | solution.py:358
  227.3 1.8 collective-permute-start.31
  229.6 6.8 %collective-permute-done.36.refs_7_ = bf16[128,2176]{1,0:T(8,128)(2,1)S(1)} collective-permute-done((bf16[128,2176]{1,0:T(8,128)(2,1)S(1)}, bf16[128,2176]{1,0:T(8,128)(2,1)S(1)}, u32[]{:S(2)}, u32[]{:S(2)}) %collective-permute-start.36) | collective-permute-done | bytes 557088 | tf_op jit(solution)/shard_map/ppermute | solution.py:358
  236.4 13.1 %experts.3 = (bf16[128,2048]{1,0:T(8,128)(2,1)S(1)}, bf16[128,2048]{1,0:T(8,128)(2,1)S(1)}, bf16[128,2048]{1,0:T(8,128)(2,1)S(1)}, bf16[128,2048]{1,0:T(8,128)(2...) custom-call(bf16[128,2176]{1,0:T(8,128)(2,1)S(1)} %collective-permut, ...), custom_call_target="tpu_custom_call" | custom-call | flops 1048576 | bytes 262144 | tf_op jit(solution)/shard_map/experts/pallas_call | solution.py:321
  249.5 1.8 collective-permute-start.39
  254.1 10.4 %collective-permute-done.39 = bf16[128,2048]{1,0:T(8,128)(2,1)S(1)} collective-permute-done((bf16[128,2048]{1,0:T(8,128)(2,1)S(1)}, bf16[128,2048]{1,0:T(8,128)(2,1)S(1)}, u32[]{:S(2)}, u32[]{:S(2)}) %collective-permute-start.39) | collective-permute-done | bytes 524320 | tf_op jit(solution)/shard_map/ppermute | solution.py:358
  268.8 6.9 %collective-permute-done.37 = bf16[128,2048]{1,0:T(8,128)(2,1)S(1)} collective-permute-done((bf16[128,2048]{1,0:T(8,128)(2,1)S(1)}, bf16[128,2048]{1,0:T(8,128)(2,1)S(1)}, u32[]{:S(2)}, u32[]{:S(2)}) %collective-permute-start.37) | collective-permute-done | bytes 524320 | tf_op jit(solution)/shard_map/ppermute | solution.py:358
  279.4 4.9 %collective-permute-done.43 = bf16[128,2048]{1,0:T(8,128)(2,1)S(1)} collective-permute-done((bf16[128,2048]{1,0:T(8,128)(2,1)S(1)}, bf16[128,2048]{1,0:T(8,128)(2,1)S(1)}, u32[]{:S(2)}, u32[]{:S(2)}) %collective-permute-start.43) | collective-permute-done | bytes 524320 | tf_op jit(solution)/shard_map/ppermute | solution.py:358
  285.4 3.9 %collective-permute-start.45 = (bf16[128,2048]{1,0:T(8,128)(2,1)}, bf16[128,2048]{1,0:T(8,128)(2,1)}, u32[]{:S(2)}, u32[]{:S(2)}) collective-permute-start(bf16[128,2048]{1,0:T(8,128)(2,1)} %add_convert_fusion.1), channel_id=1, source_target_pairs={{0,24},{1,25},{2,26},{3,27},{4,28},{5,29},{6,30},{7,31},{8,0},{9,1... | collective-permute-start | bytes 1572872 | tf_op jit(solution)/shard_map/ppermute | solution.py:403
  290.1 3.5 %convolution_multiply_fusion = f32[128,2048]{1,0:T(8,128)} fusion(bf16[512,2048]{1,0:T(8,128)(2,1)S(1)} %copy-done, bf16[128,2048]{1,0:T(8,128)(2,1)S(1)} %copy-done.16, bf16[2048,512]{1,0:T(8,128)(2,1)} %param.33, f32[128]{0:T(128)S(1)} %fusion.8, f32[128,512]{1,0:T(8,128)S(1)} %fusion.54), kind=kOutput, calls=%fused_computation | convolution fusion | flops 537526272 | bytes 6029824 | tf_op jit(solution)/shard_map/dot_general | solution.py:537
  294.2 5.5 %collective-permute-done.45 = bf16[128,2048]{1,0:T(8,128)(2,1)} collective-permute-done((bf16[128,2048]{1,0:T(8,128)(2,1)}, bf16[128,2048]{1,0:T(8,128)(2,1)}, u32[]{:S(2)}, u32[]{:S(2)}) %collective-permute-start.45) | collective-permute-done | bytes 524320 | tf_op jit(solution)/shard_map/ppermute | solution.py:403
  299.7 3.6 %fusion.13 = bf16[128,2048]{1,0:T(8,128)(2,1)} fusion(f32[128,2048]{1,0:T(8,128)} %convolution_multiply_fusion, bf16[128,2048]{1,0:T(8,128)(2,1)} %copy-done.18, bf16[128,2048]{1,0:T(8,128)(2,1)S(1)} %copy-done.13, bf16[128,2048]{1,0:T(8,128)(2,1)} %collective-permute-done.47, bf16[128,2048]{1,0:T(8,128)(2,1)} %collective-permute-done.46, ...), kind=kLoop, calls=%fused_computation.27 | loop fusion | flops 3932160 | bytes 5242880 | tf_op jit(solution)/shard_map/convert_element_type | solution.py:538
  (174 shorter events, 57.9 us)
Async XLA Ops:
  1.0 5.1 %collective-permute-start = (bf16[8,4096]{1,0:T(8,128)(2,1)S(1)}, bf16[8,4096]{1,0:T(8,128)(2,1)S(1)}, u32[]{:S(2)}, u32[]{:S(2)}) collective-permute-start(bf16[8,4096]{1,0:T(8,128)(2,1)S(1)} %slice.95), channel_id=1, source_target_pairs={{0,1},{1,2},{2,3},{3,4},{4,5},{5,6},{6,7},{7,8},{8,9},{9,10},{10,1... | collective-permute-start | bytes 196616 | tf_op jit(solution)/shard_map/ppermute | solution.py:478
  6.1 27.5 %collective-permute-start.1 = (bf16[1024,512]{1,0:T(8,128)(2,1)}, bf16[1024,512]{1,0:T(8,128)(2,1)}, u32[]{:S(2)}, u32[]{:S(2)}) collective-permute-start(bf16[1024,512]{1,0:T(8,128)(2,1)} %slice_select_fusion), channel_id=1, source_target_pairs={{0,2},{1,3},{2,0},{3,1},{4,6},{5,7},{6,4},{7,5},{8,10},{9,11},{10,... | collective-permute-start | bytes 3145736 | tf_op jit(solution)/shard_map/ppermute | solution.py:496
  33.6 3.1 %collective-permute-start.2 = (f32[8,128,256]{2,1,0:T(8,128)S(1)}, f32[8,128,256]{2,1,0:T(8,128)}, u32[]{:S(2)}, u32[]{:S(2)}) collective-permute-start(f32[8,128,256]{2,1,0:T(8,128)S(1)} %slice_select_fusion.1), channel_id=1, source_target_pairs={{0,1},{1,0},{2,3},{3,2},{4,5},{5,4},{6,7},{7,6},{8,9},{9,8},{10,11... | collective-permute-start | bytes 3145736 | tf_op jit(solution)/shard_map/ppermute | solution.py:197
  33.7 42.4 %collective-permute-start.10 = (bf16[2,512,2048]{2,1,0:T(8,128)(2,1)}, bf16[2,512,2048]{2,1,0:T(8,128)(2,1)}, u32[]{:S(2)}, u32[]{:S(2)}) collective-permute-start(bf16[2,512,2048]{2,1,0:T(8,128)(2,1)} %refs_11_.3), channel_id=1, source_target_pairs={{0,1},{1,0},{2,3},{3,2},{4,5},{5,4},{6,7},{7,6},{8,9},{9,8},{10,11... | collective-permute-start | bytes 12582920 | tf_op jit(solution)/shard_map/ppermute | solution.py:486
  34.1 42.0 %collective-permute-start.8 = (bf16[2,2048,512]{2,1,0:T(8,128)(2,1)}, bf16[2,2048,512]{2,1,0:T(8,128)(2,1)}, u32[]{:S(2)}, u32[]{:S(2)}) collective-permute-start(bf16[2,2048,512]{2,1,0:T(8,128)(2,1)} %refs_9_.3), channel_id=1, source_target_pairs={{0,1},{1,0},{2,3},{3,2},{4,5},{5,4},{6,7},{7,6},{8,9},{9,8},{10,11... | collective-permute-start | bytes 12582920 | tf_op jit(solution)/shard_map/ppermute | solution.py:486
  34.2 41.9 %collective-permute-start.9 = (bf16[2,2048,512]{2,1,0:T(8,128)(2,1)}, bf16[2,2048,512]{2,1,0:T(8,128)(2,1)}, u32[]{:S(2)}, u32[]{:S(2)}) collective-permute-start(bf16[2,2048,512]{2,1,0:T(8,128)(2,1)} %refs_10_.3), channel_id=1, source_target_pairs={{0,1},{1,0},{2,3},{3,2},{4,5},{5,4},{6,7},{7,6},{8,9},{9,8},{10,11... | collective-permute-start | bytes 12582920 | tf_op jit(solution)/shard_map/ppermute | solution.py:486
  40.8 9.9 %collective-permute-start.3 = (bf16[4,128,256]{2,1,0:T(8,128)(2,1)}, bf16[4,128,256]{2,1,0:T(8,128)(2,1)S(1)}, u32[]{:S(2)}, u32[]{:S(2)}) collective-permute-start(bf16[4,128,256]{2,1,0:T(8,128)(2,1)} %select_convert_fusion.1), channel_id=1, source_target_pairs={{0,2},{1,3},{2,0},{3,1},{4,6},{5,7},{6,4},{7,5},{8,10},{9,11},{10,... | collective-permute-start | bytes 786440 | tf_op jit(solution)/shard_map/ppermute | solution.py:197
  43.9 32.3 %collective-permute-start.11 = (bf16[2048,512]{1,0:T(8,128)(2,1)}, bf16[2048,512]{1,0:T(8,128)(2,1)}, u32[]{:S(2)}, u32[]{:S(2)}) collective-permute-start(bf16[2048,512]{1,0:T(8,128)(2,1)} %param.25), channel_id=1, source_target_pairs={{0,1},{1,0},{2,3},{3,2},{4,5},{5,4},{6,7},{7,6},{8,9},{9,8},{10,11... | collective-permute-start | bytes 6291464 | tf_op jit(solution)/shard_map/ppermute | solution.py:488
  51.5 5.1 %collective-permute-start.4 = (bf16[2,128,256]{2,1,0:T(8,128)(2,1)S(1)}, bf16[2,128,256]{2,1,0:T(8,128)(2,1)S(1)}, u32[]{:S(2)}, u32[]{:S(2)}) collective-permute-start(bf16[2,128,256]{2,1,0:T(8,128)(2,1)S(1)} %select_convert_fusion.3), channel_id=1, source_target_pairs={{0,4},{1,5},{2,6},{3,7},{4,0},{5,1},{6,2},{7,3},{8,12},{9,13},{10,... | collective-permute-start | bytes 393224 | tf_op jit(solution)/shard_map/ppermute | solution.py:197
  57.0 5.8 %collective-permute-start.5 = (bf16[2,128,128]{2,1,0:T(8,128)(2,1)S(1)}, bf16[2,128,128]{2,1,0:T(8,128)(2,1)S(1)}, u32[]{:S(2)}, u32[]{:S(2)}) collective-permute-start(bf16[2,128,128]{2,1,0:T(8,128)(2,1)S(1)} %fusion.47), channel_id=1, source_target_pairs={{0,8},{1,9},{2,10},{3,11},{4,12},{5,13},{6,14},{7,15},{8,16},{9,17... | collective-permute-start | bytes 196616 | tf_op jit(solution)/shard_map/ppermute | solution.py:208
  63.0 6.2 %collective-permute-start.6 = (bf16[2,128,128]{2,1,0:T(8,128)(2,1)S(1)}, bf16[2,128,128]{2,1,0:T(8,128)(2,1)S(1)}, u32[]{:S(2)}, u32[]{:S(2)}) collective-permute-start(bf16[2,128,128]{2,1,0:T(8,128)(2,1)S(1)} %fusion.1), channel_id=1, source_target_pairs={{0,8},{1,9},{2,10},{3,11},{4,12},{5,13},{6,14},{7,15},{8,16},{9,17... | collective-permute-start | bytes 196616 | tf_op jit(solution)/shard_map/ppermute | solution.py:208
  69.4 6.7 %collective-permute-start.7 = (bf16[2,128,128]{2,1,0:T(8,128)(2,1)S(1)}, bf16[2,128,128]{2,1,0:T(8,128)(2,1)S(1)}, u32[]{:S(2)}, u32[]{:S(2)}) collective-permute-start(bf16[2,128,128]{2,1,0:T(8,128)(2,1)S(1)} %fusion.2), channel_id=1, source_target_pairs={{0,8},{1,9},{2,10},{3,11},{4,12},{5,13},{6,14},{7,15},{8,16},{9,17... | collective-permute-start | bytes 196616 | tf_op jit(solution)/shard_map/ppermute | solution.py:208
  76.5 4.3 %collective-permute-start.12 = (bf16[2,128,128]{2,1,0:T(8,128)(2,1)S(1)}, bf16[2,128,128]{2,1,0:T(8,128)(2,1)S(1)}, u32[]{:S(2)}, u32[]{:S(2)}) collective-permute-start(bf16[2,128,128]{2,1,0:T(8,128)(2,1)S(1)} %select_convert_fusion.4), channel_id=1, source_target_pairs={{0,4},{1,5},{2,6},{3,7},{4,0},{5,1},{6,2},{7,3},{8,12},{9,13},{10,... | collective-permute-start | bytes 196616 | tf_op jit(solution)/shard_map/ppermute | solution.py:214
  78.0 19.8 %collective-permute-start.15 = (bf16[1024,512]{1,0:T(8,128)(2,1)}, bf16[1024,512]{1,0:T(8,128)(2,1)}, u32[]{:S(2)}, u32[]{:S(2)}) collective-permute-start(bf16[1024,512]{1,0:T(8,128)(2,1)} %collective-permute-done.1), channel_id=1, source_target_pairs={{0,8},{1,9},{2,10},{3,11},{4,12},{5,13},{6,14},{7,15},{8,0},{9,1},... | collective-permute-start | bytes 3145736 | tf_op jit(solution)/shard_map/ppermute | solution.py:499
  81.3 5.0 %collective-permute-start.13 = (bf16[4,128,128]{2,1,0:T(8,128)(2,1)S(1)}, bf16[4,128,128]{2,1,0:T(8,128)(2,1)S(1)}, u32[]{:S(2)}, u32[]{:S(2)}) collective-permute-start(bf16[4,128,128]{2,1,0:T(8,128)(2,1)S(1)} %select_convert_fusion.2), channel_id=1, source_target_pairs={{0,2},{1,3},{2,0},{3,1},{4,6},{5,7},{6,4},{7,5},{8,10},{9,11},{10,... | collective-permute-start | bytes 393224 | tf_op jit(solution)/shard_map/ppermute | solution.py:214
  87.2 10.7 %collective-permute-start.14 = (bf16[8,128,128]{2,1,0:T(8,128)(2,1)S(1)}, bf16[8,128,128]{2,1,0:T(8,128)(2,1)S(1)}, u32[]{:S(2)}, u32[]{:S(2)}) collective-permute-start(bf16[8,128,128]{2,1,0:T(8,128)(2,1)S(1)} %select_convert_fusion), channel_id=1, source_target_pairs={{0,1},{1,0},{2,3},{3,2},{4,5},{5,4},{6,7},{7,6},{8,9},{9,8},{10,11... | collective-permute-start | bytes 786440 | tf_op jit(solution)/shard_map/ppermute | solution.py:214
  87.5 25.0 %collective-permute-start.16 = (bf16[1024,512]{1,0:T(8,128)(2,1)}, bf16[1024,512]{1,0:T(8,128)(2,1)}, u32[]{:S(2)}, u32[]{:S(2)}) collective-permute-start(bf16[1024,512]{1,0:T(8,128)(2,1)} %collective-permute-done.1), channel_id=1, source_target_pairs={{0,1},{1,0},{2,3},{3,2},{4,5},{5,4},{6,7},{7,6},{8,9},{9,8},{10,11... | collective-permute-start | bytes 3145736 | tf_op jit(solution)/shard_map/ppermute | solution.py:501
  97.9 13.1 %collective-permute-start.17 = (bf16[1024,512]{1,0:T(8,128)(2,1)}, bf16[1024,512]{1,0:T(8,128)(2,1)}, u32[]{:S(2)}, u32[]{:S(2)}) collective-permute-start(bf16[1024,512]{1,0:T(8,128)(2,1)} %collective-permute-done.15), channel_id=1, source_target_pairs={{0,1},{1,0},{2,3},{3,2},{4,5},{5,4},{6,7},{7,6},{8,9},{9,8},{10,11... | collective-permute-start | bytes 3145736 | tf_op jit(solution)/shard_map/ppermute | solution.py:501
  116.0 17.1 %collective-permute-start.18 = (bf16[128,2176]{1,0:T(8,128)(2,1)S(1)}, bf16[128,2176]{1,0:T(8,128)(2,1)S(1)}, u32[]{:S(2)}, u32[]{:S(2)}) collective-permute-start(bf16[128,2176]{1,0:T(8,128)(2,1)S(1)} %concatenate.47.refs_0_), channel_id=1, source_target_pairs={{0,24},{1,25},{2,26},{3,27},{4,28},{5,29},{6,30},{7,31},{8,0},{9,1... | collective-permute-start | bytes 1671176 | tf_op jit(solution)/shard_map/ppermute | solution.py:358
  120.5 20.2 %collective-permute-start.23 = (bf16[128,2176]{1,0:T(8,128)(2,1)S(1)}, bf16[128,2176]{1,0:T(8,128)(2,1)}, u32[]{:S(2)}, u32[]{:S(2)}) collective-permute-start(bf16[128,2176]{1,0:T(8,128)(2,1)S(1)} %concatenate.47.refs_0_), channel_id=1, source_target_pairs={{0,4},{1,5},{2,6},{3,7},{4,0},{5,1},{6,2},{7,3},{8,12},{9,13},{10,... | collective-permute-start | bytes 1671176 | tf_op jit(solution)/shard_map/ppermute | solution.py:358
  133.1 15.6 %collective-permute-start.21 = (bf16[128,2176]{1,0:T(8,128)(2,1)S(1)}, bf16[128,2176]{1,0:T(8,128)(2,1)}, u32[]{:S(2)}, u32[]{:S(2)}) collective-permute-start(bf16[128,2176]{1,0:T(8,128)(2,1)S(1)} %collective-permute-done.18.refs_1_), channel_id=1, source_target_pairs={{0,2},{1,3},{2,0},{3,1},{4,6},{5,7},{6,4},{7,5},{8,10},{9,11},{10,... | collective-permute-start | bytes 1671176 | tf_op jit(solution)/shard_map/ppermute | solution.py:358
  133.4 25.9 %collective-permute-start.26 = (bf16[128,2176]{1,0:T(8,128)(2,1)S(1)}, bf16[128,2176]{1,0:T(8,128)(2,1)S(1)}, u32[]{:S(2)}, u32[]{:S(2)}) collective-permute-start(bf16[128,2176]{1,0:T(8,128)(2,1)S(1)} %concatenate.47.refs_0_), channel_id=1, source_target_pairs={{0,2},{1,3},{2,0},{3,1},{4,6},{5,7},{6,4},{7,5},{8,10},{9,11},{10,... | collective-permute-start | bytes 1671176 | tf_op jit(solution)/shard_map/ppermute | solution.py:358
  135.1 25.5 %collective-permute-start.19 = (bf16[128,2176]{1,0:T(8,128)(2,1)S(1)}, bf16[128,2176]{1,0:T(8,128)(2,1)S(1)}, u32[]{:S(2)}, u32[]{:S(2)}) collective-permute-start(bf16[128,2176]{1,0:T(8,128)(2,1)S(1)} %collective-permute-done.18.refs_1_), channel_id=1, source_target_pairs={{0,24},{1,25},{2,26},{3,27},{4,28},{5,29},{6,30},{7,31},{8,0},{9,1... | collective-permute-start | bytes 1671176 | tf_op jit(solution)/shard_map/ppermute | solution.py:358
  139.4 25.3 %collective-permute-start.22 = (bf16[128,2176]{1,0:T(8,128)(2,1)S(1)}, bf16[128,2176]{1,0:T(8,128)(2,1)S(1)}, u32[]{:S(2)}, u32[]{:S(2)}) collective-permute-start(bf16[128,2176]{1,0:T(8,128)(2,1)S(1)} %collective-permute-done.18.refs_1_), channel_id=1, source_target_pairs={{0,4},{1,5},{2,6},{3,7},{4,0},{5,1},{6,2},{7,3},{8,12},{9,13},{10,... | collective-permute-start | bytes 1671176 | tf_op jit(solution)/shard_map/ppermute | solution.py:358
  160.1 13.7 %collective-permute-start.27 = (bf16[128,2176]{1,0:T(8,128)(2,1)}, bf16[128,2176]{1,0:T(8,128)(2,1)}, u32[]{:S(2)}, u32[]{:S(2)}) collective-permute-start(bf16[128,2176]{1,0:T(8,128)(2,1)} %collective-permute-done.23.refs_2_), channel_id=1, source_target_pairs={{0,2},{1,3},{2,0},{3,1},{4,6},{5,7},{6,4},{7,5},{8,10},{9,11},{10,... | collective-permute-start | bytes 1671176 | tf_op jit(solution)/shard_map/ppermute | solution.py:358
  160.6 14.7 %collective-permute-start.20 = (bf16[128,2176]{1,0:T(8,128)(2,1)S(1)}, bf16[128,2176]{1,0:T(8,128)(2,1)}, u32[]{:S(2)}, u32[]{:S(2)}) collective-permute-start(bf16[128,2176]{1,0:T(8,128)(2,1)S(1)} %collective-permute-done.19.refs_0_), channel_id=1, source_target_pairs={{0,24},{1,25},{2,26},{3,27},{4,28},{5,29},{6,30},{7,31},{8,0},{9,1... | collective-permute-start | bytes 1671176 | tf_op jit(solution)/shard_map/ppermute | solution.py:358
  165.5 13.1 %collective-permute-start.24 = (bf16[128,2176]{1,0:T(8,128)(2,1)}, bf16[128,2176]{1,0:T(8,128)(2,1)}, u32[]{:S(2)}, u32[]{:S(2)}) collective-permute-start(bf16[128,2176]{1,0:T(8,128)(2,1)} %collective-permute-done.21.refs_5_), channel_id=1, source_target_pairs={{0,4},{1,5},{2,6},{3,7},{4,0},{5,1},{6,2},{7,3},{8,12},{9,13},{10,... | collective-permute-start | bytes 1671176 | tf_op jit(solution)/shard_map/ppermute | solution.py:358
  175.3 15.8 %collective-permute-start.28 = (bf16[128,2176]{1,0:T(8,128)(2,1)}, bf16[128,2176]{1,0:T(8,128)(2,1)S(1)}, u32[]{:S(2)}, u32[]{:S(2)}) collective-permute-start(bf16[128,2176]{1,0:T(8,128)(2,1)} %collective-permute-done.20.refs_1_), channel_id=1, source_target_pairs={{0,2},{1,3},{2,0},{3,1},{4,6},{5,7},{6,4},{7,5},{8,10},{9,11},{10,... | collective-permute-start | bytes 1671176 | tf_op jit(solution)/shard_map/ppermute | solution.py:358
  178.6 15.8 %collective-permute-start.25 = (bf16[128,2176]{1,0:T(8,128)(2,1)}, bf16[128,2176]{1,0:T(8,128)(2,1)S(1)}, u32[]{:S(2)}, u32[]{:S(2)}) collective-permute-start(bf16[128,2176]{1,0:T(8,128)(2,1)} %collective-permute-done.20.refs_1_), channel_id=1, source_target_pairs={{0,4},{1,5},{2,6},{3,7},{4,0},{5,1},{6,2},{7,3},{8,12},{9,13},{10,... | collective-permute-start | bytes 1671176 | tf_op jit(solution)/shard_map/ppermute | solution.py:358
  180.3 33.5 %collective-permute-start.33 = (bf16[128,2176]{1,0:T(8,128)(2,1)S(1)}, bf16[128,2176]{1,0:T(8,128)(2,1)S(1)}, u32[]{:S(2)}, u32[]{:S(2)}) collective-permute-start(bf16[128,2176]{1,0:T(8,128)(2,1)S(1)} %collective-permute-done.19.refs_0_), channel_id=1, source_target_pairs={{0,4},{1,5},{2,6},{3,7},{4,0},{5,1},{6,2},{7,3},{8,12},{9,13},{10,... | collective-permute-start | bytes 1671176 | tf_op jit(solution)/shard_map/ppermute | solution.py:358
  180.8 33.5 %collective-permute-start.34 = (bf16[128,2176]{1,0:T(8,128)(2,1)S(1)}, bf16[128,2176]{1,0:T(8,128)(2,1)S(1)}, u32[]{:S(2)}, u32[]{:S(2)}) collective-permute-start(bf16[128,2176]{1,0:T(8,128)(2,1)S(1)} %collective-permute-done.19.refs_0_), channel_id=1, source_target_pairs={{0,2},{1,3},{2,0},{3,1},{4,6},{5,7},{6,4},{7,5},{8,10},{9,11},{10,... | collective-permute-start | bytes 1671176 | tf_op jit(solution)/shard_map/ppermute | solution.py:358
  212.2 14.9 %collective-permute-start.30 = (bf16[128,2048]{1,0:T(8,128)(2,1)S(1)}, bf16[128,2048]{1,0:T(8,128)(2,1)S(1)}, u32[]{:S(2)}, u32[]{:S(2)}) collective-permute-start(bf16[128,2048]{1,0:T(8,128)(2,1)S(1)} %get-tuple-element.69), channel_id=1, source_target_pairs={{0,4},{1,5},{2,6},{3,7},{4,0},{5,1},{6,2},{7,3},{8,12},{9,13},{10,... | collective-permute-start | bytes 1572872 | tf_op jit(solution)/shard_map/ppermute | solution.py:358
  213.8 22.6 %collective-permute-start.36 = (bf16[128,2176]{1,0:T(8,128)(2,1)S(1)}, bf16[128,2176]{1,0:T(8,128)(2,1)S(1)}, u32[]{:S(2)}, u32[]{:S(2)}) collective-permute-start(bf16[128,2176]{1,0:T(8,128)(2,1)S(1)} %collective-permute-done.28.refs_5_), channel_id=1, source_target_pairs={{0,4},{1,5},{2,6},{3,7},{4,0},{5,1},{6,2},{7,3},{8,12},{9,13},{10,... | collective-permute-start | bytes 1671176 | tf_op jit(solution)/shard_map/ppermute | solution.py:358
  214.3 22.1 %collective-permute-start.35 = (bf16[128,2176]{1,0:T(8,128)(2,1)S(1)}, bf16[128,2176]{1,0:T(8,128)(2,1)S(1)}, u32[]{:S(2)}, u32[]{:S(2)}) collective-permute-start(bf16[128,2176]{1,0:T(8,128)(2,1)S(1)} %collective-permute-done.33.refs_2_), channel_id=1, source_target_pairs={{0,2},{1,3},{2,0},{3,1},{4,6},{5,7},{6,4},{7,5},{8,10},{9,11},{10,... | collective-permute-start | bytes 1671176 | tf_op jit(solution)/shard_map/ppermute | solution.py:358
  216.0 33.5 %collective-permute-start.38 = (bf16[128,2048]{1,0:T(8,128)(2,1)S(1)}, bf16[128,2048]{1,0:T(8,128)(2,1)S(1)}, u32[]{:S(2)}, u32[]{:S(2)}) collective-permute-start(bf16[128,2048]{1,0:T(8,128)(2,1)S(1)} %get-tuple-element.82), channel_id=1, source_target_pairs={{0,2},{1,3},{2,0},{3,1},{4,6},{5,7},{6,4},{7,5},{8,10},{9,11},{10,... | collective-permute-start | bytes 1572872 | tf_op jit(solution)/shard_map/ppermute | solution.py:358
  227.3 25.1 %collective-permute-start.31 = (bf16[128,2048]{1,0:T(8,128)(2,1)S(1)}, bf16[128,2048]{1,0:T(8,128)(2,1)S(1)}, u32[]{:S(2)}, u32[]{:S(2)}) collective-permute-start(bf16[128,2048]{1,0:T(8,128)(2,1)S(1)} %add_convert_fusion.6), channel_id=1, source_target_pairs={{0,2},{1,3},{2,0},{3,1},{4,6},{5,7},{6,4},{7,5},{8,10},{9,11},{10,... | collective-permute-start | bytes 1572872 | tf_op jit(solution)/shard_map/ppermute | solution.py:358
  229.1 24.7 %collective-permute-start.29 = (bf16[128,2048]{1,0:T(8,128)(2,1)S(1)}, bf16[128,2048]{1,0:T(8,128)(2,1)S(1)}, u32[]{:S(2)}, u32[]{:S(2)}) collective-permute-start(bf16[128,2048]{1,0:T(8,128)(2,1)S(1)} %get-tuple-element.68), channel_id=1, source_target_pairs={{0,4},{1,5},{2,6},{3,7},{4,0},{5,1},{6,2},{7,3},{8,12},{9,13},{10,... | collective-permute-start | bytes 1572872 | tf_op jit(solution)/shard_map/ppermute | solution.py:358
  249.5 14.9 %collective-permute-start.39 = (bf16[128,2048]{1,0:T(8,128)(2,1)S(1)}, bf16[128,2048]{1,0:T(8,128)(2,1)S(1)}, u32[]{:S(2)}, u32[]{:S(2)}) collective-permute-start(bf16[128,2048]{1,0:T(8,128)(2,1)S(1)} %get-tuple-element.83), channel_id=1, source_target_pairs={{0,2},{1,3},{2,0},{3,1},{4,6},{5,7},{6,4},{7,5},{8,10},{9,11},{10,... | collective-permute-start | bytes 1572872 | tf_op jit(solution)/shard_map/ppermute | solution.py:358
  251.8 14.9 %collective-permute-start.42 = (bf16[128,2048]{1,0:T(8,128)(2,1)S(1)}, bf16[128,2048]{1,0:T(8,128)(2,1)S(1)}, u32[]{:S(2)}, u32[]{:S(2)}) collective-permute-start(bf16[128,2048]{1,0:T(8,128)(2,1)S(1)} %get-tuple-element.89), channel_id=1, source_target_pairs={{0,4},{1,5},{2,6},{3,7},{4,0},{5,1},{6,2},{7,3},{8,12},{9,13},{10,... | collective-permute-start | bytes 1572872 | tf_op jit(solution)/shard_map/ppermute | solution.py:358
  252.4 23.3 %collective-permute-start.37 = (bf16[128,2048]{1,0:T(8,128)(2,1)S(1)}, bf16[128,2048]{1,0:T(8,128)(2,1)S(1)}, u32[]{:S(2)}, u32[]{:S(2)}) collective-permute-start(bf16[128,2048]{1,0:T(8,128)(2,1)S(1)} %get-tuple-element.80), channel_id=1, source_target_pairs={{0,2},{1,3},{2,0},{3,1},{4,6},{5,7},{6,4},{7,5},{8,10},{9,11},{10,... | collective-permute-start | bytes 1572872 | tf_op jit(solution)/shard_map/ppermute | solution.py:358
  254.0 14.8 %collective-permute-start.32 = (bf16[128,2048]{1,0:T(8,128)(2,1)S(1)}, bf16[128,2048]{1,0:T(8,128)(2,1)S(1)}, u32[]{:S(2)}, u32[]{:S(2)}) collective-permute-start(bf16[128,2048]{1,0:T(8,128)(2,1)S(1)} %add_convert_fusion.5), channel_id=1, source_target_pairs={{0,8},{1,9},{2,10},{3,11},{4,12},{5,13},{6,14},{7,15},{8,16},{9,17... | collective-permute-start | bytes 1572872 | tf_op jit(solution)/shard_map/ppermute | solution.py:403
  264.6 13.7 %collective-permute-start.40 = (bf16[128,2048]{1,0:T(8,128)(2,1)S(1)}, bf16[128,2048]{1,0:T(8,128)(2,1)S(1)}, u32[]{:S(2)}, u32[]{:S(2)}) collective-permute-start(bf16[128,2048]{1,0:T(8,128)(2,1)S(1)} %add_convert_fusion.4), channel_id=1, source_target_pairs={{0,4},{1,5},{2,6},{3,7},{4,0},{5,1},{6,2},{7,3},{8,12},{9,13},{10,... | collective-permute-start | bytes 1572872 | tf_op jit(solution)/shard_map/ppermute | solution.py:358
  266.7 17.6 %collective-permute-start.43 = (bf16[128,2048]{1,0:T(8,128)(2,1)S(1)}, bf16[128,2048]{1,0:T(8,128)(2,1)S(1)}, u32[]{:S(2)}, u32[]{:S(2)}) collective-permute-start(bf16[128,2048]{1,0:T(8,128)(2,1)S(1)} %get-tuple-element.90), channel_id=1, source_target_pairs={{0,4},{1,5},{2,6},{3,7},{4,0},{5,1},{6,2},{7,3},{8,12},{9,13},{10,... | collective-permute-start | bytes 1572872 | tf_op jit(solution)/shard_map/ppermute | solution.py:358
  267.4 16.9 %collective-permute-start.44 = (bf16[128,2048]{1,0:T(8,128)(2,1)S(1)}, bf16[128,2048]{1,0:T(8,128)(2,1)S(1)}, u32[]{:S(2)}, u32[]{:S(2)}) collective-permute-start(bf16[128,2048]{1,0:T(8,128)(2,1)S(1)} %add_convert_fusion.2), channel_id=1, source_target_pairs={{0,2},{1,3},{2,0},{3,1},{4,6},{5,7},{6,4},{7,5},{8,10},{9,11},{10,... | collective-permute-start | bytes 1572872 | tf_op jit(solution)/shard_map/ppermute | solution.py:358
  275.7 17.8 %collective-permute-start.46 = (bf16[128,2048]{1,0:T(8,128)(2,1)}, bf16[128,2048]{1,0:T(8,128)(2,1)}, u32[]{:S(2)}, u32[]{:S(2)}) collective-permute-start(bf16[128,2048]{1,0:T(8,128)(2,1)} %get-tuple-element.96), channel_id=1, source_target_pairs={{0,2},{1,3},{2,0},{3,1},{4,6},{5,7},{6,4},{7,5},{8,10},{9,11},{10,... | collective-permute-start | bytes 1572872 | tf_op jit(solution)/shard_map/ppermute | solution.py:358
  279.4 14.8 %collective-permute-start.41 = (bf16[128,2048]{1,0:T(8,128)(2,1)}, bf16[128,2048]{1,0:T(8,128)(2,1)}, u32[]{:S(2)}, u32[]{:S(2)}) collective-permute-start(bf16[128,2048]{1,0:T(8,128)(2,1)} %add_convert_fusion.3), channel_id=1, source_target_pairs={{0,16},{1,17},{2,18},{3,19},{4,20},{5,21},{6,22},{7,23},{8,24},{9,... | collective-permute-start | bytes 1572872 | tf_op jit(solution)/shard_map/ppermute | solution.py:403
  285.4 14.3 %collective-permute-start.45 = (bf16[128,2048]{1,0:T(8,128)(2,1)}, bf16[128,2048]{1,0:T(8,128)(2,1)}, u32[]{:S(2)}, u32[]{:S(2)}) collective-permute-start(bf16[128,2048]{1,0:T(8,128)(2,1)} %add_convert_fusion.1), channel_id=1, source_target_pairs={{0,24},{1,25},{2,26},{3,27},{4,28},{5,29},{6,30},{7,31},{8,0},{9,1... | collective-permute-start | bytes 1572872 | tf_op jit(solution)/shard_map/ppermute | solution.py:403
  289.3 10.4 %collective-permute-start.47 = (bf16[128,2048]{1,0:T(8,128)(2,1)}, bf16[128,2048]{1,0:T(8,128)(2,1)}, u32[]{:S(2)}, u32[]{:S(2)}) collective-permute-start(bf16[128,2048]{1,0:T(8,128)(2,1)} %add_convert_fusion), channel_id=1, source_target_pairs={{0,4},{1,5},{2,6},{3,7},{4,0},{5,1},{6,2},{7,3},{8,12},{9,13},{10,... | collective-permute-start | bytes 1572872 | tf_op jit(solution)/shard_map/ppermute | solution.py:358
  (30 other events, 535.3 us)

commit v5 on v4

--- a/solution.py
+++ b/solution.py
@@ -193,7 +193,7 @@
         give = jnp.where(upper, held[:share], held[share:])
         kind = F32 if step == 1 else BF16
         if step == 1 and ready is not None:
-            give = tie(give, ready)
+            give = tie(give, *ready)
         got = lax.ppermute(give.astype(kind), AXES, [(i, i ^ step) for i in range(count)]).astype(F32)
         early, late = jnp.where(upper, got, keep), jnp.where(upper, keep, got)
         merged = apply(late[:, :, :head], early)
@@ -347,6 +347,48 @@
     return sum(p.astype(F32) for p in parts[1:]) + parts[0].astype(F32)
 
 
+def project_kernel(spots_ref, normed_ref, residual_ref, gain_ref, *refs, counts):
+    parts, (mix_ref, routed_ref, sum_ref) = refs[:-3], refs[-3:]
+    depth = normed_ref.shape[1]
+    half = depth // 2
+    low, high = normed_ref[:, :half], normed_ref[:, half:]
+    odd = spots_ref[len(counts)] == 1
+    mine, others = jnp.where(odd, high, low), jnp.where(odd, low, high)
+    ordered = jnp.concatenate([mine, others], axis=1)
+    first = 0
+    for k, n in enumerate(counts):
+        left = normed_ref[...] if n == 1 else ordered
+        total, at = None, 0
+        for w_ref in parts[first : first + n]:
+            rows = w_ref.shape[0]
+            product = dot(left[:, at : at + rows], w_ref[...])
+            total = product if total is None else total + product
+            at += rows
+        first += n
+        width = total.shape[1]
+        sum_ref[:, pl.ds(pl.multiple_of(spots_ref[k] * width, width), width)] = total
+    mix = (residual_ref[...].astype(F32) + sum_ref[...]).astype(BF16)
+    mix_ref[...] = mix
+    wide = mix.astype(F32)
+    scale = lax.rsqrt(jnp.mean(wide * wide, axis=-1, keepdims=True) + EPS)
+    routed_ref[...] = (wide * scale * gain_ref[...]).astype(BF16)
+
+
+def project(spots, normed, residual, gain, parts):
+    vmem = pl.BlockSpec(memory_space=pltpu.VMEM)
+    flat = sum(parts, [])
+    return pl.pallas_call(
+        functools.partial(project_kernel, counts=[len(p) for p in parts]),
+        in_specs=[pl.BlockSpec(memory_space=pltpu.SMEM)] + [vmem] * (3 + len(flat)),
+        out_specs=[vmem] * 2,
+        out_shape=[jax.ShapeDtypeStruct(residual.shape, BF16)] * 2,
+        scratch_shapes=[pltpu.VMEM(residual.shape, F32)],
+        cost_estimate=pl.CostEstimate(flops=1, bytes_accessed=residual.size, transcendentals=0),
+        compiler_params=pltpu.CompilerParams(vmem_limit_bytes=24 * 2**20),
+        name="project",
+    )(spots, normed, residual, gain[None], *flat)
+
+
 class Links:
     def __init__(self, layout):
         self.layout, self.sent = layout, {}
@@ -406,8 +448,8 @@
         return plus(block, back).astype(BF16)
 
     back1 = links.send(sums[1][3], "x")
-    back0 = links.send(sums[0][3], "y")
-    straight1 = links.send(sums[1][1], "x")
+    back0 = links.send(tie(sums[0][3], back1), "y")
+    straight1 = links.send(tie(sums[1][1], back1), "x")
     last1 = links.send(added(sums[1][2], back1), "y")
     total = [own_turn(1, straight1, last1)]
     for a, b in pairs[1:]:
@@ -482,42 +524,44 @@
     paired = (x, y, cores) == (2, 2, 2) and z % 2 == 0 and twin is not None
     columns = lax.axis_size("exp")
     beside = {i ^ j for i, j in moves_to(layout, lambda c: (c[0], c[1], c[2] ^ 1, c[3]))} if z % 2 == 0 else set()
-    near = columns == 4 and None not in (twin, facing) and twin | facing == columns - 1 and len(beside) == 1
+    along = flip(layout, x=1)
+    near = columns == 4 and None not in (twin, facing, along) and twin | facing == columns - 1 and len(beside) == 1
     swaps = [lax.ppermute(w, AXES, moves(layout, core=1)) for w in (weights if paired else ())]
     if near:
         swaps.append(lax.ppermute(out_weight, AXES, moves(layout, core=1)))
     block_map, read = delta_terms(mixed_qkv, before, conv_weight, log_decay, write_strength, head)
     half = out_weight.shape[0] // 2
-    odd = (place & min(beside)) != 0 if near else None
+    quarter = half // 2
+    odd = ((place & min(beside)) != 0) ^ ((place & along) != 0) if near else None
 
     some = None
     if near:
         some = jnp.where(odd, out_weight[half:], out_weight[:half])
-        some = lax.ppermute(tie(some, before), AXES, moves(layout, y=1))
+        some = [
+            lax.ppermute(w, AXES, moves(layout, y=1))
+            for w in lax.optimization_barrier((some[:quarter], some[quarter:], before))[:2]
+        ]
     state, middle = starting_states(block_map, count, place, some, swaps)
     if near:
-        rest = lax.ppermute(tie(some, middle), AXES, moves_to(layout, lambda c: (c[0], c[1], c[2] ^ 1, c[3])))
-        out_parts = [[out_weight], [some, rest], swaps[-1:]]
+        pieces = tie(some[0], middle), tie(some[1], middle)
+        rest = [
+            lax.ppermute(pieces[0], AXES, moves(layout, x=1)),
+            lax.ppermute(pieces[1], AXES, moves_to(layout, lambda c: (c[0], c[1], c[2] ^ 1, c[3]))),
+        ]
+        out_parts = [[out_weight], [*some, *rest], swaps[-1:]]
         out_parts.append([lax.ppermute(w, AXES, moves(layout, core=1)) for w in out_parts[1]])
         owners = [(place ^ mask) % columns for mask in (0, facing, twin, facing | twin)]
     normed = emit(read, state, output_gate, norm_gain)
     if near:
-        mine = jnp.where(odd, normed[:, half:], normed[:, :half])
-        others = jnp.where(odd, normed[:, :half], normed[:, half:])
-        products = []
-        for part in out_parts:
-            by = [normed] if len(part) == 1 else [mine, others]
-            products.append(sum(jnp.dot(n, w, preferred_element_type=F32) for n, w in zip(by, part)))
-        projected = jnp.concatenate(
-            [sum(jnp.where(o == e, p, 0.0) for o, p in zip(owners, products)) for e in range(columns)], axis=1
-        )
+        spots = jnp.stack([jnp.int32(o) for o in owners] + [odd.astype(jnp.int32)])
+        after_mix, routed_in = project(spots, normed, residual, post_gain, out_parts)
     else:
         projected = jnp.dot(normed, lax.all_gather(out_weight, "exp", axis=1, tiled=True), preferred_element_type=F32)
-    after_mix = (residual.astype(F32) + projected).astype(BF16)
+        after_mix = (residual.astype(F32) + projected).astype(BF16)
+        after_wide = after_mix.astype(F32)
+        scale = lax.rsqrt(jnp.mean(after_wide * after_wide, axis=-1, keepdims=True) + EPS)
+        routed_in = (after_wide * scale * post_gain).astype(BF16)
     after_wide = after_mix.astype(F32)
-    routed_in = (
-        after_wide * lax.rsqrt(jnp.mean(after_wide * after_wide, axis=-1, keepdims=True) + EPS) * post_gain
-    ).astype(BF16)
 
     experts = expert_gate.shape[0] * count
     capacity = rows * expert_ids.shape[1] * 6 // (experts * 5)

time: 304 us -> 299 us (0.984)
  matrix products: 19.3 us -> 9.56 us
  other arithmetic: 15.6 us -> 8.88 us
  Pallas kernels: 45.8 us -> 50.4 us
  local copies, waits for them, and re-layouts: 11.8 us -> 15.8 us
    dot_general x6 -> x0, matrix products: 10.7 us -> none  [local(): jnp.dot(n, w, preferred_element_type=F32)]
    ppermute x27, waiting for transfers between devices: 92.6 us -> 98.9 us  [send(): queue.append(lax.ppermute(value, AXES, moves(self.layout, **{link: turn})))]
    ppermute x2 -> x4, waiting for transfers between devices: 15.5 us -> 10.1 us  [the longest x2 5.54 us: local(): lax.ppermute(w, AXES, moves(layout, y=1))]
    pallas_call x0 -> x1, Pallas kernels: none -> 4.84 us  [project(): pl.pallas_call(functools.partial(project_kernel, counts=[len(p) for p in...]
    ppermute x3, waiting for transfers between devices: 6.15 us -> 10.5 us  [own_turn(): lax.ppermute(part.astype(BF16), AXES, moves(layout, z=t))]
    convert_element_type x2 -> x0, other arithmetic: 3.75 us -> none  [the longest x1 3.56 us: local(): return (after_wide + routed + shared_out).astype(BF16)]
    unnamed x61 -> x67, local copies, waits for them, and re-layouts: 9.04 us -> 11.9 us
    ppermute x2 -> x4, starting transfers between devices: 5.91 us -> 6.43 us  [the longest x2 3.42 us: local(): lax.ppermute(w, AXES, moves(layout, y=1))]
  transfers between devices with their start and end apart: 48 -> 52, of which waited for: 26 -> 28; matrix products, arithmetic and copies ran while one was open for 10% -> 5% of each run, Pallas kernels for 15% -> 15%
where the time goes in v5:
time: 299 us; the launch traced here: 298 us
  waiting for transfers between devices  139 us (46%)
  starting transfers between devices  73.3 us (25%)
  Pallas kernels  50.4 us (17%)
  local copies, waits for them, and re-layouts  15.8 us (5%)
  matrix products  9.56 us (3%)
  other arithmetic  8.88 us (3%)
    ppermute x27, waiting for transfers between devices, send(): queue.append(lax.ppermute(value, AXES, moves(self.layout, **{link: turn})))  98.9 us
    ppermute x27, starting transfers between devices, send(): queue.append(lax.ppermute(value, AXES, moves(self.layout, **{link: turn})))  40.7 us
    pallas_call x2, Pallas kernels, run_experts(): pl.pallas_call(functools.partial(expert_kernel, width=width, capacity=cap...  27.5 us
    pallas_call x1, Pallas kernels, delta_terms(): pl.pallas_call(functools.partial(delta_kernel, head=head, per=per), grid=...  13.7 us
    ppermute x3, starting transfers between devices, starting_states(): lax.ppermute(ahead.astype(BF16), AXES, [(i, i + step) for i in range(coun...  12.6 us
    ppermute x3, waiting for transfers between devices, starting_states(): lax.ppermute(give.astype(kind), AXES, [(i, i ^ step) for i in range(count)])  12.1 us
    unnamed x67, local copies, waits for them, and re-layouts  11.9 us
    ppermute x3, waiting for transfers between devices, own_turn(): lax.ppermute(part.astype(BF16), AXES, moves(layout, z=t))  10.5 us
  transfers between devices with their start and end apart: 52, of which 28 were waited for; matrix products, arithmetic and copies ran while one was open for 5% of the time, Pallas kernels for 15%

profile of v5, /device:TPU:0, one launch (start us, length us, event | category | flops | bytes accessed | tf_op | source)
XLA Modules:
  0.0 297.6 jit_solution(13054348113311011164)
XLA Ops:
  1.0 2.3 collective-permute-start
  6.1 3.4 %collective-permute-start.1 = (bf16[512,512]{1,0:T(8,128)(2,1)}, bf16[512,512]{1,0:T(8,128)(2,1)}, u32[]{:S(2)}, u32[]{:S(2)}) collective-permute-start(bf16[512,512]{1,0:T(8,128)(2,1)} %get-tuple-element.61), channel_id=1, source_target_pairs={{0,2},{1,3},{2,0},{3,1},{4,6},{5,7},{6,4},{7,5},{8,10},{9,11},{10,... | collective-permute-start | bytes 1572872 | tf_op jit(solution)/shard_map/ppermute | solution.py:541
  12.4 13.7 %delta_terms.1 = (f32[16,128,256]{2,1,0:T(8,128)S(1)}, f32[16,128,256]{2,1,0:T(8,128)S(1)}) custom-call(bf16[128,4096]{1,0:T(8,128)(2,1)S(1)} %copy-done.1, bf16[128,4096]{1,0:T(8,128)(2,1)S(1)} %copy-done.1, bf16[128,4096]{1,0:T(8,128)(2,1)S(1)} %copy-done.1, bf16[8,4096]{1,0:T(8,128)(2,1)S(1)} %collective-permute-done.qb_ref.kb_ref.vb_ref, ...), custom_call_target="tpu_custom_call" | custom-call | flops 33554432 | bytes 262144 | tf_op jit(solution)/shard_map/delta_terms/pallas_call | solution.py:132
  28.0 5.5 %collective-permute-done.2.refs_2_ = bf16[512,512]{1,0:T(8,128)(2,1)} collective-permute-done((bf16[512,512]{1,0:T(8,128)(2,1)}, bf16[512,512]{1,0:T(8,128)(2,1)}, u32[]{:S(2)}, u32[]{:S(2)}) %collective-permute-start.2) | collective-permute-done | bytes 524320 | tf_op jit(solution)/shard_map/ppermute | solution.py:541
  34.6 2.1 collective-permute-done.3
  36.7 2.1 broadcast_select_fusion.1
  40.7 3.2 %collective-permute-start.4 = (bf16[4,128,256]{2,1,0:T(8,128)(2,1)}, bf16[4,128,256]{2,1,0:T(8,128)(2,1)S(1)}, u32[]{:S(2)}, u32[]{:S(2)}) collective-permute-start(bf16[4,128,256]{2,1,0:T(8,128)(2,1)} %select_convert_fusion.1), channel_id=1, source_target_pairs={{0,2},{1,3},{2,0},{3,1},{4,6},{5,7},{6,4},{7,5},{8,10},{9,11},{10,... | collective-permute-start | bytes 786440 | tf_op jit(solution)/shard_map/ppermute | solution.py:197
  43.9 6.8 %collective-permute-done.4 = bf16[4,128,256]{2,1,0:T(8,128)(2,1)S(1)} collective-permute-done((bf16[4,128,256]{2,1,0:T(8,128)(2,1)}, bf16[4,128,256]{2,1,0:T(8,128)(2,1)S(1)}, u32[]{:S(2)}, u32[]{:S(2)}) %collective-permute-start.4) | collective-permute-done | bytes 262176 | tf_op jit(solution)/shard_map/ppermute | solution.py:197
  51.5 1.9 collective-permute-start.5
  53.4 3.2 %collective-permute-done.5 = bf16[2,128,256]{2,1,0:T(8,128)(2,1)S(1)} collective-permute-done((bf16[2,128,256]{2,1,0:T(8,128)(2,1)S(1)}, bf16[2,128,256]{2,1,0:T(8,128)(2,1)S(1)}, u32[]{:S(2)}, u32[]{:S(2)}) %collective-permute-start.5) | collective-permute-done | bytes 131104 | tf_op jit(solution)/shard_map/ppermute | solution.py:197
  57.1 3.9 %collective-permute-start.6 = (bf16[2,128,128]{2,1,0:T(8,128)(2,1)S(1)}, bf16[2,128,128]{2,1,0:T(8,128)(2,1)S(1)}, u32[]{:S(2)}, u32[]{:S(2)}) collective-permute-start(bf16[2,128,128]{2,1,0:T(8,128)(2,1)S(1)} %fusion.33), channel_id=1, source_target_pairs={{0,8},{1,9},{2,10},{3,11},{4,12},{5,13},{6,14},{7,15},{8,16},{9,17... | collective-permute-start | bytes 196616 | tf_op jit(solution)/shard_map/ppermute | solution.py:208
  60.9 1.9 collective-permute-done.6
  63.0 4.3 %collective-permute-start.7 = (bf16[2,128,128]{2,1,0:T(8,128)(2,1)S(1)}, bf16[2,128,128]{2,1,0:T(8,128)(2,1)S(1)}, u32[]{:S(2)}, u32[]{:S(2)}) collective-permute-start(bf16[2,128,128]{2,1,0:T(8,128)(2,1)S(1)} %fusion), channel_id=1, source_target_pairs={{0,8},{1,9},{2,10},{3,11},{4,12},{5,13},{6,14},{7,15},{8,16},{9,17... | collective-permute-start | bytes 196616 | tf_op jit(solution)/shard_map/ppermute | solution.py:208
  67.3 1.9 collective-permute-done.7
  69.4 4.4 %collective-permute-start.8 = (bf16[2,128,128]{2,1,0:T(8,128)(2,1)S(1)}, bf16[2,128,128]{2,1,0:T(8,128)(2,1)S(1)}, u32[]{:S(2)}, u32[]{:S(2)}) collective-permute-start(bf16[2,128,128]{2,1,0:T(8,128)(2,1)S(1)} %fusion.1), channel_id=1, source_target_pairs={{0,8},{1,9},{2,10},{3,11},{4,12},{5,13},{6,14},{7,15},{8,16},{9,17... | collective-permute-start | bytes 196616 | tf_op jit(solution)/shard_map/ppermute | solution.py:208
  73.9 2.2 collective-permute-done.8
  78.5 2.5 collective-permute-start.17
  83.9 3.5 %collective-permute-done.16.refs_3_ = bf16[512,512]{1,0:T(8,128)(2,1)S(1)} collective-permute-done((bf16[512,512]{1,0:T(8,128)(2,1)}, bf16[512,512]{1,0:T(8,128)(2,1)S(1)}, u32[]{:S(2)}, u32[]{:S(2)}) %collective-permute-start.16) | collective-permute-done | bytes 524320 | tf_op jit(solution)/shard_map/ppermute | solution.py:548
  93.2 4.4 %emit.1.normed_ref = bf16[128,2048]{1,0:T(8,128)(2,1)} custom-call(f32[16,128,256]{2,1,0:T(8,128)} %copy-done.5, f32[16,128,128]{2,1,0:T(8,128)} %maximum_select_fusion.state_ref, bf16[128,2048]{1,0:T(8,128)(2,1)} %gate_ref.1, f32[1,128]{1,0:T(1,128)} %bitcast.51), custom_call_target="tpu_custom_call" | custom-call | tf_op jit(solution)/shard_map/emit/pallas_call | solution.py:162
  99.7 4.8 %project.1 = (bf16[128,2048]{1,0:T(8,128)(2,1)S(1)}, bf16[128,2048]{1,0:T(8,128)(2,1)S(1)}) custom-call(s32[5]{0:T(128)S(1)} %stack.36.spots_ref, bf16[128,2048]{1,0:T(8,128)(2,1)S(1)} %copy-done.4, bf16[128,2048]{1,0:T(8,128)(2,1)S(1)} %copy-done.13, f32[1,2048]{1,0:T(1,128)S(1)} %bitcast.49, bf16[2048,512]{1,0:T(8,128)(2,1)} %refs_0_.1, ...), custom_call_target="tpu_custom_call" | custom-call | flops 1 | bytes 262144 | tf_op jit(solution)/shard_map/project/pallas_call | solution.py:380
  105.7 4.1 %collective-permute-start.22 = (bf16[128,2176]{1,0:T(8,128)(2,1)S(1)}, bf16[128,2176]{1,0:T(8,128)(2,1)S(1)}, u32[]{:S(2)}, u32[]{:S(2)}) collective-permute-start(bf16[128,2176]{1,0:T(8,128)(2,1)S(1)} %concatenate.43.refs_0_), channel_id=1, source_target_pairs={{0,24},{1,25},{2,26},{3,27},{4,28},{5,29},{6,30},{7,31},{8,0},{9,1... | collective-permute-start | bytes 1671176 | tf_op jit(solution)/shard_map/ppermute | solution.py:400
  109.8 12.4 %collective-permute-done.22.refs_1_ = bf16[128,2176]{1,0:T(8,128)(2,1)S(1)} collective-permute-done((bf16[128,2176]{1,0:T(8,128)(2,1)S(1)}, bf16[128,2176]{1,0:T(8,128)(2,1)S(1)}, u32[]{:S(2)}, u32[]{:S(2)}) %collective-permute-start.22) | collective-permute-done | bytes 557088 | tf_op jit(solution)/shard_map/ppermute | solution.py:400
  122.2 4.3 %collective-permute-start.23 = (bf16[128,2176]{1,0:T(8,128)(2,1)S(1)}, bf16[128,2176]{1,0:T(8,128)(2,1)}, u32[]{:S(2)}, u32[]{:S(2)}) collective-permute-start(bf16[128,2176]{1,0:T(8,128)(2,1)S(1)} %collective-permute-done.22.refs_1_), channel_id=1, source_target_pairs={{0,24},{1,25},{2,26},{3,27},{4,28},{5,29},{6,30},{7,31},{8,0},{9,1... | collective-permute-start | bytes 1671176 | tf_op jit(solution)/shard_map/ppermute | solution.py:400
  131.3 6.7 %collective-permute-done.23.refs_0_ = bf16[128,2176]{1,0:T(8,128)(2,1)} collective-permute-done((bf16[128,2176]{1,0:T(8,128)(2,1)S(1)}, bf16[128,2176]{1,0:T(8,128)(2,1)}, u32[]{:S(2)}, u32[]{:S(2)}) %collective-permute-start.23) | collective-permute-done | bytes 557088 | tf_op jit(solution)/shard_map/ppermute | solution.py:400
  138.1 4.4 %collective-permute-start.24 = (bf16[128,2176]{1,0:T(8,128)(2,1)}, bf16[128,2176]{1,0:T(8,128)(2,1)}, u32[]{:S(2)}, u32[]{:S(2)}) collective-permute-start(bf16[128,2176]{1,0:T(8,128)(2,1)} %collective-permute-done.23.refs_0_), channel_id=1, source_target_pairs={{0,24},{1,25},{2,26},{3,27},{4,28},{5,29},{6,30},{7,31},{8,0},{9,1... | collective-permute-start | bytes 1671176 | tf_op jit(solution)/shard_map/ppermute | solution.py:400
  144.3 9.2 %collective-permute-done.27.refs_2_ = bf16[128,2176]{1,0:T(8,128)(2,1)} collective-permute-done((bf16[128,2176]{1,0:T(8,128)(2,1)S(1)}, bf16[128,2176]{1,0:T(8,128)(2,1)}, u32[]{:S(2)}, u32[]{:S(2)}) %collective-permute-start.27) | collective-permute-done | bytes 557088 | tf_op jit(solution)/shard_map/ppermute | solution.py:400
  154.6 1.7 collective-permute-start.31
  156.4 10.0 %collective-permute-done.28.refs_7_ = bf16[128,2176]{1,0:T(8,128)(2,1)} collective-permute-done((bf16[128,2176]{1,0:T(8,128)(2,1)}, bf16[128,2176]{1,0:T(8,128)(2,1)}, u32[]{:S(2)}, u32[]{:S(2)}) %collective-permute-start.28) | collective-permute-done | bytes 557088 | tf_op jit(solution)/shard_map/ppermute | solution.py:400
  167.4 1.7 collective-permute-start.32
  171.4 10.8 %collective-permute-done.29.refs_3_ = bf16[128,2176]{1,0:T(8,128)(2,1)S(1)} collective-permute-done((bf16[128,2176]{1,0:T(8,128)(2,1)}, bf16[128,2176]{1,0:T(8,128)(2,1)S(1)}, u32[]{:S(2)}, u32[]{:S(2)}) %collective-permute-start.29) | collective-permute-done | bytes 557088 | tf_op jit(solution)/shard_map/ppermute | solution.py:400
  186.4 14.5 %experts.2 = (bf16[128,2048]{1,0:T(8,128)(2,1)S(1)}, bf16[128,2048]{1,0:T(8,128)(2,1)S(1)}, bf16[128,2048]{1,0:T(8,128)(2,1)S(1)}, bf16[128,2048]{1,0:T(8,128)(2...) custom-call(bf16[128,2176]{1,0:T(8,128)(2,1)S(1)} %concatenate.43.re, ...), custom_call_target="tpu_custom_call" | custom-call | flops 1048576 | bytes 262144 | tf_op jit(solution)/shard_map/experts/pallas_call | solution.py:321
  200.9 1.8 collective-permute-start.33
  204.7 11.1 %collective-permute-done.33 = bf16[128,2048]{1,0:T(8,128)(2,1)S(1)} collective-permute-done((bf16[128,2048]{1,0:T(8,128)(2,1)S(1)}, bf16[128,2048]{1,0:T(8,128)(2,1)S(1)}, u32[]{:S(2)}, u32[]{:S(2)}) %collective-permute-start.33) | collective-permute-done | bytes 524320 | tf_op jit(solution)/shard_map/ppermute | solution.py:400
  215.8 1.7 collective-permute-start.42
  218.0 1.7 collective-permute-start.34
  219.7 4.5 %collective-permute-done.40.refs_7_ = bf16[128,2176]{1,0:T(8,128)(2,1)S(1)} collective-permute-done((bf16[128,2176]{1,0:T(8,128)(2,1)S(1)}, bf16[128,2176]{1,0:T(8,128)(2,1)S(1)}, u32[]{:S(2)}, u32[]{:S(2)}) %collective-permute-start.40) | collective-permute-done | bytes 557088 | tf_op jit(solution)/shard_map/ppermute | solution.py:400
  224.2 13.0 %experts.3 = (bf16[128,2048]{1,0:T(8,128)(2,1)S(1)}, bf16[128,2048]{1,0:T(8,128)(2,1)S(1)}, bf16[128,2048]{1,0:T(8,128)(2,1)S(1)}, bf16[128,2048]{1,0:T(8,128)(2...) custom-call(bf16[128,2176]{1,0:T(8,128)(2,1)} %collective-permute-do, ...), custom_call_target="tpu_custom_call" | custom-call | flops 1048576 | bytes 262144 | tf_op jit(solution)/shard_map/experts/pallas_call | solution.py:321
  237.3 1.8 collective-permute-start.46
  241.5 10.7 %collective-permute-done.46 = bf16[128,2048]{1,0:T(8,128)(2,1)S(1)} collective-permute-done((bf16[128,2048]{1,0:T(8,128)(2,1)S(1)}, bf16[128,2048]{1,0:T(8,128)(2,1)S(1)}, u32[]{:S(2)}, u32[]{:S(2)}) %collective-permute-start.46) | collective-permute-done | bytes 524320 | tf_op jit(solution)/shard_map/ppermute | solution.py:400
  252.2 1.7 collective-permute-start.47
  254.5 1.8 collective-permute-start.48
  256.4 8.8 %collective-permute-done.41 = bf16[128,2048]{1,0:T(8,128)(2,1)S(1)} collective-permute-done((bf16[128,2048]{1,0:T(8,128)(2,1)S(1)}, bf16[128,2048]{1,0:T(8,128)(2,1)S(1)}, u32[]{:S(2)}, u32[]{:S(2)}) %collective-permute-start.41) | collective-permute-done | bytes 524320 | tf_op jit(solution)/shard_map/ppermute | solution.py:400
  265.9 6.7 %collective-permute-done.44 = bf16[128,2048]{1,0:T(8,128)(2,1)S(1)} collective-permute-done((bf16[128,2048]{1,0:T(8,128)(2,1)S(1)}, bf16[128,2048]{1,0:T(8,128)(2,1)S(1)}, u32[]{:S(2)}, u32[]{:S(2)}) %collective-permute-start.44) | collective-permute-done | bytes 524320 | tf_op jit(solution)/shard_map/ppermute | solution.py:400
  272.6 1.7 collective-permute-start.51
  276.8 4.9 %collective-permute-done.51 = bf16[128,2048]{1,0:T(8,128)(2,1)S(1)} collective-permute-done((bf16[128,2048]{1,0:T(8,128)(2,1)S(1)}, bf16[128,2048]{1,0:T(8,128)(2,1)S(1)}, u32[]{:S(2)}, u32[]{:S(2)}) %collective-permute-start.51) | collective-permute-done | bytes 524320 | tf_op jit(solution)/shard_map/ppermute | solution.py:400
  281.8 3.7 %collective-permute-done.49 = bf16[128,2048]{1,0:T(8,128)(2,1)S(1)} collective-permute-done((bf16[128,2048]{1,0:T(8,128)(2,1)S(1)}, bf16[128,2048]{1,0:T(8,128)(2,1)S(1)}, u32[]{:S(2)}, u32[]{:S(2)}) %collective-permute-start.49) | collective-permute-done | bytes 524320 | tf_op jit(solution)/shard_map/ppermute | solution.py:445
  285.5 6.8 %collective-permute-done.45 = bf16[128,2048]{1,0:T(8,128)(2,1)S(1)} collective-permute-done((bf16[128,2048]{1,0:T(8,128)(2,1)S(1)}, bf16[128,2048]{1,0:T(8,128)(2,1)S(1)}, u32[]{:S(2)}, u32[]{:S(2)}) %collective-permute-start.45) | collective-permute-done | bytes 524320 | tf_op jit(solution)/shard_map/ppermute | solution.py:445
  293.1 4.5 %add_convert_fusion = bf16[128,2048]{1,0:T(8,128)(2,1)} fusion(bf16[128,2048]{1,0:T(8,128)(2,1)} %copy-done.16, bf16[128,2048]{1,0:T(8,128)(2,1)} %copy-done.25, bf16[128,2048]{1,0:T(8,128)(2,1)} %copy-done.24, bf16[128,2048]{1,0:T(8,128)(2,1)} %copy-done.26, bf16[128,2048]{1,0:T(8,128)(2,1)} %copy-done.27, bf16[128,2048]{1,0:T(8,128)(2,1)} %copy-done.23, ...), kind=kOutput, calls=%fused_computation.19 | convolution fusion | flops 541458432 | bytes 9175552 | tf_op jit(solution)/shard_map/dot_general | solution.py:581
  (180 shorter events, 52.1 us)
Async XLA Ops:
  1.0 5.1 %collective-permute-start = (bf16[8,4096]{1,0:T(8,128)(2,1)S(1)}, bf16[8,4096]{1,0:T(8,128)(2,1)S(1)}, u32[]{:S(2)}, u32[]{:S(2)}) collective-permute-start(bf16[8,4096]{1,0:T(8,128)(2,1)S(1)} %slice.93), channel_id=1, source_target_pairs={{0,1},{1,2},{2,3},{3,4},{4,5},{5,6},{6,7},{7,8},{8,9},{9,10},{10,1... | collective-permute-start | bytes 196616 | tf_op jit(solution)/shard_map/ppermute | solution.py:520
  6.1 21.9 %collective-permute-start.1 = (bf16[512,512]{1,0:T(8,128)(2,1)}, bf16[512,512]{1,0:T(8,128)(2,1)}, u32[]{:S(2)}, u32[]{:S(2)}) collective-permute-start(bf16[512,512]{1,0:T(8,128)(2,1)} %get-tuple-element.61), channel_id=1, source_target_pairs={{0,2},{1,3},{2,0},{3,1},{4,6},{5,7},{6,4},{7,5},{8,10},{9,11},{10,... | collective-permute-start | bytes 1572872 | tf_op jit(solution)/shard_map/ppermute | solution.py:541
  9.5 24.0 %collective-permute-start.2 = (bf16[512,512]{1,0:T(8,128)(2,1)}, bf16[512,512]{1,0:T(8,128)(2,1)}, u32[]{:S(2)}, u32[]{:S(2)}) collective-permute-start(bf16[512,512]{1,0:T(8,128)(2,1)} %get-tuple-element.62), channel_id=1, source_target_pairs={{0,2},{1,3},{2,0},{3,1},{4,6},{5,7},{6,4},{7,5},{8,10},{9,11},{10,... | collective-permute-start | bytes 1572872 | tf_op jit(solution)/shard_map/ppermute | solution.py:541
  33.7 42.4 %collective-permute-start.9 = (bf16[2,2048,512]{2,1,0:T(8,128)(2,1)}, bf16[2,2048,512]{2,1,0:T(8,128)(2,1)}, u32[]{:S(2)}, u32[]{:S(2)}) collective-permute-start(bf16[2,2048,512]{2,1,0:T(8,128)(2,1)} %refs_9_.3), channel_id=1, source_target_pairs={{0,1},{1,0},{2,3},{3,2},{4,5},{5,4},{6,7},{7,6},{8,9},{9,8},{10,11... | collective-permute-start | bytes 12582920 | tf_op jit(solution)/shard_map/ppermute | solution.py:529
  34.1 42.0 %collective-permute-start.10 = (bf16[2,2048,512]{2,1,0:T(8,128)(2,1)}, bf16[2,2048,512]{2,1,0:T(8,128)(2,1)}, u32[]{:S(2)}, u32[]{:S(2)}) collective-permute-start(bf16[2,2048,512]{2,1,0:T(8,128)(2,1)} %refs_10_.3), channel_id=1, source_target_pairs={{0,1},{1,0},{2,3},{3,2},{4,5},{5,4},{6,7},{7,6},{8,9},{9,8},{10,11... | collective-permute-start | bytes 12582920 | tf_op jit(solution)/shard_map/ppermute | solution.py:529
  34.2 41.9 %collective-permute-start.11 = (bf16[2,512,2048]{2,1,0:T(8,128)(2,1)}, bf16[2,512,2048]{2,1,0:T(8,128)(2,1)}, u32[]{:S(2)}, u32[]{:S(2)}) collective-permute-start(bf16[2,512,2048]{2,1,0:T(8,128)(2,1)} %refs_11_.3), channel_id=1, source_target_pairs={{0,1},{1,0},{2,3},{3,2},{4,5},{5,4},{6,7},{7,6},{8,9},{9,8},{10,11... | collective-permute-start | bytes 12582920 | tf_op jit(solution)/shard_map/ppermute | solution.py:529
  40.7 10.0 %collective-permute-start.4 = (bf16[4,128,256]{2,1,0:T(8,128)(2,1)}, bf16[4,128,256]{2,1,0:T(8,128)(2,1)S(1)}, u32[]{:S(2)}, u32[]{:S(2)}) collective-permute-start(bf16[4,128,256]{2,1,0:T(8,128)(2,1)} %select_convert_fusion.1), channel_id=1, source_target_pairs={{0,2},{1,3},{2,0},{3,1},{4,6},{5,7},{6,4},{7,5},{8,10},{9,11},{10,... | collective-permute-start | bytes 786440 | tf_op jit(solution)/shard_map/ppermute | solution.py:197
  43.9 32.2 %collective-permute-start.12 = (bf16[2048,512]{1,0:T(8,128)(2,1)}, bf16[2048,512]{1,0:T(8,128)(2,1)}, u32[]{:S(2)}, u32[]{:S(2)}) collective-permute-start(bf16[2048,512]{1,0:T(8,128)(2,1)} %refs_0_.1), channel_id=1, source_target_pairs={{0,1},{1,0},{2,3},{3,2},{4,5},{5,4},{6,7},{7,6},{8,9},{9,8},{10,11... | collective-permute-start | bytes 6291464 | tf_op jit(solution)/shard_map/ppermute | solution.py:531
  57.1 5.8 %collective-permute-start.6 = (bf16[2,128,128]{2,1,0:T(8,128)(2,1)S(1)}, bf16[2,128,128]{2,1,0:T(8,128)(2,1)S(1)}, u32[]{:S(2)}, u32[]{:S(2)}) collective-permute-start(bf16[2,128,128]{2,1,0:T(8,128)(2,1)S(1)} %fusion.33), channel_id=1, source_target_pairs={{0,8},{1,9},{2,10},{3,11},{4,12},{5,13},{6,14},{7,15},{8,16},{9,17... | collective-permute-start | bytes 196616 | tf_op jit(solution)/shard_map/ppermute | solution.py:208
  63.0 6.2 %collective-permute-start.7 = (bf16[2,128,128]{2,1,0:T(8,128)(2,1)S(1)}, bf16[2,128,128]{2,1,0:T(8,128)(2,1)S(1)}, u32[]{:S(2)}, u32[]{:S(2)}) collective-permute-start(bf16[2,128,128]{2,1,0:T(8,128)(2,1)S(1)} %fusion), channel_id=1, source_target_pairs={{0,8},{1,9},{2,10},{3,11},{4,12},{5,13},{6,14},{7,15},{8,16},{9,17... | collective-permute-start | bytes 196616 | tf_op jit(solution)/shard_map/ppermute | solution.py:208
  69.4 6.6 %collective-permute-start.8 = (bf16[2,128,128]{2,1,0:T(8,128)(2,1)S(1)}, bf16[2,128,128]{2,1,0:T(8,128)(2,1)S(1)}, u32[]{:S(2)}, u32[]{:S(2)}) collective-permute-start(bf16[2,128,128]{2,1,0:T(8,128)(2,1)S(1)} %fusion.1), channel_id=1, source_target_pairs={{0,8},{1,9},{2,10},{3,11},{4,12},{5,13},{6,14},{7,15},{8,16},{9,17... | collective-permute-start | bytes 196616 | tf_op jit(solution)/shard_map/ppermute | solution.py:208
  78.0 9.4 %collective-permute-start.16 = (bf16[512,512]{1,0:T(8,128)(2,1)}, bf16[512,512]{1,0:T(8,128)(2,1)S(1)}, u32[]{:S(2)}, u32[]{:S(2)}) collective-permute-start(bf16[512,512]{1,0:T(8,128)(2,1)} %collective-permute-done.1.refs_1_), channel_id=1, source_target_pairs={{0,4},{1,5},{2,6},{3,7},{4,0},{5,1},{6,2},{7,3},{8,12},{9,13},{10,... | collective-permute-start | bytes 1572872 | tf_op jit(solution)/shard_map/ppermute | solution.py:548
  78.5 10.0 %collective-permute-start.17 = (bf16[512,512]{1,0:T(8,128)(2,1)}, bf16[512,512]{1,0:T(8,128)(2,1)}, u32[]{:S(2)}, u32[]{:S(2)}) collective-permute-start(bf16[512,512]{1,0:T(8,128)(2,1)} %collective-permute-done.2.refs_2_), channel_id=1, source_target_pairs={{0,8},{1,9},{2,10},{3,11},{4,12},{5,13},{6,14},{7,15},{8,0},{9,1},... | collective-permute-start | bytes 1572872 | tf_op jit(solution)/shard_map/ppermute | solution.py:549
  81.8 6.6 %collective-permute-start.14 = (bf16[4,128,128]{2,1,0:T(8,128)(2,1)S(1)}, bf16[4,128,128]{2,1,0:T(8,128)(2,1)S(1)}, u32[]{:S(2)}, u32[]{:S(2)}) collective-permute-start(bf16[4,128,128]{2,1,0:T(8,128)(2,1)S(1)} %select_convert_fusion.2), channel_id=1, source_target_pairs={{0,2},{1,3},{2,0},{3,1},{4,6},{5,7},{6,4},{7,5},{8,10},{9,11},{10,... | collective-permute-start | bytes 393224 | tf_op jit(solution)/shard_map/ppermute | solution.py:214
  83.4 14.2 %collective-permute-start.18 = (bf16[512,512]{1,0:T(8,128)(2,1)}, bf16[512,512]{1,0:T(8,128)(2,1)}, u32[]{:S(2)}, u32[]{:S(2)}) collective-permute-start(bf16[512,512]{1,0:T(8,128)(2,1)} %collective-permute-done.1.refs_1_), channel_id=1, source_target_pairs={{0,1},{1,0},{2,3},{3,2},{4,5},{5,4},{6,7},{7,6},{8,9},{9,8},{10,11... | collective-permute-start | bytes 1572872 | tf_op jit(solution)/shard_map/ppermute | solution.py:552
  83.4 14.2 %collective-permute-start.19 = (bf16[512,512]{1,0:T(8,128)(2,1)}, bf16[512,512]{1,0:T(8,128)(2,1)}, u32[]{:S(2)}, u32[]{:S(2)}) collective-permute-start(bf16[512,512]{1,0:T(8,128)(2,1)} %collective-permute-done.2.refs_2_), channel_id=1, source_target_pairs={{0,1},{1,0},{2,3},{3,2},{4,5},{5,4},{6,7},{7,6},{8,9},{9,8},{10,11... | collective-permute-start | bytes 1572872 | tf_op jit(solution)/shard_map/ppermute | solution.py:552
  87.4 10.3 %collective-permute-start.20 = (bf16[512,512]{1,0:T(8,128)(2,1)S(1)}, bf16[512,512]{1,0:T(8,128)(2,1)}, u32[]{:S(2)}, u32[]{:S(2)}) collective-permute-start(bf16[512,512]{1,0:T(8,128)(2,1)S(1)} %collective-permute-done.16.refs_3_), channel_id=1, source_target_pairs={{0,1},{1,0},{2,3},{3,2},{4,5},{5,4},{6,7},{7,6},{8,9},{9,8},{10,11... | collective-permute-start | bytes 1572872 | tf_op jit(solution)/shard_map/ppermute | solution.py:552
  88.4 9.2 %collective-permute-start.21 = (bf16[512,512]{1,0:T(8,128)(2,1)}, bf16[512,512]{1,0:T(8,128)(2,1)}, u32[]{:S(2)}, u32[]{:S(2)}) collective-permute-start(bf16[512,512]{1,0:T(8,128)(2,1)} %collective-permute-done.17.refs_4_), channel_id=1, source_target_pairs={{0,1},{1,0},{2,3},{3,2},{4,5},{5,4},{6,7},{7,6},{8,9},{9,8},{10,11... | collective-permute-start | bytes 1572872 | tf_op jit(solution)/shard_map/ppermute | solution.py:552
  105.7 16.5 %collective-permute-start.22 = (bf16[128,2176]{1,0:T(8,128)(2,1)S(1)}, bf16[128,2176]{1,0:T(8,128)(2,1)S(1)}, u32[]{:S(2)}, u32[]{:S(2)}) collective-permute-start(bf16[128,2176]{1,0:T(8,128)(2,1)S(1)} %concatenate.43.refs_0_), channel_id=1, source_target_pairs={{0,24},{1,25},{2,26},{3,27},{4,28},{5,29},{6,30},{7,31},{8,0},{9,1... | collective-permute-start | bytes 1671176 | tf_op jit(solution)/shard_map/ppermute | solution.py:400
  122.2 15.9 %collective-permute-start.23 = (bf16[128,2176]{1,0:T(8,128)(2,1)S(1)}, bf16[128,2176]{1,0:T(8,128)(2,1)}, u32[]{:S(2)}, u32[]{:S(2)}) collective-permute-start(bf16[128,2176]{1,0:T(8,128)(2,1)S(1)} %collective-permute-done.22.refs_1_), channel_id=1, source_target_pairs={{0,24},{1,25},{2,26},{3,27},{4,28},{5,29},{6,30},{7,31},{8,0},{9,1... | collective-permute-start | bytes 1671176 | tf_op jit(solution)/shard_map/ppermute | solution.py:400
  126.5 16.0 %collective-permute-start.25 = (bf16[128,2176]{1,0:T(8,128)(2,1)S(1)}, bf16[128,2176]{1,0:T(8,128)(2,1)}, u32[]{:S(2)}, u32[]{:S(2)}) collective-permute-start(bf16[128,2176]{1,0:T(8,128)(2,1)S(1)} %collective-permute-done.22.refs_1_), channel_id=1, source_target_pairs={{0,2},{1,3},{2,0},{3,1},{4,6},{5,7},{6,4},{7,5},{8,10},{9,11},{10,... | collective-permute-start | bytes 1671176 | tf_op jit(solution)/shard_map/ppermute | solution.py:400
  127.9 15.6 %collective-permute-start.26 = (bf16[128,2176]{1,0:T(8,128)(2,1)S(1)}, bf16[128,2176]{1,0:T(8,128)(2,1)S(1)}, u32[]{:S(2)}, u32[]{:S(2)}) collective-permute-start(bf16[128,2176]{1,0:T(8,128)(2,1)S(1)} %collective-permute-done.22.refs_1_), channel_id=1, source_target_pairs={{0,4},{1,5},{2,6},{3,7},{4,0},{5,1},{6,2},{7,3},{8,12},{9,13},{10,... | collective-permute-start | bytes 1671176 | tf_op jit(solution)/shard_map/ppermute | solution.py:400
  129.0 24.4 %collective-permute-start.27 = (bf16[128,2176]{1,0:T(8,128)(2,1)S(1)}, bf16[128,2176]{1,0:T(8,128)(2,1)}, u32[]{:S(2)}, u32[]{:S(2)}) collective-permute-start(bf16[128,2176]{1,0:T(8,128)(2,1)S(1)} %concatenate.43.refs_0_), channel_id=1, source_target_pairs={{0,4},{1,5},{2,6},{3,7},{4,0},{5,1},{6,2},{7,3},{8,12},{9,13},{10,... | collective-permute-start | bytes 1671176 | tf_op jit(solution)/shard_map/ppermute | solution.py:400
  130.7 23.1 %collective-permute-start.30 = (bf16[128,2176]{1,0:T(8,128)(2,1)S(1)}, bf16[128,2176]{1,0:T(8,128)(2,1)S(1)}, u32[]{:S(2)}, u32[]{:S(2)}) collective-permute-start(bf16[128,2176]{1,0:T(8,128)(2,1)S(1)} %concatenate.43.refs_0_), channel_id=1, source_target_pairs={{0,2},{1,3},{2,0},{3,1},{4,6},{5,7},{6,4},{7,5},{8,10},{9,11},{10,... | collective-permute-start | bytes 1671176 | tf_op jit(solution)/shard_map/ppermute | solution.py:400
  138.1 18.3 %collective-permute-start.24 = (bf16[128,2176]{1,0:T(8,128)(2,1)}, bf16[128,2176]{1,0:T(8,128)(2,1)}, u32[]{:S(2)}, u32[]{:S(2)}) collective-permute-start(bf16[128,2176]{1,0:T(8,128)(2,1)} %collective-permute-done.23.refs_0_), channel_id=1, source_target_pairs={{0,24},{1,25},{2,26},{3,27},{4,28},{5,29},{6,30},{7,31},{8,0},{9,1... | collective-permute-start | bytes 1671176 | tf_op jit(solution)/shard_map/ppermute | solution.py:400
  153.5 12.9 %collective-permute-start.28 = (bf16[128,2176]{1,0:T(8,128)(2,1)}, bf16[128,2176]{1,0:T(8,128)(2,1)}, u32[]{:S(2)}, u32[]{:S(2)}) collective-permute-start(bf16[128,2176]{1,0:T(8,128)(2,1)} %collective-permute-done.25.refs_5_), channel_id=1, source_target_pairs={{0,4},{1,5},{2,6},{3,7},{4,0},{5,1},{6,2},{7,3},{8,12},{9,13},{10,... | collective-permute-start | bytes 1671176 | tf_op jit(solution)/shard_map/ppermute | solution.py:400
  154.6 12.8 %collective-permute-start.31 = (bf16[128,2176]{1,0:T(8,128)(2,1)}, bf16[128,2176]{1,0:T(8,128)(2,1)}, u32[]{:S(2)}, u32[]{:S(2)}) collective-permute-start(bf16[128,2176]{1,0:T(8,128)(2,1)} %collective-permute-done.27.refs_2_), channel_id=1, source_target_pairs={{0,2},{1,3},{2,0},{3,1},{4,6},{5,7},{6,4},{7,5},{8,10},{9,11},{10,... | collective-permute-start | bytes 1671176 | tf_op jit(solution)/shard_map/ppermute | solution.py:400
  166.4 15.8 %collective-permute-start.29 = (bf16[128,2176]{1,0:T(8,128)(2,1)}, bf16[128,2176]{1,0:T(8,128)(2,1)S(1)}, u32[]{:S(2)}, u32[]{:S(2)}) collective-permute-start(bf16[128,2176]{1,0:T(8,128)(2,1)} %collective-permute-done.24.refs_1_), channel_id=1, source_target_pairs={{0,4},{1,5},{2,6},{3,7},{4,0},{5,1},{6,2},{7,3},{8,12},{9,13},{10,... | collective-permute-start | bytes 1671176 | tf_op jit(solution)/shard_map/ppermute | solution.py:400
  167.4 15.8 %collective-permute-start.32 = (bf16[128,2176]{1,0:T(8,128)(2,1)}, bf16[128,2176]{1,0:T(8,128)(2,1)S(1)}, u32[]{:S(2)}, u32[]{:S(2)}) collective-permute-start(bf16[128,2176]{1,0:T(8,128)(2,1)} %collective-permute-done.24.refs_1_), channel_id=1, source_target_pairs={{0,2},{1,3},{2,0},{3,1},{4,6},{5,7},{6,4},{7,5},{8,10},{9,11},{10,... | collective-permute-start | bytes 1671176 | tf_op jit(solution)/shard_map/ppermute | solution.py:400
  169.3 33.3 %collective-permute-start.37 = (bf16[128,2176]{1,0:T(8,128)(2,1)}, bf16[128,2176]{1,0:T(8,128)(2,1)S(1)}, u32[]{:S(2)}, u32[]{:S(2)}) collective-permute-start(bf16[128,2176]{1,0:T(8,128)(2,1)} %collective-permute-done.23.refs_0_), channel_id=1, source_target_pairs={{0,4},{1,5},{2,6},{3,7},{4,0},{5,1},{6,2},{7,3},{8,12},{9,13},{10,... | collective-permute-start | bytes 1671176 | tf_op jit(solution)/shard_map/ppermute | solution.py:400
  169.9 32.8 %collective-permute-start.38 = (bf16[128,2176]{1,0:T(8,128)(2,1)}, bf16[128,2176]{1,0:T(8,128)(2,1)S(1)}, u32[]{:S(2)}, u32[]{:S(2)}) collective-permute-start(bf16[128,2176]{1,0:T(8,128)(2,1)} %collective-permute-done.23.refs_0_), channel_id=1, source_target_pairs={{0,2},{1,3},{2,0},{3,1},{4,6},{5,7},{6,4},{7,5},{8,10},{9,11},{10,... | collective-permute-start | bytes 1671176 | tf_op jit(solution)/shard_map/ppermute | solution.py:400
  200.9 14.9 %collective-permute-start.33 = (bf16[128,2048]{1,0:T(8,128)(2,1)S(1)}, bf16[128,2048]{1,0:T(8,128)(2,1)S(1)}, u32[]{:S(2)}, u32[]{:S(2)}) collective-permute-start(bf16[128,2048]{1,0:T(8,128)(2,1)S(1)} %get-tuple-element.79), channel_id=1, source_target_pairs={{0,4},{1,5},{2,6},{3,7},{4,0},{5,1},{6,2},{7,3},{8,12},{9,13},{10,... | collective-permute-start | bytes 1572872 | tf_op jit(solution)/shard_map/ppermute | solution.py:400
  202.6 17.1 %collective-permute-start.39 = (bf16[128,2176]{1,0:T(8,128)(2,1)S(1)}, bf16[128,2176]{1,0:T(8,128)(2,1)S(1)}, u32[]{:S(2)}, u32[]{:S(2)}) collective-permute-start(bf16[128,2176]{1,0:T(8,128)(2,1)S(1)} %collective-permute-done.37.refs_2_), channel_id=1, source_target_pairs={{0,2},{1,3},{2,0},{3,1},{4,6},{5,7},{6,4},{7,5},{8,10},{9,11},{10,... | collective-permute-start | bytes 1671176 | tf_op jit(solution)/shard_map/ppermute | solution.py:400
  203.2 21.0 %collective-permute-start.40 = (bf16[128,2176]{1,0:T(8,128)(2,1)S(1)}, bf16[128,2176]{1,0:T(8,128)(2,1)S(1)}, u32[]{:S(2)}, u32[]{:S(2)}) collective-permute-start(bf16[128,2176]{1,0:T(8,128)(2,1)S(1)} %collective-permute-done.32.refs_5_), channel_id=1, source_target_pairs={{0,4},{1,5},{2,6},{3,7},{4,0},{5,1},{6,2},{7,3},{8,12},{9,13},{10,... | collective-permute-start | bytes 1671176 | tf_op jit(solution)/shard_map/ppermute | solution.py:400
  215.8 23.3 %collective-permute-start.42 = (bf16[128,2048]{1,0:T(8,128)(2,1)S(1)}, bf16[128,2048]{1,0:T(8,128)(2,1)S(1)}, u32[]{:S(2)}, u32[]{:S(2)}) collective-permute-start(bf16[128,2048]{1,0:T(8,128)(2,1)S(1)} %get-tuple-element.94), channel_id=1, source_target_pairs={{0,2},{1,3},{2,0},{3,1},{4,6},{5,7},{6,4},{7,5},{8,10},{9,11},{10,... | collective-permute-start | bytes 1572872 | tf_op jit(solution)/shard_map/ppermute | solution.py:400
  217.7 22.0 %collective-permute-start.35 = (bf16[128,2048]{1,0:T(8,128)(2,1)S(1)}, bf16[128,2048]{1,0:T(8,128)(2,1)S(1)}, u32[]{:S(2)}, u32[]{:S(2)}) collective-permute-start(bf16[128,2048]{1,0:T(8,128)(2,1)S(1)} %add_convert_fusion.7), channel_id=1, source_target_pairs={{0,2},{1,3},{2,0},{3,1},{4,6},{5,7},{6,4},{7,5},{8,10},{9,11},{10,... | collective-permute-start | bytes 1572872 | tf_op jit(solution)/shard_map/ppermute | solution.py:400
  218.0 21.6 %collective-permute-start.34 = (bf16[128,2048]{1,0:T(8,128)(2,1)S(1)}, bf16[128,2048]{1,0:T(8,128)(2,1)S(1)}, u32[]{:S(2)}, u32[]{:S(2)}) collective-permute-start(bf16[128,2048]{1,0:T(8,128)(2,1)S(1)} %get-tuple-element.80), channel_id=1, source_target_pairs={{0,4},{1,5},{2,6},{3,7},{4,0},{5,1},{6,2},{7,3},{8,12},{9,13},{10,... | collective-permute-start | bytes 1572872 | tf_op jit(solution)/shard_map/ppermute | solution.py:400
  237.3 14.9 %collective-permute-start.46 = (bf16[128,2048]{1,0:T(8,128)(2,1)S(1)}, bf16[128,2048]{1,0:T(8,128)(2,1)S(1)}, u32[]{:S(2)}, u32[]{:S(2)}) collective-permute-start(bf16[128,2048]{1,0:T(8,128)(2,1)S(1)} %get-tuple-element.101), channel_id=1, source_target_pairs={{0,4},{1,5},{2,6},{3,7},{4,0},{5,1},{6,2},{7,3},{8,12},{9,13},{10,... | collective-permute-start | bytes 1572872 | tf_op jit(solution)/shard_map/ppermute | solution.py:400
  239.0 14.9 %collective-permute-start.43 = (bf16[128,2048]{1,0:T(8,128)(2,1)S(1)}, bf16[128,2048]{1,0:T(8,128)(2,1)S(1)}, u32[]{:S(2)}, u32[]{:S(2)}) collective-permute-start(bf16[128,2048]{1,0:T(8,128)(2,1)S(1)} %get-tuple-element.95), channel_id=1, source_target_pairs={{0,2},{1,3},{2,0},{3,1},{4,6},{5,7},{6,4},{7,5},{8,10},{9,11},{10,... | collective-permute-start | bytes 1572872 | tf_op jit(solution)/shard_map/ppermute | solution.py:400
  239.9 16.5 %collective-permute-start.36 = (bf16[128,2048]{1,0:T(8,128)(2,1)S(1)}, bf16[128,2048]{1,0:T(8,128)(2,1)S(1)}, u32[]{:S(2)}, u32[]{:S(2)}) collective-permute-start(bf16[128,2048]{1,0:T(8,128)(2,1)S(1)} %add_convert_fusion.6), channel_id=1, source_target_pairs={{0,8},{1,9},{2,10},{3,11},{4,12},{5,13},{6,14},{7,15},{8,16},{9,17... | collective-permute-start | bytes 1572872 | tf_op jit(solution)/shard_map/ppermute | solution.py:445
  240.0 25.2 %collective-permute-start.41 = (bf16[128,2048]{1,0:T(8,128)(2,1)S(1)}, bf16[128,2048]{1,0:T(8,128)(2,1)S(1)}, u32[]{:S(2)}, u32[]{:S(2)}) collective-permute-start(bf16[128,2048]{1,0:T(8,128)(2,1)S(1)} %get-tuple-element.91), channel_id=1, source_target_pairs={{0,2},{1,3},{2,0},{3,1},{4,6},{5,7},{6,4},{7,5},{8,10},{9,11},{10,... | collective-permute-start | bytes 1572872 | tf_op jit(solution)/shard_map/ppermute | solution.py:400
  252.2 22.1 %collective-permute-start.47 = (bf16[128,2048]{1,0:T(8,128)(2,1)S(1)}, bf16[128,2048]{1,0:T(8,128)(2,1)S(1)}, u32[]{:S(2)}, u32[]{:S(2)}) collective-permute-start(bf16[128,2048]{1,0:T(8,128)(2,1)S(1)} %get-tuple-element.102), channel_id=1, source_target_pairs={{0,4},{1,5},{2,6},{3,7},{4,0},{5,1},{6,2},{7,3},{8,12},{9,13},{10,... | collective-permute-start | bytes 1572872 | tf_op jit(solution)/shard_map/ppermute | solution.py:400
  254.0 18.6 %collective-permute-start.44 = (bf16[128,2048]{1,0:T(8,128)(2,1)S(1)}, bf16[128,2048]{1,0:T(8,128)(2,1)S(1)}, u32[]{:S(2)}, u32[]{:S(2)}) collective-permute-start(bf16[128,2048]{1,0:T(8,128)(2,1)S(1)} %add_convert_fusion.5), channel_id=1, source_target_pairs={{0,4},{1,5},{2,6},{3,7},{4,0},{5,1},{6,2},{7,3},{8,12},{9,13},{10,... | collective-permute-start | bytes 1572872 | tf_op jit(solution)/shard_map/ppermute | solution.py:400
  254.5 19.8 %collective-permute-start.48 = (bf16[128,2048]{1,0:T(8,128)(2,1)S(1)}, bf16[128,2048]{1,0:T(8,128)(2,1)S(1)}, u32[]{:S(2)}, u32[]{:S(2)}) collective-permute-start(bf16[128,2048]{1,0:T(8,128)(2,1)S(1)} %add_convert_fusion.3), channel_id=1, source_target_pairs={{0,2},{1,3},{2,0},{3,1},{4,6},{5,7},{6,4},{7,5},{8,10},{9,11},{10,... | collective-permute-start | bytes 1572872 | tf_op jit(solution)/shard_map/ppermute | solution.py:400
  265.1 11.7 %collective-permute-start.50 = (bf16[128,2048]{1,0:T(8,128)(2,1)S(1)}, bf16[128,2048]{1,0:T(8,128)(2,1)S(1)}, u32[]{:S(2)}, u32[]{:S(2)}) collective-permute-start(bf16[128,2048]{1,0:T(8,128)(2,1)S(1)} %get-tuple-element.108), channel_id=1, source_target_pairs={{0,2},{1,3},{2,0},{3,1},{4,6},{5,7},{6,4},{7,5},{8,10},{9,11},{10,... | collective-permute-start | bytes 1572872 | tf_op jit(solution)/shard_map/ppermute | solution.py:400
  272.6 9.2 %collective-permute-start.51 = (bf16[128,2048]{1,0:T(8,128)(2,1)S(1)}, bf16[128,2048]{1,0:T(8,128)(2,1)S(1)}, u32[]{:S(2)}, u32[]{:S(2)}) collective-permute-start(bf16[128,2048]{1,0:T(8,128)(2,1)S(1)} %add_convert_fusion.1), channel_id=1, source_target_pairs={{0,4},{1,5},{2,6},{3,7},{4,0},{5,1},{6,2},{7,3},{8,12},{9,13},{10,... | collective-permute-start | bytes 1572872 | tf_op jit(solution)/shard_map/ppermute | solution.py:400
  274.6 10.9 %collective-permute-start.49 = (bf16[128,2048]{1,0:T(8,128)(2,1)S(1)}, bf16[128,2048]{1,0:T(8,128)(2,1)S(1)}, u32[]{:S(2)}, u32[]{:S(2)}) collective-permute-start(bf16[128,2048]{1,0:T(8,128)(2,1)S(1)} %add_convert_fusion.2), channel_id=1, source_target_pairs={{0,24},{1,25},{2,26},{3,27},{4,28},{5,29},{6,30},{7,31},{8,0},{9,1... | collective-permute-start | bytes 1572872 | tf_op jit(solution)/shard_map/ppermute | solution.py:445
  275.7 16.6 %collective-permute-start.45 = (bf16[128,2048]{1,0:T(8,128)(2,1)S(1)}, bf16[128,2048]{1,0:T(8,128)(2,1)S(1)}, u32[]{:S(2)}, u32[]{:S(2)}) collective-permute-start(bf16[128,2048]{1,0:T(8,128)(2,1)S(1)} %add_convert_fusion.4), channel_id=1, source_target_pairs={{0,16},{1,17},{2,18},{3,19},{4,20},{5,21},{6,22},{7,23},{8,24},{9,... | collective-permute-start | bytes 1572872 | tf_op jit(solution)/shard_map/ppermute | solution.py:445
  (37 other events, 510.9 us)

commit v6 on v5

--- a/solution.py
+++ b/solution.py
@@ -158,7 +158,7 @@
 def emit(read, state, output_gate, gain):
     vheads, rows, head2 = read.shape
     head = head2 // 2
-    n = 4 if vheads % 4 == 0 else 1
+    n = 8 if vheads % 8 == 0 else 1
     return pl.pallas_call(
         emit_kernel,
         grid=(vheads // n,),
@@ -459,7 +459,7 @@
         straight_b, last_b = links.send(sums[b][1], "x"), links.send(added(sums[b][2], back_b), "y")
         total.append(own_turn(b, straight_b, last_b))
     last0 = links.send(added(tie(sums[0][1], total[0]), back0), "x")
-    straight0 = links.send(tie(sums[0][2], total[0]), "y")
+    straight0 = links.send(tie(sums[0][2], total[0], back0), "y")
     return plus(own_turn(0, straight0, last0), *total)
 
 

time: 299 us -> 297 us (level)
  no operation moved by 1% of the time
where the time goes in v6:
time: 297 us; the launch traced here: 296 us
  waiting for transfers between devices  139 us (47%)
  starting transfers between devices  73.2 us (25%)
  Pallas kernels  49.2 us (17%)
  local copies, waits for them, and re-layouts  15.8 us (5%)
  matrix products  9.57 us (3%)
  other arithmetic  8.88 us (3%)
    ppermute x27, waiting for transfers between devices, send(): queue.append(lax.ppermute(value, AXES, moves(self.layout, **{link: turn})))  99 us
    ppermute x27, starting transfers between devices, send(): queue.append(lax.ppermute(value, AXES, moves(self.layout, **{link: turn})))  40.6 us
    pallas_call x2, Pallas kernels, run_experts(): pl.pallas_call(functools.partial(expert_kernel, width=width, capacity=cap...  27.5 us
    pallas_call x1, Pallas kernels, delta_terms(): pl.pallas_call(functools.partial(delta_kernel, head=head, per=per), grid=...  13.7 us
    ppermute x3, starting transfers between devices, starting_states(): lax.ppermute(ahead.astype(BF16), AXES, [(i, i + step) for i in range(coun...  12.6 us
    ppermute x3, waiting for transfers between devices, starting_states(): lax.ppermute(give.astype(kind), AXES, [(i, i ^ step) for i in range(count)])  12.1 us
    unnamed x67, local copies, waits for them, and re-layouts  11.9 us
    ppermute x3, waiting for transfers between devices, own_turn(): lax.ppermute(part.astype(BF16), AXES, moves(layout, z=t))  10.4 us
  transfers between devices with their start and end apart: 52, of which 28 were waited for; matrix products, arithmetic and copies ran while one was open for 5% of the time, Pallas kernels for 15%

profile of v6, /device:TPU:0, one launch (start us, length us, event | category | flops | bytes accessed | tf_op | source)
XLA Modules:
  0.0 296.4 jit_solution(14362823814030286705)
XLA Ops:
  1.0 2.3 collective-permute-start
  6.1 3.4 %collective-permute-start.1 = (bf16[512,512]{1,0:T(8,128)(2,1)}, bf16[512,512]{1,0:T(8,128)(2,1)}, u32[]{:S(2)}, u32[]{:S(2)}) collective-permute-start(bf16[512,512]{1,0:T(8,128)(2,1)} %get-tuple-element.61), channel_id=1, source_target_pairs={{0,2},{1,3},{2,0},{3,1},{4,6},{5,7},{6,4},{7,5},{8,10},{9,11},{10,... | collective-permute-start | bytes 1572872 | tf_op jit(solution)/shard_map/ppermute | solution.py:541
  12.4 13.7 %delta_terms.1 = (f32[16,128,256]{2,1,0:T(8,128)S(1)}, f32[16,128,256]{2,1,0:T(8,128)S(1)}) custom-call(bf16[128,4096]{1,0:T(8,128)(2,1)S(1)} %copy-done.1, bf16[128,4096]{1,0:T(8,128)(2,1)S(1)} %copy-done.1, bf16[128,4096]{1,0:T(8,128)(2,1)S(1)} %copy-done.1, bf16[8,4096]{1,0:T(8,128)(2,1)S(1)} %collective-permute-done.qb_ref.kb_ref.vb_ref, ...), custom_call_target="tpu_custom_call" | custom-call | flops 33554432 | bytes 262144 | tf_op jit(solution)/shard_map/delta_terms/pallas_call | solution.py:132
  28.0 5.5 %collective-permute-done.2.refs_2_ = bf16[512,512]{1,0:T(8,128)(2,1)} collective-permute-done((bf16[512,512]{1,0:T(8,128)(2,1)}, bf16[512,512]{1,0:T(8,128)(2,1)}, u32[]{:S(2)}, u32[]{:S(2)}) %collective-permute-start.2) | collective-permute-done | bytes 524320 | tf_op jit(solution)/shard_map/ppermute | solution.py:541
  34.6 2.1 collective-permute-done.3
  36.7 2.1 broadcast_select_fusion.1
  40.7 3.2 %collective-permute-start.4 = (bf16[4,128,256]{2,1,0:T(8,128)(2,1)}, bf16[4,128,256]{2,1,0:T(8,128)(2,1)S(1)}, u32[]{:S(2)}, u32[]{:S(2)}) collective-permute-start(bf16[4,128,256]{2,1,0:T(8,128)(2,1)} %select_convert_fusion.1), channel_id=1, source_target_pairs={{0,2},{1,3},{2,0},{3,1},{4,6},{5,7},{6,4},{7,5},{8,10},{9,11},{10,... | collective-permute-start | bytes 786440 | tf_op jit(solution)/shard_map/ppermute | solution.py:197
  43.9 6.8 %collective-permute-done.4 = bf16[4,128,256]{2,1,0:T(8,128)(2,1)S(1)} collective-permute-done((bf16[4,128,256]{2,1,0:T(8,128)(2,1)}, bf16[4,128,256]{2,1,0:T(8,128)(2,1)S(1)}, u32[]{:S(2)}, u32[]{:S(2)}) %collective-permute-start.4) | collective-permute-done | bytes 262176 | tf_op jit(solution)/shard_map/ppermute | solution.py:197
  51.5 1.9 collective-permute-start.5
  53.4 3.2 %collective-permute-done.5 = bf16[2,128,256]{2,1,0:T(8,128)(2,1)S(1)} collective-permute-done((bf16[2,128,256]{2,1,0:T(8,128)(2,1)S(1)}, bf16[2,128,256]{2,1,0:T(8,128)(2,1)S(1)}, u32[]{:S(2)}, u32[]{:S(2)}) %collective-permute-start.5) | collective-permute-done | bytes 131104 | tf_op jit(solution)/shard_map/ppermute | solution.py:197
  57.1 3.9 %collective-permute-start.6 = (bf16[2,128,128]{2,1,0:T(8,128)(2,1)S(1)}, bf16[2,128,128]{2,1,0:T(8,128)(2,1)S(1)}, u32[]{:S(2)}, u32[]{:S(2)}) collective-permute-start(bf16[2,128,128]{2,1,0:T(8,128)(2,1)S(1)} %fusion.33), channel_id=1, source_target_pairs={{0,8},{1,9},{2,10},{3,11},{4,12},{5,13},{6,14},{7,15},{8,16},{9,17... | collective-permute-start | bytes 196616 | tf_op jit(solution)/shard_map/ppermute | solution.py:208
  60.9 1.9 collective-permute-done.6
  63.0 4.3 %collective-permute-start.7 = (bf16[2,128,128]{2,1,0:T(8,128)(2,1)S(1)}, bf16[2,128,128]{2,1,0:T(8,128)(2,1)S(1)}, u32[]{:S(2)}, u32[]{:S(2)}) collective-permute-start(bf16[2,128,128]{2,1,0:T(8,128)(2,1)S(1)} %fusion), channel_id=1, source_target_pairs={{0,8},{1,9},{2,10},{3,11},{4,12},{5,13},{6,14},{7,15},{8,16},{9,17... | collective-permute-start | bytes 196616 | tf_op jit(solution)/shard_map/ppermute | solution.py:208
  67.3 1.9 collective-permute-done.7
  69.4 4.4 %collective-permute-start.8 = (bf16[2,128,128]{2,1,0:T(8,128)(2,1)S(1)}, bf16[2,128,128]{2,1,0:T(8,128)(2,1)S(1)}, u32[]{:S(2)}, u32[]{:S(2)}) collective-permute-start(bf16[2,128,128]{2,1,0:T(8,128)(2,1)S(1)} %fusion.1), channel_id=1, source_target_pairs={{0,8},{1,9},{2,10},{3,11},{4,12},{5,13},{6,14},{7,15},{8,16},{9,17... | collective-permute-start | bytes 196616 | tf_op jit(solution)/shard_map/ppermute | solution.py:208
  73.9 2.2 collective-permute-done.8
  78.5 2.5 collective-permute-start.17
  83.9 3.5 %collective-permute-done.16.refs_3_ = bf16[512,512]{1,0:T(8,128)(2,1)S(1)} collective-permute-done((bf16[512,512]{1,0:T(8,128)(2,1)}, bf16[512,512]{1,0:T(8,128)(2,1)S(1)}, u32[]{:S(2)}, u32[]{:S(2)}) %collective-permute-start.16) | collective-permute-done | bytes 524320 | tf_op jit(solution)/shard_map/ppermute | solution.py:548
  93.2 3.2 %emit.1.normed_ref = bf16[128,2048]{1,0:T(8,128)(2,1)} custom-call(f32[16,128,256]{2,1,0:T(8,128)} %copy-done.5, f32[16,128,128]{2,1,0:T(8,128)} %maximum_select_fusion.state_ref, bf16[128,2048]{1,0:T(8,128)(2,1)} %gate_ref.1, f32[1,128]{1,0:T(1,128)} %bitcast.51), custom_call_target="tpu_custom_call" | custom-call | tf_op jit(solution)/shard_map/emit/pallas_call | solution.py:162
  98.6 4.8 %project.1 = (bf16[128,2048]{1,0:T(8,128)(2,1)S(1)}, bf16[128,2048]{1,0:T(8,128)(2,1)S(1)}) custom-call(s32[5]{0:T(128)S(1)} %stack.36.spots_ref, bf16[128,2048]{1,0:T(8,128)(2,1)S(1)} %copy-done.4, bf16[128,2048]{1,0:T(8,128)(2,1)S(1)} %copy-done.13, f32[1,2048]{1,0:T(1,128)S(1)} %bitcast.49, bf16[2048,512]{1,0:T(8,128)(2,1)} %refs_0_.1, ...), custom_call_target="tpu_custom_call" | custom-call | flops 1 | bytes 262144 | tf_op jit(solution)/shard_map/project/pallas_call | solution.py:380
  104.5 4.1 %collective-permute-start.22 = (bf16[128,2176]{1,0:T(8,128)(2,1)S(1)}, bf16[128,2176]{1,0:T(8,128)(2,1)S(1)}, u32[]{:S(2)}, u32[]{:S(2)}) collective-permute-start(bf16[128,2176]{1,0:T(8,128)(2,1)S(1)} %concatenate.43.refs_0_), channel_id=1, source_target_pairs={{0,24},{1,25},{2,26},{3,27},{4,28},{5,29},{6,30},{7,31},{8,0},{9,1... | collective-permute-start | bytes 1671176 | tf_op jit(solution)/shard_map/ppermute | solution.py:400
  108.6 12.4 %collective-permute-done.22.refs_1_ = bf16[128,2176]{1,0:T(8,128)(2,1)S(1)} collective-permute-done((bf16[128,2176]{1,0:T(8,128)(2,1)S(1)}, bf16[128,2176]{1,0:T(8,128)(2,1)S(1)}, u32[]{:S(2)}, u32[]{:S(2)}) %collective-permute-start.22) | collective-permute-done | bytes 557088 | tf_op jit(solution)/shard_map/ppermute | solution.py:400
  121.0 4.3 %collective-permute-start.23 = (bf16[128,2176]{1,0:T(8,128)(2,1)S(1)}, bf16[128,2176]{1,0:T(8,128)(2,1)}, u32[]{:S(2)}, u32[]{:S(2)}) collective-permute-start(bf16[128,2176]{1,0:T(8,128)(2,1)S(1)} %collective-permute-done.22.refs_1_), channel_id=1, source_target_pairs={{0,24},{1,25},{2,26},{3,27},{4,28},{5,29},{6,30},{7,31},{8,0},{9,1... | collective-permute-start | bytes 1671176 | tf_op jit(solution)/shard_map/ppermute | solution.py:400
  127.9 1.7 collective-permute-start.27
  130.2 6.7 %collective-permute-done.23.refs_0_ = bf16[128,2176]{1,0:T(8,128)(2,1)} collective-permute-done((bf16[128,2176]{1,0:T(8,128)(2,1)S(1)}, bf16[128,2176]{1,0:T(8,128)(2,1)}, u32[]{:S(2)}, u32[]{:S(2)}) %collective-permute-start.23) | collective-permute-done | bytes 557088 | tf_op jit(solution)/shard_map/ppermute | solution.py:400
  136.9 4.4 %collective-permute-start.24 = (bf16[128,2176]{1,0:T(8,128)(2,1)}, bf16[128,2176]{1,0:T(8,128)(2,1)}, u32[]{:S(2)}, u32[]{:S(2)}) collective-permute-start(bf16[128,2176]{1,0:T(8,128)(2,1)} %collective-permute-done.23.refs_0_), channel_id=1, source_target_pairs={{0,24},{1,25},{2,26},{3,27},{4,28},{5,29},{6,30},{7,31},{8,0},{9,1... | collective-permute-start | bytes 1671176 | tf_op jit(solution)/shard_map/ppermute | solution.py:400
  143.2 9.2 %collective-permute-done.27.refs_2_ = bf16[128,2176]{1,0:T(8,128)(2,1)} collective-permute-done((bf16[128,2176]{1,0:T(8,128)(2,1)S(1)}, bf16[128,2176]{1,0:T(8,128)(2,1)}, u32[]{:S(2)}, u32[]{:S(2)}) %collective-permute-start.27) | collective-permute-done | bytes 557088 | tf_op jit(solution)/shard_map/ppermute | solution.py:400
  153.5 1.7 collective-permute-start.31
  155.2 10.0 %collective-permute-done.28.refs_7_ = bf16[128,2176]{1,0:T(8,128)(2,1)} collective-permute-done((bf16[128,2176]{1,0:T(8,128)(2,1)}, bf16[128,2176]{1,0:T(8,128)(2,1)}, u32[]{:S(2)}, u32[]{:S(2)}) %collective-permute-start.28) | collective-permute-done | bytes 557088 | tf_op jit(solution)/shard_map/ppermute | solution.py:400
  166.3 1.7 collective-permute-start.32
  170.2 10.8 %collective-permute-done.29.refs_3_ = bf16[128,2176]{1,0:T(8,128)(2,1)S(1)} collective-permute-done((bf16[128,2176]{1,0:T(8,128)(2,1)}, bf16[128,2176]{1,0:T(8,128)(2,1)S(1)}, u32[]{:S(2)}, u32[]{:S(2)}) %collective-permute-start.29) | collective-permute-done | bytes 557088 | tf_op jit(solution)/shard_map/ppermute | solution.py:400
  185.2 14.5 %experts.2 = (bf16[128,2048]{1,0:T(8,128)(2,1)S(1)}, bf16[128,2048]{1,0:T(8,128)(2,1)S(1)}, bf16[128,2048]{1,0:T(8,128)(2,1)S(1)}, bf16[128,2048]{1,0:T(8,128)(2...) custom-call(bf16[128,2176]{1,0:T(8,128)(2,1)S(1)} %concatenate.43.re, ...), custom_call_target="tpu_custom_call" | custom-call | flops 1048576 | bytes 262144 | tf_op jit(solution)/shard_map/experts/pallas_call | solution.py:321
  199.7 1.8 collective-permute-start.33
  203.6 11.1 %collective-permute-done.33 = bf16[128,2048]{1,0:T(8,128)(2,1)S(1)} collective-permute-done((bf16[128,2048]{1,0:T(8,128)(2,1)S(1)}, bf16[128,2048]{1,0:T(8,128)(2,1)S(1)}, u32[]{:S(2)}, u32[]{:S(2)}) %collective-permute-start.33) | collective-permute-done | bytes 524320 | tf_op jit(solution)/shard_map/ppermute | solution.py:400
  214.6 1.8 collective-permute-start.42
  216.8 1.7 collective-permute-start.34
  218.6 4.5 %collective-permute-done.40.refs_7_ = bf16[128,2176]{1,0:T(8,128)(2,1)S(1)} collective-permute-done((bf16[128,2176]{1,0:T(8,128)(2,1)S(1)}, bf16[128,2176]{1,0:T(8,128)(2,1)S(1)}, u32[]{:S(2)}, u32[]{:S(2)}) %collective-permute-start.40) | collective-permute-done | bytes 557088 | tf_op jit(solution)/shard_map/ppermute | solution.py:400
  223.1 13.0 %experts.3 = (bf16[128,2048]{1,0:T(8,128)(2,1)S(1)}, bf16[128,2048]{1,0:T(8,128)(2,1)S(1)}, bf16[128,2048]{1,0:T(8,128)(2,1)S(1)}, bf16[128,2048]{1,0:T(8,128)(2...) custom-call(bf16[128,2176]{1,0:T(8,128)(2,1)} %collective-permute-do, ...), custom_call_target="tpu_custom_call" | custom-call | flops 1048576 | bytes 262144 | tf_op jit(solution)/shard_map/experts/pallas_call | solution.py:321
  236.1 1.7 collective-permute-start.46
  240.3 10.8 %collective-permute-done.46 = bf16[128,2048]{1,0:T(8,128)(2,1)S(1)} collective-permute-done((bf16[128,2048]{1,0:T(8,128)(2,1)S(1)}, bf16[128,2048]{1,0:T(8,128)(2,1)S(1)}, u32[]{:S(2)}, u32[]{:S(2)}) %collective-permute-start.46) | collective-permute-done | bytes 524320 | tf_op jit(solution)/shard_map/ppermute | solution.py:400
  251.1 1.7 collective-permute-start.47
  253.4 1.8 collective-permute-start.48
  255.2 8.7 %collective-permute-done.41 = bf16[128,2048]{1,0:T(8,128)(2,1)S(1)} collective-permute-done((bf16[128,2048]{1,0:T(8,128)(2,1)S(1)}, bf16[128,2048]{1,0:T(8,128)(2,1)S(1)}, u32[]{:S(2)}, u32[]{:S(2)}) %collective-permute-start.41) | collective-permute-done | bytes 524320 | tf_op jit(solution)/shard_map/ppermute | solution.py:400
  264.7 6.8 %collective-permute-done.44 = bf16[128,2048]{1,0:T(8,128)(2,1)S(1)} collective-permute-done((bf16[128,2048]{1,0:T(8,128)(2,1)S(1)}, bf16[128,2048]{1,0:T(8,128)(2,1)S(1)}, u32[]{:S(2)}, u32[]{:S(2)}) %collective-permute-start.44) | collective-permute-done | bytes 524320 | tf_op jit(solution)/shard_map/ppermute | solution.py:400
  275.7 4.9 %collective-permute-done.51 = bf16[128,2048]{1,0:T(8,128)(2,1)S(1)} collective-permute-done((bf16[128,2048]{1,0:T(8,128)(2,1)S(1)}, bf16[128,2048]{1,0:T(8,128)(2,1)S(1)}, u32[]{:S(2)}, u32[]{:S(2)}) %collective-permute-start.51) | collective-permute-done | bytes 524320 | tf_op jit(solution)/shard_map/ppermute | solution.py:400
  280.7 3.7 %collective-permute-done.49 = bf16[128,2048]{1,0:T(8,128)(2,1)S(1)} collective-permute-done((bf16[128,2048]{1,0:T(8,128)(2,1)S(1)}, bf16[128,2048]{1,0:T(8,128)(2,1)S(1)}, u32[]{:S(2)}, u32[]{:S(2)}) %collective-permute-start.49) | collective-permute-done | bytes 524320 | tf_op jit(solution)/shard_map/ppermute | solution.py:445
  284.3 6.8 %collective-permute-done.45 = bf16[128,2048]{1,0:T(8,128)(2,1)S(1)} collective-permute-done((bf16[128,2048]{1,0:T(8,128)(2,1)S(1)}, bf16[128,2048]{1,0:T(8,128)(2,1)S(1)}, u32[]{:S(2)}, u32[]{:S(2)}) %collective-permute-start.45) | collective-permute-done | bytes 524320 | tf_op jit(solution)/shard_map/ppermute | solution.py:445
  291.9 4.5 %add_convert_fusion = bf16[128,2048]{1,0:T(8,128)(2,1)} fusion(bf16[128,2048]{1,0:T(8,128)(2,1)} %copy-done.16, bf16[128,2048]{1,0:T(8,128)(2,1)} %copy-done.25, bf16[128,2048]{1,0:T(8,128)(2,1)} %copy-done.24, bf16[128,2048]{1,0:T(8,128)(2,1)} %copy-done.26, bf16[128,2048]{1,0:T(8,128)(2,1)} %copy-done.27, bf16[128,2048]{1,0:T(8,128)(2,1)} %copy-done.23, ...), kind=kOutput, calls=%fused_computation.19 | convolution fusion | flops 541458432 | bytes 9175552 | tf_op jit(solution)/shard_map/dot_general | solution.py:581
  (180 shorter events, 52.2 us)
Async XLA Ops:
  1.0 5.1 %collective-permute-start = (bf16[8,4096]{1,0:T(8,128)(2,1)S(1)}, bf16[8,4096]{1,0:T(8,128)(2,1)S(1)}, u32[]{:S(2)}, u32[]{:S(2)}) collective-permute-start(bf16[8,4096]{1,0:T(8,128)(2,1)S(1)} %slice.93), channel_id=1, source_target_pairs={{0,1},{1,2},{2,3},{3,4},{4,5},{5,6},{6,7},{7,8},{8,9},{9,10},{10,1... | collective-permute-start | bytes 196616 | tf_op jit(solution)/shard_map/ppermute | solution.py:520
  6.1 21.9 %collective-permute-start.1 = (bf16[512,512]{1,0:T(8,128)(2,1)}, bf16[512,512]{1,0:T(8,128)(2,1)}, u32[]{:S(2)}, u32[]{:S(2)}) collective-permute-start(bf16[512,512]{1,0:T(8,128)(2,1)} %get-tuple-element.61), channel_id=1, source_target_pairs={{0,2},{1,3},{2,0},{3,1},{4,6},{5,7},{6,4},{7,5},{8,10},{9,11},{10,... | collective-permute-start | bytes 1572872 | tf_op jit(solution)/shard_map/ppermute | solution.py:541
  9.5 24.0 %collective-permute-start.2 = (bf16[512,512]{1,0:T(8,128)(2,1)}, bf16[512,512]{1,0:T(8,128)(2,1)}, u32[]{:S(2)}, u32[]{:S(2)}) collective-permute-start(bf16[512,512]{1,0:T(8,128)(2,1)} %get-tuple-element.62), channel_id=1, source_target_pairs={{0,2},{1,3},{2,0},{3,1},{4,6},{5,7},{6,4},{7,5},{8,10},{9,11},{10,... | collective-permute-start | bytes 1572872 | tf_op jit(solution)/shard_map/ppermute | solution.py:541
  33.7 42.4 %collective-permute-start.9 = (bf16[2,2048,512]{2,1,0:T(8,128)(2,1)}, bf16[2,2048,512]{2,1,0:T(8,128)(2,1)}, u32[]{:S(2)}, u32[]{:S(2)}) collective-permute-start(bf16[2,2048,512]{2,1,0:T(8,128)(2,1)} %refs_9_.3), channel_id=1, source_target_pairs={{0,1},{1,0},{2,3},{3,2},{4,5},{5,4},{6,7},{7,6},{8,9},{9,8},{10,11... | collective-permute-start | bytes 12582920 | tf_op jit(solution)/shard_map/ppermute | solution.py:529
  34.1 42.0 %collective-permute-start.10 = (bf16[2,2048,512]{2,1,0:T(8,128)(2,1)}, bf16[2,2048,512]{2,1,0:T(8,128)(2,1)}, u32[]{:S(2)}, u32[]{:S(2)}) collective-permute-start(bf16[2,2048,512]{2,1,0:T(8,128)(2,1)} %refs_10_.3), channel_id=1, source_target_pairs={{0,1},{1,0},{2,3},{3,2},{4,5},{5,4},{6,7},{7,6},{8,9},{9,8},{10,11... | collective-permute-start | bytes 12582920 | tf_op jit(solution)/shard_map/ppermute | solution.py:529
  34.2 41.9 %collective-permute-start.11 = (bf16[2,512,2048]{2,1,0:T(8,128)(2,1)}, bf16[2,512,2048]{2,1,0:T(8,128)(2,1)}, u32[]{:S(2)}, u32[]{:S(2)}) collective-permute-start(bf16[2,512,2048]{2,1,0:T(8,128)(2,1)} %refs_11_.3), channel_id=1, source_target_pairs={{0,1},{1,0},{2,3},{3,2},{4,5},{5,4},{6,7},{7,6},{8,9},{9,8},{10,11... | collective-permute-start | bytes 12582920 | tf_op jit(solution)/shard_map/ppermute | solution.py:529
  40.7 10.0 %collective-permute-start.4 = (bf16[4,128,256]{2,1,0:T(8,128)(2,1)}, bf16[4,128,256]{2,1,0:T(8,128)(2,1)S(1)}, u32[]{:S(2)}, u32[]{:S(2)}) collective-permute-start(bf16[4,128,256]{2,1,0:T(8,128)(2,1)} %select_convert_fusion.1), channel_id=1, source_target_pairs={{0,2},{1,3},{2,0},{3,1},{4,6},{5,7},{6,4},{7,5},{8,10},{9,11},{10,... | collective-permute-start | bytes 786440 | tf_op jit(solution)/shard_map/ppermute | solution.py:197
  43.9 32.2 %collective-permute-start.12 = (bf16[2048,512]{1,0:T(8,128)(2,1)}, bf16[2048,512]{1,0:T(8,128)(2,1)}, u32[]{:S(2)}, u32[]{:S(2)}) collective-permute-start(bf16[2048,512]{1,0:T(8,128)(2,1)} %refs_0_.1), channel_id=1, source_target_pairs={{0,1},{1,0},{2,3},{3,2},{4,5},{5,4},{6,7},{7,6},{8,9},{9,8},{10,11... | collective-permute-start | bytes 6291464 | tf_op jit(solution)/shard_map/ppermute | solution.py:531
  57.1 5.8 %collective-permute-start.6 = (bf16[2,128,128]{2,1,0:T(8,128)(2,1)S(1)}, bf16[2,128,128]{2,1,0:T(8,128)(2,1)S(1)}, u32[]{:S(2)}, u32[]{:S(2)}) collective-permute-start(bf16[2,128,128]{2,1,0:T(8,128)(2,1)S(1)} %fusion.33), channel_id=1, source_target_pairs={{0,8},{1,9},{2,10},{3,11},{4,12},{5,13},{6,14},{7,15},{8,16},{9,17... | collective-permute-start | bytes 196616 | tf_op jit(solution)/shard_map/ppermute | solution.py:208
  63.0 6.2 %collective-permute-start.7 = (bf16[2,128,128]{2,1,0:T(8,128)(2,1)S(1)}, bf16[2,128,128]{2,1,0:T(8,128)(2,1)S(1)}, u32[]{:S(2)}, u32[]{:S(2)}) collective-permute-start(bf16[2,128,128]{2,1,0:T(8,128)(2,1)S(1)} %fusion), channel_id=1, source_target_pairs={{0,8},{1,9},{2,10},{3,11},{4,12},{5,13},{6,14},{7,15},{8,16},{9,17... | collective-permute-start | bytes 196616 | tf_op jit(solution)/shard_map/ppermute | solution.py:208
  69.4 6.6 %collective-permute-start.8 = (bf16[2,128,128]{2,1,0:T(8,128)(2,1)S(1)}, bf16[2,128,128]{2,1,0:T(8,128)(2,1)S(1)}, u32[]{:S(2)}, u32[]{:S(2)}) collective-permute-start(bf16[2,128,128]{2,1,0:T(8,128)(2,1)S(1)} %fusion.1), channel_id=1, source_target_pairs={{0,8},{1,9},{2,10},{3,11},{4,12},{5,13},{6,14},{7,15},{8,16},{9,17... | collective-permute-start | bytes 196616 | tf_op jit(solution)/shard_map/ppermute | solution.py:208
  78.0 9.4 %collective-permute-start.16 = (bf16[512,512]{1,0:T(8,128)(2,1)}, bf16[512,512]{1,0:T(8,128)(2,1)S(1)}, u32[]{:S(2)}, u32[]{:S(2)}) collective-permute-start(bf16[512,512]{1,0:T(8,128)(2,1)} %collective-permute-done.1.refs_1_), channel_id=1, source_target_pairs={{0,4},{1,5},{2,6},{3,7},{4,0},{5,1},{6,2},{7,3},{8,12},{9,13},{10,... | collective-permute-start | bytes 1572872 | tf_op jit(solution)/shard_map/ppermute | solution.py:548
  78.5 10.0 %collective-permute-start.17 = (bf16[512,512]{1,0:T(8,128)(2,1)}, bf16[512,512]{1,0:T(8,128)(2,1)}, u32[]{:S(2)}, u32[]{:S(2)}) collective-permute-start(bf16[512,512]{1,0:T(8,128)(2,1)} %collective-permute-done.2.refs_2_), channel_id=1, source_target_pairs={{0,8},{1,9},{2,10},{3,11},{4,12},{5,13},{6,14},{7,15},{8,0},{9,1},... | collective-permute-start | bytes 1572872 | tf_op jit(solution)/shard_map/ppermute | solution.py:549
  81.8 6.6 %collective-permute-start.14 = (bf16[4,128,128]{2,1,0:T(8,128)(2,1)S(1)}, bf16[4,128,128]{2,1,0:T(8,128)(2,1)S(1)}, u32[]{:S(2)}, u32[]{:S(2)}) collective-permute-start(bf16[4,128,128]{2,1,0:T(8,128)(2,1)S(1)} %select_convert_fusion.2), channel_id=1, source_target_pairs={{0,2},{1,3},{2,0},{3,1},{4,6},{5,7},{6,4},{7,5},{8,10},{9,11},{10,... | collective-permute-start | bytes 393224 | tf_op jit(solution)/shard_map/ppermute | solution.py:214
  83.4 13.1 %collective-permute-start.18 = (bf16[512,512]{1,0:T(8,128)(2,1)}, bf16[512,512]{1,0:T(8,128)(2,1)}, u32[]{:S(2)}, u32[]{:S(2)}) collective-permute-start(bf16[512,512]{1,0:T(8,128)(2,1)} %collective-permute-done.1.refs_1_), channel_id=1, source_target_pairs={{0,1},{1,0},{2,3},{3,2},{4,5},{5,4},{6,7},{7,6},{8,9},{9,8},{10,11... | collective-permute-start | bytes 1572872 | tf_op jit(solution)/shard_map/ppermute | solution.py:552
  83.4 13.1 %collective-permute-start.19 = (bf16[512,512]{1,0:T(8,128)(2,1)}, bf16[512,512]{1,0:T(8,128)(2,1)}, u32[]{:S(2)}, u32[]{:S(2)}) collective-permute-start(bf16[512,512]{1,0:T(8,128)(2,1)} %collective-permute-done.2.refs_2_), channel_id=1, source_target_pairs={{0,1},{1,0},{2,3},{3,2},{4,5},{5,4},{6,7},{7,6},{8,9},{9,8},{10,11... | collective-permute-start | bytes 1572872 | tf_op jit(solution)/shard_map/ppermute | solution.py:552
  87.4 9.1 %collective-permute-start.20 = (bf16[512,512]{1,0:T(8,128)(2,1)S(1)}, bf16[512,512]{1,0:T(8,128)(2,1)}, u32[]{:S(2)}, u32[]{:S(2)}) collective-permute-start(bf16[512,512]{1,0:T(8,128)(2,1)S(1)} %collective-permute-done.16.refs_3_), channel_id=1, source_target_pairs={{0,1},{1,0},{2,3},{3,2},{4,5},{5,4},{6,7},{7,6},{8,9},{9,8},{10,11... | collective-permute-start | bytes 1572872 | tf_op jit(solution)/shard_map/ppermute | solution.py:552
  88.4 8.0 %collective-permute-start.21 = (bf16[512,512]{1,0:T(8,128)(2,1)}, bf16[512,512]{1,0:T(8,128)(2,1)}, u32[]{:S(2)}, u32[]{:S(2)}) collective-permute-start(bf16[512,512]{1,0:T(8,128)(2,1)} %collective-permute-done.17.refs_4_), channel_id=1, source_target_pairs={{0,1},{1,0},{2,3},{3,2},{4,5},{5,4},{6,7},{7,6},{8,9},{9,8},{10,11... | collective-permute-start | bytes 1572872 | tf_op jit(solution)/shard_map/ppermute | solution.py:552
  104.5 16.5 %collective-permute-start.22 = (bf16[128,2176]{1,0:T(8,128)(2,1)S(1)}, bf16[128,2176]{1,0:T(8,128)(2,1)S(1)}, u32[]{:S(2)}, u32[]{:S(2)}) collective-permute-start(bf16[128,2176]{1,0:T(8,128)(2,1)S(1)} %concatenate.43.refs_0_), channel_id=1, source_target_pairs={{0,24},{1,25},{2,26},{3,27},{4,28},{5,29},{6,30},{7,31},{8,0},{9,1... | collective-permute-start | bytes 1671176 | tf_op jit(solution)/shard_map/ppermute | solution.py:400
  121.0 15.9 %collective-permute-start.23 = (bf16[128,2176]{1,0:T(8,128)(2,1)S(1)}, bf16[128,2176]{1,0:T(8,128)(2,1)}, u32[]{:S(2)}, u32[]{:S(2)}) collective-permute-start(bf16[128,2176]{1,0:T(8,128)(2,1)S(1)} %collective-permute-done.22.refs_1_), channel_id=1, source_target_pairs={{0,24},{1,25},{2,26},{3,27},{4,28},{5,29},{6,30},{7,31},{8,0},{9,1... | collective-permute-start | bytes 1671176 | tf_op jit(solution)/shard_map/ppermute | solution.py:400
  125.3 16.0 %collective-permute-start.25 = (bf16[128,2176]{1,0:T(8,128)(2,1)S(1)}, bf16[128,2176]{1,0:T(8,128)(2,1)}, u32[]{:S(2)}, u32[]{:S(2)}) collective-permute-start(bf16[128,2176]{1,0:T(8,128)(2,1)S(1)} %collective-permute-done.22.refs_1_), channel_id=1, source_target_pairs={{0,2},{1,3},{2,0},{3,1},{4,6},{5,7},{6,4},{7,5},{8,10},{9,11},{10,... | collective-permute-start | bytes 1671176 | tf_op jit(solution)/shard_map/ppermute | solution.py:400
  126.8 15.6 %collective-permute-start.26 = (bf16[128,2176]{1,0:T(8,128)(2,1)S(1)}, bf16[128,2176]{1,0:T(8,128)(2,1)S(1)}, u32[]{:S(2)}, u32[]{:S(2)}) collective-permute-start(bf16[128,2176]{1,0:T(8,128)(2,1)S(1)} %collective-permute-done.22.refs_1_), channel_id=1, source_target_pairs={{0,4},{1,5},{2,6},{3,7},{4,0},{5,1},{6,2},{7,3},{8,12},{9,13},{10,... | collective-permute-start | bytes 1671176 | tf_op jit(solution)/shard_map/ppermute | solution.py:400
  127.9 24.4 %collective-permute-start.27 = (bf16[128,2176]{1,0:T(8,128)(2,1)S(1)}, bf16[128,2176]{1,0:T(8,128)(2,1)}, u32[]{:S(2)}, u32[]{:S(2)}) collective-permute-start(bf16[128,2176]{1,0:T(8,128)(2,1)S(1)} %concatenate.43.refs_0_), channel_id=1, source_target_pairs={{0,4},{1,5},{2,6},{3,7},{4,0},{5,1},{6,2},{7,3},{8,12},{9,13},{10,... | collective-permute-start | bytes 1671176 | tf_op jit(solution)/shard_map/ppermute | solution.py:400
  129.6 23.1 %collective-permute-start.30 = (bf16[128,2176]{1,0:T(8,128)(2,1)S(1)}, bf16[128,2176]{1,0:T(8,128)(2,1)S(1)}, u32[]{:S(2)}, u32[]{:S(2)}) collective-permute-start(bf16[128,2176]{1,0:T(8,128)(2,1)S(1)} %concatenate.43.refs_0_), channel_id=1, source_target_pairs={{0,2},{1,3},{2,0},{3,1},{4,6},{5,7},{6,4},{7,5},{8,10},{9,11},{10,... | collective-permute-start | bytes 1671176 | tf_op jit(solution)/shard_map/ppermute | solution.py:400
  136.9 18.3 %collective-permute-start.24 = (bf16[128,2176]{1,0:T(8,128)(2,1)}, bf16[128,2176]{1,0:T(8,128)(2,1)}, u32[]{:S(2)}, u32[]{:S(2)}) collective-permute-start(bf16[128,2176]{1,0:T(8,128)(2,1)} %collective-permute-done.23.refs_0_), channel_id=1, source_target_pairs={{0,24},{1,25},{2,26},{3,27},{4,28},{5,29},{6,30},{7,31},{8,0},{9,1... | collective-permute-start | bytes 1671176 | tf_op jit(solution)/shard_map/ppermute | solution.py:400
  152.3 12.9 %collective-permute-start.28 = (bf16[128,2176]{1,0:T(8,128)(2,1)}, bf16[128,2176]{1,0:T(8,128)(2,1)}, u32[]{:S(2)}, u32[]{:S(2)}) collective-permute-start(bf16[128,2176]{1,0:T(8,128)(2,1)} %collective-permute-done.25.refs_5_), channel_id=1, source_target_pairs={{0,4},{1,5},{2,6},{3,7},{4,0},{5,1},{6,2},{7,3},{8,12},{9,13},{10,... | collective-permute-start | bytes 1671176 | tf_op jit(solution)/shard_map/ppermute | solution.py:400
  153.5 12.8 %collective-permute-start.31 = (bf16[128,2176]{1,0:T(8,128)(2,1)}, bf16[128,2176]{1,0:T(8,128)(2,1)}, u32[]{:S(2)}, u32[]{:S(2)}) collective-permute-start(bf16[128,2176]{1,0:T(8,128)(2,1)} %collective-permute-done.27.refs_2_), channel_id=1, source_target_pairs={{0,2},{1,3},{2,0},{3,1},{4,6},{5,7},{6,4},{7,5},{8,10},{9,11},{10,... | collective-permute-start | bytes 1671176 | tf_op jit(solution)/shard_map/ppermute | solution.py:400
  165.2 15.8 %collective-permute-start.29 = (bf16[128,2176]{1,0:T(8,128)(2,1)}, bf16[128,2176]{1,0:T(8,128)(2,1)S(1)}, u32[]{:S(2)}, u32[]{:S(2)}) collective-permute-start(bf16[128,2176]{1,0:T(8,128)(2,1)} %collective-permute-done.24.refs_1_), channel_id=1, source_target_pairs={{0,4},{1,5},{2,6},{3,7},{4,0},{5,1},{6,2},{7,3},{8,12},{9,13},{10,... | collective-permute-start | bytes 1671176 | tf_op jit(solution)/shard_map/ppermute | solution.py:400
  166.3 15.8 %collective-permute-start.32 = (bf16[128,2176]{1,0:T(8,128)(2,1)}, bf16[128,2176]{1,0:T(8,128)(2,1)S(1)}, u32[]{:S(2)}, u32[]{:S(2)}) collective-permute-start(bf16[128,2176]{1,0:T(8,128)(2,1)} %collective-permute-done.24.refs_1_), channel_id=1, source_target_pairs={{0,2},{1,3},{2,0},{3,1},{4,6},{5,7},{6,4},{7,5},{8,10},{9,11},{10,... | collective-permute-start | bytes 1671176 | tf_op jit(solution)/shard_map/ppermute | solution.py:400
  168.2 33.3 %collective-permute-start.37 = (bf16[128,2176]{1,0:T(8,128)(2,1)}, bf16[128,2176]{1,0:T(8,128)(2,1)S(1)}, u32[]{:S(2)}, u32[]{:S(2)}) collective-permute-start(bf16[128,2176]{1,0:T(8,128)(2,1)} %collective-permute-done.23.refs_0_), channel_id=1, source_target_pairs={{0,4},{1,5},{2,6},{3,7},{4,0},{5,1},{6,2},{7,3},{8,12},{9,13},{10,... | collective-permute-start | bytes 1671176 | tf_op jit(solution)/shard_map/ppermute | solution.py:400
  168.7 32.7 %collective-permute-start.38 = (bf16[128,2176]{1,0:T(8,128)(2,1)}, bf16[128,2176]{1,0:T(8,128)(2,1)S(1)}, u32[]{:S(2)}, u32[]{:S(2)}) collective-permute-start(bf16[128,2176]{1,0:T(8,128)(2,1)} %collective-permute-done.23.refs_0_), channel_id=1, source_target_pairs={{0,2},{1,3},{2,0},{3,1},{4,6},{5,7},{6,4},{7,5},{8,10},{9,11},{10,... | collective-permute-start | bytes 1671176 | tf_op jit(solution)/shard_map/ppermute | solution.py:400
  199.7 14.9 %collective-permute-start.33 = (bf16[128,2048]{1,0:T(8,128)(2,1)S(1)}, bf16[128,2048]{1,0:T(8,128)(2,1)S(1)}, u32[]{:S(2)}, u32[]{:S(2)}) collective-permute-start(bf16[128,2048]{1,0:T(8,128)(2,1)S(1)} %get-tuple-element.79), channel_id=1, source_target_pairs={{0,4},{1,5},{2,6},{3,7},{4,0},{5,1},{6,2},{7,3},{8,12},{9,13},{10,... | collective-permute-start | bytes 1572872 | tf_op jit(solution)/shard_map/ppermute | solution.py:400
  201.5 17.1 %collective-permute-start.39 = (bf16[128,2176]{1,0:T(8,128)(2,1)S(1)}, bf16[128,2176]{1,0:T(8,128)(2,1)S(1)}, u32[]{:S(2)}, u32[]{:S(2)}) collective-permute-start(bf16[128,2176]{1,0:T(8,128)(2,1)S(1)} %collective-permute-done.37.refs_2_), channel_id=1, source_target_pairs={{0,2},{1,3},{2,0},{3,1},{4,6},{5,7},{6,4},{7,5},{8,10},{9,11},{10,... | collective-permute-start | bytes 1671176 | tf_op jit(solution)/shard_map/ppermute | solution.py:400
  202.1 21.0 %collective-permute-start.40 = (bf16[128,2176]{1,0:T(8,128)(2,1)S(1)}, bf16[128,2176]{1,0:T(8,128)(2,1)S(1)}, u32[]{:S(2)}, u32[]{:S(2)}) collective-permute-start(bf16[128,2176]{1,0:T(8,128)(2,1)S(1)} %collective-permute-done.32.refs_5_), channel_id=1, source_target_pairs={{0,4},{1,5},{2,6},{3,7},{4,0},{5,1},{6,2},{7,3},{8,12},{9,13},{10,... | collective-permute-start | bytes 1671176 | tf_op jit(solution)/shard_map/ppermute | solution.py:400
  214.6 23.3 %collective-permute-start.42 = (bf16[128,2048]{1,0:T(8,128)(2,1)S(1)}, bf16[128,2048]{1,0:T(8,128)(2,1)S(1)}, u32[]{:S(2)}, u32[]{:S(2)}) collective-permute-start(bf16[128,2048]{1,0:T(8,128)(2,1)S(1)} %get-tuple-element.94), channel_id=1, source_target_pairs={{0,2},{1,3},{2,0},{3,1},{4,6},{5,7},{6,4},{7,5},{8,10},{9,11},{10,... | collective-permute-start | bytes 1572872 | tf_op jit(solution)/shard_map/ppermute | solution.py:400
  216.5 22.0 %collective-permute-start.35 = (bf16[128,2048]{1,0:T(8,128)(2,1)S(1)}, bf16[128,2048]{1,0:T(8,128)(2,1)S(1)}, u32[]{:S(2)}, u32[]{:S(2)}) collective-permute-start(bf16[128,2048]{1,0:T(8,128)(2,1)S(1)} %add_convert_fusion.7), channel_id=1, source_target_pairs={{0,2},{1,3},{2,0},{3,1},{4,6},{5,7},{6,4},{7,5},{8,10},{9,11},{10,... | collective-permute-start | bytes 1572872 | tf_op jit(solution)/shard_map/ppermute | solution.py:400
  216.8 21.6 %collective-permute-start.34 = (bf16[128,2048]{1,0:T(8,128)(2,1)S(1)}, bf16[128,2048]{1,0:T(8,128)(2,1)S(1)}, u32[]{:S(2)}, u32[]{:S(2)}) collective-permute-start(bf16[128,2048]{1,0:T(8,128)(2,1)S(1)} %get-tuple-element.80), channel_id=1, source_target_pairs={{0,4},{1,5},{2,6},{3,7},{4,0},{5,1},{6,2},{7,3},{8,12},{9,13},{10,... | collective-permute-start | bytes 1572872 | tf_op jit(solution)/shard_map/ppermute | solution.py:400
  236.1 14.9 %collective-permute-start.46 = (bf16[128,2048]{1,0:T(8,128)(2,1)S(1)}, bf16[128,2048]{1,0:T(8,128)(2,1)S(1)}, u32[]{:S(2)}, u32[]{:S(2)}) collective-permute-start(bf16[128,2048]{1,0:T(8,128)(2,1)S(1)} %get-tuple-element.101), channel_id=1, source_target_pairs={{0,4},{1,5},{2,6},{3,7},{4,0},{5,1},{6,2},{7,3},{8,12},{9,13},{10,... | collective-permute-start | bytes 1572872 | tf_op jit(solution)/shard_map/ppermute | solution.py:400
  237.9 14.9 %collective-permute-start.43 = (bf16[128,2048]{1,0:T(8,128)(2,1)S(1)}, bf16[128,2048]{1,0:T(8,128)(2,1)S(1)}, u32[]{:S(2)}, u32[]{:S(2)}) collective-permute-start(bf16[128,2048]{1,0:T(8,128)(2,1)S(1)} %get-tuple-element.95), channel_id=1, source_target_pairs={{0,2},{1,3},{2,0},{3,1},{4,6},{5,7},{6,4},{7,5},{8,10},{9,11},{10,... | collective-permute-start | bytes 1572872 | tf_op jit(solution)/shard_map/ppermute | solution.py:400
  238.7 16.5 %collective-permute-start.36 = (bf16[128,2048]{1,0:T(8,128)(2,1)S(1)}, bf16[128,2048]{1,0:T(8,128)(2,1)S(1)}, u32[]{:S(2)}, u32[]{:S(2)}) collective-permute-start(bf16[128,2048]{1,0:T(8,128)(2,1)S(1)} %add_convert_fusion.6), channel_id=1, source_target_pairs={{0,8},{1,9},{2,10},{3,11},{4,12},{5,13},{6,14},{7,15},{8,16},{9,17... | collective-permute-start | bytes 1572872 | tf_op jit(solution)/shard_map/ppermute | solution.py:445
  238.8 25.2 %collective-permute-start.41 = (bf16[128,2048]{1,0:T(8,128)(2,1)S(1)}, bf16[128,2048]{1,0:T(8,128)(2,1)S(1)}, u32[]{:S(2)}, u32[]{:S(2)}) collective-permute-start(bf16[128,2048]{1,0:T(8,128)(2,1)S(1)} %get-tuple-element.91), channel_id=1, source_target_pairs={{0,2},{1,3},{2,0},{3,1},{4,6},{5,7},{6,4},{7,5},{8,10},{9,11},{10,... | collective-permute-start | bytes 1572872 | tf_op jit(solution)/shard_map/ppermute | solution.py:400
  251.1 22.1 %collective-permute-start.47 = (bf16[128,2048]{1,0:T(8,128)(2,1)S(1)}, bf16[128,2048]{1,0:T(8,128)(2,1)S(1)}, u32[]{:S(2)}, u32[]{:S(2)}) collective-permute-start(bf16[128,2048]{1,0:T(8,128)(2,1)S(1)} %get-tuple-element.102), channel_id=1, source_target_pairs={{0,4},{1,5},{2,6},{3,7},{4,0},{5,1},{6,2},{7,3},{8,12},{9,13},{10,... | collective-permute-start | bytes 1572872 | tf_op jit(solution)/shard_map/ppermute | solution.py:400
  252.9 18.6 %collective-permute-start.44 = (bf16[128,2048]{1,0:T(8,128)(2,1)S(1)}, bf16[128,2048]{1,0:T(8,128)(2,1)S(1)}, u32[]{:S(2)}, u32[]{:S(2)}) collective-permute-start(bf16[128,2048]{1,0:T(8,128)(2,1)S(1)} %add_convert_fusion.5), channel_id=1, source_target_pairs={{0,4},{1,5},{2,6},{3,7},{4,0},{5,1},{6,2},{7,3},{8,12},{9,13},{10,... | collective-permute-start | bytes 1572872 | tf_op jit(solution)/shard_map/ppermute | solution.py:400
  253.4 19.7 %collective-permute-start.48 = (bf16[128,2048]{1,0:T(8,128)(2,1)S(1)}, bf16[128,2048]{1,0:T(8,128)(2,1)S(1)}, u32[]{:S(2)}, u32[]{:S(2)}) collective-permute-start(bf16[128,2048]{1,0:T(8,128)(2,1)S(1)} %add_convert_fusion.3), channel_id=1, source_target_pairs={{0,2},{1,3},{2,0},{3,1},{4,6},{5,7},{6,4},{7,5},{8,10},{9,11},{10,... | collective-permute-start | bytes 1572872 | tf_op jit(solution)/shard_map/ppermute | solution.py:400
  264.0 11.7 %collective-permute-start.50 = (bf16[128,2048]{1,0:T(8,128)(2,1)S(1)}, bf16[128,2048]{1,0:T(8,128)(2,1)S(1)}, u32[]{:S(2)}, u32[]{:S(2)}) collective-permute-start(bf16[128,2048]{1,0:T(8,128)(2,1)S(1)} %get-tuple-element.108), channel_id=1, source_target_pairs={{0,2},{1,3},{2,0},{3,1},{4,6},{5,7},{6,4},{7,5},{8,10},{9,11},{10,... | collective-permute-start | bytes 1572872 | tf_op jit(solution)/shard_map/ppermute | solution.py:400
  271.5 9.2 %collective-permute-start.51 = (bf16[128,2048]{1,0:T(8,128)(2,1)S(1)}, bf16[128,2048]{1,0:T(8,128)(2,1)S(1)}, u32[]{:S(2)}, u32[]{:S(2)}) collective-permute-start(bf16[128,2048]{1,0:T(8,128)(2,1)S(1)} %add_convert_fusion.1), channel_id=1, source_target_pairs={{0,4},{1,5},{2,6},{3,7},{4,0},{5,1},{6,2},{7,3},{8,12},{9,13},{10,... | collective-permute-start | bytes 1572872 | tf_op jit(solution)/shard_map/ppermute | solution.py:400
  273.4 10.9 %collective-permute-start.49 = (bf16[128,2048]{1,0:T(8,128)(2,1)S(1)}, bf16[128,2048]{1,0:T(8,128)(2,1)S(1)}, u32[]{:S(2)}, u32[]{:S(2)}) collective-permute-start(bf16[128,2048]{1,0:T(8,128)(2,1)S(1)} %add_convert_fusion.2), channel_id=1, source_target_pairs={{0,24},{1,25},{2,26},{3,27},{4,28},{5,29},{6,30},{7,31},{8,0},{9,1... | collective-permute-start | bytes 1572872 | tf_op jit(solution)/shard_map/ppermute | solution.py:445
  274.6 16.6 %collective-permute-start.45 = (bf16[128,2048]{1,0:T(8,128)(2,1)S(1)}, bf16[128,2048]{1,0:T(8,128)(2,1)S(1)}, u32[]{:S(2)}, u32[]{:S(2)}) collective-permute-start(bf16[128,2048]{1,0:T(8,128)(2,1)S(1)} %add_convert_fusion.4), channel_id=1, source_target_pairs={{0,16},{1,17},{2,18},{3,19},{4,20},{5,21},{6,22},{7,23},{8,24},{9,... | collective-permute-start | bytes 1572872 | tf_op jit(solution)/shard_map/ppermute | solution.py:445
  (37 other events, 507.4 us)
